TPU v7x, 256 devices: a whole 4x4x8 slice. The times are simulated.
256 devices in a mesh: aux: 8 (over z), occ: 2 (over core), vir: 16 (over y, x).
Axes of the slice: x: 4, y: 4, z: 8, core: 2. Of those that a mesh axis runs over, the one named last changes fastest.
Arguments:
- integrals: bfloat16 [32, 4000, 4000], P('aux', 'occ', 'vir'), may hold values from -4.5 to 4.5
- occ_coeffs: bfloat16 [4000, 400], replicated, may hold values from -0.09375 to 0.09375
- vir_coeffs: bfloat16 [4000, 3600], P('vir'), may hold values from -7.404361e-05 to 7.404361e-05
- occ_energy: float32 [400], replicated, may hold values from -1.5 to -0.5
- vir_energy: float32 [3600], P('vir'), may hold values from 0.2 to 2
- trial_vectors: bfloat16 [400, 8], replicated, may hold values from -0.3125 to 0.3125
- shifts: float32 [8], P('aux'), may hold values from -1 to -0.3
Outputs:
- sigma_vectors: float32 [400, 8], P(None, 'aux')
- subspace: float32 [8, 8], P(None, 'aux')
All inputs are finite; a program needn't handle non-finite values.
Results may differ from a plain program's by a relative error of at most 0.0024.
Values may be sent and summed in bfloat16 or wider, within the bound.
A program may use at most 128 MiB of HBM per device.

v0:
```python
import jax
import jax.numpy as jnp
from jax import lax
from jax.sharding import PartitionSpec as P


def fold_block(values, panel, shifts, vir_energy, first_energy, second_energy):
    coupled = jnp.einsum("nqi,qja->nija", values, panel, preferred_element_type=jnp.float32)
    divisor = (
        shifts[:, None, None, None]
        + vir_energy[None, None, None, :]
        - first_energy[None, :, None, None]
        - second_energy[None, None, :, None]
    )
    weighted = (coupled / divisor).astype(jnp.bfloat16)
    return jnp.einsum("nija,qja->nqi", weighted, panel, preferred_element_type=jnp.float32)


def local(integrals, occ_coeffs, vir_coeffs, occ_energy, vir_energy, trial_vectors, shifts):
    aux_local = integrals.shape[0]
    rows_first = integrals.shape[1]
    rows_second = integrals.shape[2]
    occ_count = occ_coeffs.shape[1]
    occ_parts = lax.axis_size("occ")
    occ_local = occ_count // occ_parts
    vir_local = vir_energy.shape[0]
    vec_local = shifts.shape[0]
    occ_index = lax.axis_index("occ")
    vir_index = lax.axis_index("vir")
    aux_index = lax.axis_index("aux")
    first_rows = lax.dynamic_slice_in_dim(occ_coeffs, occ_index * rows_first, rows_first, 0)
    second_rows = lax.dynamic_slice_in_dim(occ_coeffs, vir_index * rows_second, rows_second, 0)
    columns = first_rows
    term = jnp.einsum("mi,dmn->idn", columns, integrals, preferred_element_type=jnp.float32)
    halfway = lax.psum_scatter(
        term.reshape(occ_local * lax.axis_size("occ"), aux_local * rows_second),
        "occ",
        scatter_dimension=0,
        tiled=True,
    )
    halfway = halfway.reshape(occ_local * aux_local, rows_second).astype(jnp.bfloat16)
    columns = vir_coeffs
    hole_particle = lax.psum_scatter(
        lax.dot_general(
            columns, halfway, (((0,), (1,)), ((), ())), preferred_element_type=jnp.float32
        ).astype(jnp.bfloat16),
        "vir",
        scatter_dimension=0,
        tiled=True,
    ).astype(jnp.float32)
    hole_particle = jnp.transpose(
        hole_particle.reshape(vir_local, occ_local, aux_local), (2, 1, 0)
    ).astype(jnp.bfloat16)
    pair_term = lax.dot_general(
        second_rows, halfway, (((0,), (1,)), ((), ())), preferred_element_type=jnp.float32
    )
    pair_term = lax.psum(pair_term, "vir")
    hole_pair = jnp.transpose(pair_term.reshape(occ_count, occ_local, aux_local), (2, 0, 1)).astype(
        jnp.bfloat16
    )
    hole_pair = lax.all_gather(hole_pair, "aux", axis=0, tiled=True)
    aux_count = hole_pair.shape[0]
    own_trial = lax.dynamic_slice_in_dim(trial_vectors, aux_index * vec_local, vec_local, 1)
    reduced = jnp.einsum(
        "kn,qki->nqi", own_trial, hole_pair, preferred_element_type=jnp.float32
    ).astype(jnp.bfloat16)
    own_energy = lax.dynamic_slice_in_dim(occ_energy, occ_index * occ_local, occ_local, 0)
    gathered = lax.all_gather(hole_particle[None], ("aux", "occ"), axis=0, tiled=True)
    gathered = gathered.reshape(aux_count // aux_local, occ_parts, aux_local, occ_local, vir_local)
    folded = jnp.zeros((vec_local, aux_count, occ_local), jnp.float32)
    for column in range(occ_parts):
        panel = gathered[:, column].reshape(aux_count, occ_local, vir_local)
        second_energy = occ_energy[column * occ_local : (column + 1) * occ_local]
        folded = folded + fold_block(reduced, panel, shifts, vir_energy, own_energy, second_energy)
    folded = lax.psum(folded, "vir")
    folded = folded.astype(jnp.bfloat16)
    partial_sigma = jnp.einsum("qki,nqi->kn", hole_pair, folded, preferred_element_type=jnp.float32)
    sigma_vectors = lax.psum(partial_sigma, "occ")
    sigma_vectors = sigma_vectors + occ_energy[:, None] * own_trial.astype(jnp.float32)
    subspace = jnp.dot(
        trial_vectors.astype(jnp.float32).T, sigma_vectors, precision=lax.Precision.HIGHEST
    )
    return (sigma_vectors, subspace)


def solution(mesh):
    return jax.shard_map(
        local,
        mesh=mesh,
        in_specs=(P("aux", "occ", "vir"), P(), P("vir", None), P(), P("vir"), P(), P("aux")),
        out_specs=(P(None, "aux"), P(None, "aux")),
        check_vma=False,
    )
```

profile of v0, /device:TPU:1, one launch (start us, length us, event | category | flops | bytes accessed | tf_op | source)
XLA Modules:
  0.0 441.1 jit_solution(15388847902836251813)
XLA Ops:
  7.2 0.0 copy-start
  7.2 0.0 reduce-scatter.3.cloned.1.call-start
  7.2 1.9 copy-done
  9.1 4.1 fusion.11
  13.2 2.2 copy.15
  15.4 3.2 reshape.93
  18.6 0.0 reduce-scatter.3.cloned.1.call-update
  18.6 0.0 all-reduce.4.cloned.1.call-start
  18.7 19.0 %reduce-scatter.3.cloned.1.call-done = f32[200,1000]{1,0:T(8,128)} async-done(((f32[400,1000]{1,0:T(8,128)}), f32[200,1000]{1,0:T(8,128)}) %reduce-scatter.3.cloned.1.call-update) | async-done | bytes 800016 | tf_op jit(solution)/shard_map/reduce_scatter | solution.py:35
  37.7 2.0 convert_element_type.48
  39.6 2.2 convert_element_type.49
  41.8 5.9 %fusion.6 = bf16[3600,800]{0,1:T(8,128)(2,1)} fusion(bf16[800,250]{1,0:T(8,128)(2,1)} %convert_element_type.49, bf16[250,3600]{0,1:T(8,128)(2,1)} %param.9), kind=kOutput, calls=%fused_computation.7 | convolution fusion | flops 1442880000 | bytes 7960000 | tf_op jit(solution)/shard_map/dot_general | solution.py:44
  47.7 0.0 all-reduce.4.cloned.1.call-update
  47.7 0.0 all-gather.4.cloned.1.call-start
  47.8 2.6 fusion.34
  50.3 88.9 %all-reduce.5 = bf16[400,800]{1,0:T(8,128)(2,1)} all-reduce(f32[400,800]{1,0:T(8,128)} %fusion.34), channel_id=1, replica_groups=mesh['aux'=8,'occ'=2,'vir'=16] {'vir'}, use_global_device_ids=true, to_apply=%region_1.0 | all-reduce | flops 320000 | bytes 1920000 | tf_op jit(solution)/shard_map/psum | solution.py:57
  139.2 0.0 copy-start.5
  139.2 2.3 copy.16
  141.5 0.0 copy-start.4
  141.5 0.0 copy-start.1
  141.5 2.5 convert_element_type.51
  144.1 2.2 copy.17
  146.3 0.0 all-gather.4.cloned.1.call-update
  146.3 0.0 all-gather.6.cloned.1.call-start
  146.4 0.0 copy-done.5
  146.4 0.6 dynamic-slice
  147.6 43.2 %all-reduce.4.cloned.1.call-done = bf16[3600,800]{0,1:T(8,128)(2,1)} async-done(((bf16[3600,800]{0,1:T(8,128)(2,1)}), bf16[3600,800]{0,1:T(8,128)(2,1)}) %all-reduce.4.cloned.1.call-update) | async-done | bytes 5760016
  190.9 2.0 constant_dynamic-slice_fusion
  192.9 1.9 convert_element_type.55
  194.8 1.8 copy.61
  196.6 0.0 all-gather.6.cloned.1.call-update
  197.3 0.0 copy-done.4
  197.3 0.0 copy-done.1
  197.3 0.1 fusion.49
  197.4 0.1 broadcast_subtract_fusion
  197.5 72.0 %all-gather.4.cloned.1.call-done = bf16[32,400,200]{2,1,0:T(8,128)(2,1)} async-done(((bf16[4,400,200]{2,1,0:T(8,128)(2,1)}), bf16[32,400,200]{2,1,0:T(8,128)(2,1)}) %all-gather.4.cloned.1.call-update) | async-done | bytes 5120016 | tf_op jit(solution)/shard_map/all_gather | solution.py:61
  269.5 3.8 fusion.42
  273.3 44.2 %all-gather.6.cloned.1.call-done = bf16[64,200,225]{2,1,0:T(8,128)(2,1)} async-done(((bf16[4,200,225]{2,1,0:T(8,128)(2,1)}), bf16[64,200,225]{2,1,0:T(8,128)(2,1)}) %all-gather.6.cloned.1.call-update) | async-done | bytes 5760016 | tf_op jit(solution)/shard_map/all_gather | solution.py:68
  317.5 6.0 %fusion.48 = (bf16[8,1,4,200,225]{4,3,2,1,0:T(8,128)(2,1)}, bf16[8,1,4,200,225]{4,3,2,1,0:T(8,128)(2,1)}) fusion(bf16[8,2,4,200,225]{4,3,2,1,0:T(8,128)(2,1)} %bitcast.69), kind=kLoop, calls=%fused_computation.36 | loop fusion | bytes 11520000 | tf_op jit(solution)/shard_map/slice | solution.py:72
  323.5 14.8 %fusion.14 = f32[32,200]{1,0:T(8,128)} fusion(f32[200]{0:T(256)S(1)} %get-tuple-element.6, f32[200,225]{1,0:T(8,128)S(1)} %broadcast_subtract_fusion, bf16[32,200,225]{2,1,0:T(8,128)(2,1)} %bitcast.71, bf16[1,32,200]{2,0,1:T(2,128)(2,1)S(1)} %fusion.42), kind=kOutput, calls=%fused_computation.13 | convolution fusion | flops 1179000064 | bytes 3099200 | tf_op jit(solution)/shard_map/nija,qja->nqi/dot_general | solution.py:16
  338.3 14.3 %fusion.29 = f32[1,32,200]{2,1,0:T(8,128)S(1)} fusion(f32[32,200]{1,0:T(8,128)} %fusion.14, f32[200]{0:T(256)S(1)} %get-tuple-element.4, f32[200,225]{1,0:T(8,128)S(1)} %broadcast_subtract_fusion, bf16[32,200,225]{2,1,0:T(8,128)(2,1)} %bitcast.70, bf16[1,32,200]{2,0,1:T(2,128)(2,1)S(1)} %fusion.42), kind=kOutput, calls=%fused_computation.16 | convolution fusion | flops 1179006464 | bytes 3124800 | tf_op jit(solution)/shard_map/nija,qja->nqi/dot_general | solution.py:16
  352.6 60.4 %psum.22 = bf16[1,32,200]{2,1,0:T(8,128)(2,1)S(1)} all-reduce(f32[1,32,200]{2,1,0:T(8,128)S(1)} %fusion.29), channel_id=1, replica_groups=mesh['aux'=8,'occ'=2,'vir'=16] {'vir'}, use_global_device_ids=true, to_apply=%region_3.0 | all-reduce | flops 6400 | bytes 38400 | tf_op jit(solution)/shard_map/psum | solution.py:75
  413.0 0.0 copy-start.2
  413.0 4.7 %convolution_bitcast_fusion = f32[400,1]{0,1:T(1,128)S(1)} fusion(bf16[32,400,200]{2,1,0:T(8,128)(2,1)} %all-gather.4.cloned.1.call-done, bf16[32,200,1]{1,0,2:T(8,128)(2,1)S(1)} %bitcast.74), kind=kOutput, calls=%fused_computation.17 | convolution fusion | flops 5120000 | bytes 5134400 | tf_op jit(solution)/shard_map/qki,nqi->kn/dot_general | solution.py:77
  417.7 16.2 %psum.23 = f32[400,1]{0,1:T(1,128)S(1)} all-reduce(f32[400,1]{0,1:T(1,128)S(1)} %convolution_bitcast_fusion), channel_id=1, replica_groups=mesh['aux'=8,'occ'=2,'vir'=16] {'occ'}, use_global_device_ids=true, to_apply=%region_4.0 | all-reduce | flops 400 | bytes 3200 | tf_op jit(solution)/shard_map/psum | solution.py:78
  433.9 0.0 copy-done.2
  433.9 0.0 copy-start.3
  433.9 0.6 convolution_bitcast_fusion.1
  434.6 0.0 copy-done.3
  (2 shorter events, 0.0 us)
Async XLA Ops:
  7.2 1.9 copy-start
  7.2 30.5 %reduce-scatter.3.cloned.1.call-start = ((), (), s32[]{:S(2)}) async-start(), calls=%async_computation.1 | async-start | bytes 2457600 | tf_op jit(solution)/shard_map/reduce_scatter | solution.py:35
  18.6 172.2 %all-reduce.4.cloned.1.call-start = ((), (), s32[]{:S(2)}) async-start(), calls=%async_computation.4 | async-start | bytes 11878400
  47.7 221.7 %all-gather.4.cloned.1.call-start = ((), (), s32[]{:S(2)}) async-start(), calls=%async_computation.2 | async-start | bytes 7372800 | tf_op jit(solution)/shard_map/all_gather | solution.py:61
  139.2 7.1 %copy-start.5 = (u32[256]{0:T(256)S(1)}, u32[256]{0:T(256)}, u32[]{:S(2)}) copy-start(u32[256]{0:T(256)} %constant.35) | copy-start | bytes 3076
  141.5 55.8 %copy-start.4 = (f32[225]{0:T(256)S(1)}, f32[225]{0:T(256)}, u32[]{:S(2)}) copy-start(f32[225]{0:T(256)} %param.11) | copy-start | bytes 2704
  141.5 55.8 %copy-start.1 = (f32[400]{0:T(512)S(1)}, f32[400]{0:T(512)}, u32[]{:S(2)}) copy-start(f32[400]{0:T(512)} %param.10) | copy-start | bytes 4804
  146.3 171.2 %all-gather.6.cloned.1.call-start = ((), (), s32[]{:S(2)}) async-start(), calls=%async_computation.3 | async-start | bytes 6963200 | tf_op jit(solution)/shard_map/all_gather | solution.py:68
  413.0 20.9 %copy-start.2 = (bf16[400,8]{0,1:T(8,128)(2,1)S(1)}, bf16[400,8]{0,1:T(8,128)(2,1)}, u32[]{:S(2)}) copy-start(bf16[400,8]{0,1:T(8,128)(2,1)} %param.12) | copy-start | bytes 19204
  433.9 0.7 copy-start.3
Sparse Core Ops, SparseCore 0:
  18.7 18.8 reduce-scatter.2
  47.8 142.9 all-reduce.3
  192.7 76.7 all-gather.3
  271.1 46.2 all-gather.5
where the time goes:
time: 442 us; the launch traced here: 441 us
  waiting for transfers between devices  178 us (40%)
  blocking collectives  166 us (38%)
  matrix products  50.8 us (11%)
  local copies, waits for them, and re-layouts  29 us (7%)
  between operations  15.2 us (3%)
    psum x1, blocking collectives, local(): pair_term = lax.psum(pair_term, 'vir')  88.9 us
    all_gather x1, waiting for transfers between devices, local(): hole_pair = lax.all_gather(hole_pair, 'aux', axis=0, tiled=True)  72 us
    psum x1, blocking collectives, local(): folded = lax.psum(folded, 'vir')  60.4 us
    all_gather x1, waiting for transfers between devices, local(): lax.all_gather(hole_particle[None], ('aux', 'occ'), axis=0, tiled=True)  44.2 us
    unnamed x5, waiting for transfers between devices  43.3 us
    dot_general x2, matrix products, fold_block(): jnp.einsum('nija,qja->nqi', weighted, panel, preferred_element_type=jnp.f...  29.1 us
    reduce_scatter x1, waiting for transfers between devices, local(): lax.psum_scatter(term.reshape(occ_local * lax.axis_size('occ'), aux_local...  19 us
    psum x1, blocking collectives, local(): sigma_vectors = lax.psum(partial_sigma, 'occ')  16.2 us
  transfers between devices with their start and end apart: 4, of which 4 were waited for; matrix products, arithmetic and copies ran while one was open for 5% of the time, Pallas kernels for 0%

commit v1 on v0

v1 whole, which is shorter than its diff:
```python
import functools
import math

import jax
import jax.numpy as jnp
from jax import lax
from jax.experimental import pallas as pl
from jax.experimental.pallas import tpu as pltpu
from jax.sharding import PartitionSpec as P

MESH = pl.DeviceIdType.MESH
F32 = jnp.float32
BF16 = jnp.bfloat16


def dot(a, b):
    return jnp.dot(a, b, preferred_element_type=F32)


def dot_nt(a, b):
    return lax.dot_general(a, b, (((1,), (1,)), ((), ())), preferred_element_type=F32)


def split(value):
    high = value.astype(BF16)
    low = (value - high.astype(F32)).astype(BF16)
    return jnp.concatenate([high.astype(F32), low.astype(F32)], axis=0).astype(BF16)


def send(src, dst, send_sem, recv_sem, **device):
    copy = pltpu.make_async_remote_copy(
        src_ref=src, dst_ref=dst, send_sem=send_sem, recv_sem=recv_sem, device_id=device, device_id_type=MESH
    )
    copy.start()
    return copy


class Sizes:
    def __init__(self, mesh, integrals, occ_coeffs, vir_energy):
        self.nz = mesh["aux"]
        self.side = math.isqrt(mesh["vir"])
        self.nq, self.mu, self.nu = integrals.shape
        self.ao, self.nocc = occ_coeffs.shape
        self.half = self.nocc // 2
        self.jb = self.half // self.nz
        self.na = vir_energy.shape[0]
        self.block = 16 * (self.na // 16)
        self.rows = self.block + 16
        assert self.na == self.block + 1 and self.side**2 <= 16
        first = (self.jb + 1) // 2
        rows = -(-(self.nq * first) // 16) * 16
        width = -(-(first * self.na) // 256) * 256
        self.groups = [(0, first, 0, 0, width)]
        rest = self.jb - first
        self.groups.append((first, rest, rows, width, -(-(rest * self.na) // 256) * 256))
        self.pack = rows + -(-(self.nq * rest) // 16) * 16
        self.flat = self.groups[1][3] + self.groups[1][4]
        self.pairs = self.nz // 2
        self.lane0 = self.mu // 128 * 128
        self.shift = self.mu - self.lane0
        self.window = self.mu + self.shift
        self.lanes = -(-self.rows // 128) * 128
        self.q = self.nq * self.nz
        self.nvec = self.nz
        self.parts = -(-self.half // 128)
        last = 128 * (self.nu * (mesh["vir"] - 1) // 128) - 128
        self.view = self.ao - last
        for v in range(mesh["vir"]):
            start = 128 * (self.nu * v // 128) - 128 * ((v + 1) // mesh["vir"])
            assert start + self.view <= self.ao and self.nu * v - start + self.nu <= self.view


def kernel(
    s, int_h, occ_h, vir_h, trial, eo_row, eo_s, ve, shift_s,
    sigma_out, sub_out,
    ibuf, occ_v, pf, xf, hq, pk, hs, hg, vb, acc, bs, bx, bf, bflat, bj, bjt, base, sec, eob, ve8, shift,
    rp, rg, rx, rmsg, rall, rl, rmf, sh, fa, fl, fx, fz, fr, fg, fgx, spart, sgs, sgr, spp, spr, t32,
    in_sem, v_own, v_s, v_r, sh_s, sh_r, x_s, x_r, h_s, h_r, g_s, g_r, rg_s, rg_r, rx_s, rx_r, rz_s, rz_r, rc_s, rc_r,
    b_s, b_r, fc_s, fc_r, fz_s, fz_r, fg_s, fg_r, fx_s, fx_r, s1_s, s1_r, s2_s, s2_r,
):
    nz, side = s.nz, s.side
    z, c, v = lax.axis_index("aux"), lax.axis_index("occ"), lax.axis_index("vir")
    y, x = v // side, v % side
    g = y + c * (x - y)
    r = x + c * (y - x)
    sg = side - (side - 1) * c
    sr = 1 + (side - 1) * c

    def vid(gather, reduce):
        return gather * sg + reduce * sr

    started = []

    def go(*args, **device):
        copy = send(*args, **device)
        started.append(copy)
        return copy

    occ_in = pltpu.make_async_copy(occ_h, occ_v, in_sem.at[s.nq])
    occ_in.start()
    zero_rows = jnp.zeros((s.shift, s.nu), BF16)
    loads = []
    for q in range(s.nq):
        if s.shift:
            ibuf[q, 0 : s.shift, :] = zero_rows
            ibuf[q, s.mu : s.mu + s.shift, :] = zero_rows
        copy = pltpu.make_async_copy(
            int_h.at[q], ibuf.at[q, pl.ds(pl.multiple_of(s.shift * c, 16), s.mu), :], in_sem.at[q]
        )
        copy.start()
        loads.append(copy)
    own_v = []
    for w in range(side):
        start = pl.multiple_of(s.block * vid(g, w), 16)
        copy = pltpu.make_async_copy(vir_h.at[pl.ds(start, s.rows), :], vb.at[0, w], v_own.at[w])
        copy.start()
        own_v.append(copy)

    barrier = pltpu.get_barrier_semaphore()
    me = 2 * z + c
    for d in range(1, 2 * nz):
        other = (me + d) % (2 * nz)
        pl.semaphore_signal(barrier, inc=1, device_id={"aux": other // 2, "occ": other % 2}, device_id_type=MESH)
    for d in range(1, side * side):
        pl.semaphore_signal(barrier, inc=1, device_id={"vir": (v + d) % (side * side)}, device_id_type=MESH)
    pl.semaphore_wait(barrier, 2 * nz + side * side - 2)

    v_copies = {}
    for e in range(1, side):
        to = (g + e) % side
        for w in range(side):
            start = pl.multiple_of(s.block * vid(to, w), 16)
            v_copies[side - e, w] = go(
                vir_h.at[pl.ds(start, s.rows), :], vb.at[side - e, w], v_s.at[e - 1, w], v_r.at[side - e - 1, w],
                vir=vid(to, r),
            )
    shift[...] = jnp.full((8, 128), shift_s[0], F32)
    for e in range(1, nz):
        go(shift, sh.at[z], sh_s.at[e - 1], sh_r.at[z], aux=(z + e) % nz)
    sh[z] = shift[...]

    occ_in.wait()
    x_copies = []
    for q in range(s.nq):
        loads[q].wait()
        columns = occ_v[:, pl.ds(pl.multiple_of(s.lane0 * c, 128), s.window)]
        pf[q] = dot(columns, ibuf[q])
        x_copies.append(
            go(pf.at[q, pl.ds(pl.multiple_of(s.half * (1 - c), 8), s.half), :], xf.at[q], x_s.at[q], x_r.at[q], occ=1 - c)
        )
    start = 128 * ((s.nu * v) // 128) - 128 * ((v + 1) // (side * side))
    view = occ_v[:, pl.ds(pl.multiple_of(start, 128), s.view)].astype(F32)
    wide = -(-s.view // 128) * 128
    view = jnp.concatenate([view, jnp.zeros((s.nocc, wide - s.view), F32)], axis=1)
    sec[...] = pltpu.roll(view, wide - (s.nu * v - start), 1)[:, : s.nu].astype(BF16)
    t32[...] = trial[...].astype(F32)
    weights = split(dot(trial[...], sec[...]))
    pk[...] = jnp.zeros(pk.shape, F32)
    for q in range(s.nq):
        x_copies[q].wait_recv()
        xf[q] = xf[q] + pf[q, pl.ds(pl.multiple_of(s.half * c, 8), s.half), :]
        hq[q] = xf[q].astype(BF16)
        for to in range(nz):
            for j0, count, row0, _, _ in s.groups:
                pk[to, row0 + q * count : row0 + (q + 1) * count, :] = xf[q, to * s.jb + j0 : to * s.jb + j0 + count, :]
    hs[...] = pk[...].astype(BF16)
    for e in range(1, nz):
        to = (z + e) % nz
        go(hs.at[to], hg.at[0, z], h_s.at[e - 1], h_r.at[z], aux=to)
    hg[0, z] = hs[z]
    for e in range(1, side):
        go(
            hg.at[0, z], hg.at[side - e, z], g_s.at[e - 1, 0], g_r.at[side - e - 1, z], vir=vid((g + e) % side, r),
        )

    for q in range(s.nq):
        both = dot_nt(weights, hq[q])
        rp[q * s.nvec : (q + 1) * s.nvec, :] = both[: s.nvec] + both[s.nvec :]
    for e in range(1, side):
        go(rp, rg.at[side - e], rg_s.at[e - 1], rg_r.at[side - e - 1], vir=vid((g + e) % side, r))

    def arrived(dst, recv_sem):
        pltpu.make_async_remote_copy(
            src_ref=dst, dst_ref=dst, send_sem=recv_sem, recv_sem=recv_sem, device_id={"occ": c}, device_id_type=MESH
        ).wait_recv()

    for d in range(1, nz):
        source = (z + d) % nz
        arrived(hg.at[0, source], h_r.at[source])
        for e in range(1, side):
            go(
                hg.at[0, source], hg.at[side - e, source], g_s.at[e - 1, d], g_r.at[side - e - 1, source],
                vir=vid((g + e) % side, r),
            )
    total = rp[...]
    for d in range(1, side):
        arrived(rg.at[d], rg_r.at[d - 1])
        total = total + rg[d]
    rx[0] = total
    for e in range(1, side):
        go(rx.at[0], rx.at[side - e], rx_s.at[e - 1], rx_r.at[side - e - 1], vir=vid(g, (r + e) % side))

    tall = nz * s.pack
    for w in range(side):
        own_v[w].wait()

    def product(d):
        @pl.loop(0, side)
        def _(w):
            value = dot_nt(hg[d].reshape(tall, s.nu), vb[d, w])
            if d > 0:
                value = value + acc[w]
            acc[w] = value
            if d == side - 1:
                bs[w] = value.astype(BF16)

    product(0)
    total = rx[0]
    for d in range(1, side):
        arrived(rx.at[d], rx_r.at[d - 1])
        total = total + rx[d]
    rmsg[...] = total
    for e in range(1, nz):
        go(
            rmsg, rall.at[c, pl.ds(pl.multiple_of(z * s.nq * s.nvec, 8), s.nq * s.nvec), :], rz_s.at[e - 1], rz_r.at[z],
            aux=(z + e) % nz,
        )
    rall[c, pl.ds(pl.multiple_of(z * s.nq * s.nvec, 8), s.nq * s.nvec), :] = total
    for d in range(1, side):
        for source in range(nz):
            arrived(hg.at[d, source], g_r.at[d - 1, source])
        for w in range(side):
            v_copies[d, w].wait_recv()
        product(d)
    for e in range(1, side):
        to = (r + e) % side
        go(bs.at[to], bx.at[side - e], b_s.at[e - 1], b_r.at[side - e - 1], vir=vid(g, to))
    for d in range(1, nz):
        source = (z + d) % nz
        arrived(rall.at[c, pl.ds(pl.multiple_of(source * s.nq * s.nvec, 8), s.nq * s.nvec), :], rz_r.at[source])
        arrived(sh.at[source], sh_r.at[source])
    to_other = go(rall.at[c], rall.at[c], rc_s, rc_r, occ=1 - c)
    arrived(rall.at[1 - c], rc_r)
    nq8 = s.nq * s.nvec
    for h in range(2):
        for part in range(s.parts):
            width = min(128, s.half - part * 128)
            rl[h, part, :, 0:width] = rall[h, :, part * 128 : part * 128 + width]
    for n in range(s.nvec):
        for h in range(2):
            halves = []
            for part in range(s.parts):
                rows = [rl[h, part, pl.ds(q * s.nvec + n, nz, stride=nq8), :] for q in range(s.nq)]
                halves.append(jnp.concatenate(rows, axis=0))
            rmf[n, h * s.half : (h + 1) * s.half, :] = jnp.concatenate(halves, axis=1).T[: s.half]

    ve8[...] = jnp.ones(ve8.shape, F32)
    ve8[:, 0 : s.na] = jnp.broadcast_to(ve[...], (8, s.na))
    base[...] = jnp.ones(base.shape, F32)
    first = s.half * c + s.jb * z
    for j0, count, _, lane0, _ in s.groups:
        for j in range(count):
            base[:, lane0 + j * s.na : lane0 + (j + 1) * s.na] = ve8[:, 0 : s.na] - eo_s[first + j0 + j]
    square = jnp.broadcast_to(eo_row[...], (128, s.nocc))
    fill = -(-s.nocc // 128) * 128 - s.nocc
    eob[...] = jnp.concatenate([square, jnp.zeros((128, fill), F32)], axis=1).T[: s.nocc]

    for d in range(1, side):
        arrived(bx.at[d], b_r.at[d - 1])
    bflat[...] = jnp.zeros(bflat.shape, F32)

    @pl.loop(0, nz)
    def _(source):
        rows = pl.ds(pl.multiple_of(source * s.pack, 16), s.pack)
        value = acc[r, rows, :]
        for d in range(1, side):
            value = value + bx[d, rows, :].astype(F32)
        value = value.astype(BF16).astype(F32)
        full = jnp.concatenate([value, jnp.zeros((s.pack, s.lanes - s.rows), F32)], axis=1)
        full = pltpu.roll(full, s.lanes - v, 1)
        for part in range(s.lanes // 128):
            bf[part, rows, :] = full[:, part * 128 : (part + 1) * 128]

    for j0, count, row0, lane0, _ in s.groups:
        for j in range(count):
            parts = []
            for part in range(s.lanes // 128):
                rows = [bf[part, pl.ds(row0 + q * count + j, nz, stride=s.pack), :] for q in range(s.nq)]
                parts.append(jnp.concatenate(rows, axis=0))
            bflat[:, lane0 + j * s.na : lane0 + (j + 1) * s.na] = jnp.concatenate(parts, axis=1)[:, : s.na]
    bj[...] = bflat[...].astype(BF16)
    bjt[...] = bflat[...].T.astype(BF16)

    def fold(n, group):
        _, _, _, lane0, width = s.groups[group]
        rm = rmf[n].astype(BF16)
        row = jnp.broadcast_to(sh[n][0:1, :], (s.nocc, 128)) - eob[...]
        total = None
        for start in range(lane0, lane0 + width, 1536):
            size = min(1536, lane0 + width - start)
            divisor = jnp.concatenate([row] * (size // 128), axis=1) + base[0:1, start : start + size]
            coupled = dot(rm, bj[:, start : start + size])
            weighted = (coupled * pl.reciprocal(divisor, approx=True, full_range=False)).astype(BF16)
            term = dot(weighted, bjt[start : start + size, :])
            total = term if total is None else total + term
        return total

    @pl.loop(0, s.nvec)
    def _(n):
        fa[n] = fold(n, 0)

    rows2 = 2 * s.nq

    def to_core(p):
        return pltpu.make_async_remote_copy(
            src_ref=fl.at[p, 1 - c], dst_ref=fx.at[p], send_sem=fc_s.at[p], recv_sem=fc_r.at[p],
            device_id={"occ": 1 - c}, device_id_type=MESH,
        )

    def along_z(p, e):
        to = (z + e) % nz
        return pltpu.make_async_remote_copy(
            src_ref=fz.at[p, :, pl.ds(pl.multiple_of(to * rows2, 8), rows2), :], dst_ref=fr.at[p, z],
            send_sem=fz_s.at[p, e - 1], recv_sem=fz_r.at[p, z], device_id={"aux": to}, device_id_type=MESH,
        )

    def pass_on(p):
        to_core(p).wait_recv()
        fz[p] = fl[p, c] + fx[p]
        for e in range(1, nz):
            along_z(p, e).start()

    @pl.loop(0, s.pairs)
    def _(p):
        for m in range(2):
            n = 2 * p + m
            value = fa[n] + fold(n, 1)
            for h in range(2):
                flip = value[h * s.half : (h + 1) * s.half].T
                flip = jnp.concatenate([flip, jnp.zeros((s.q, s.parts * 128 - s.half), F32)], axis=1)
                for part in range(s.parts):
                    for q in range(s.nq):
                        fl[p, h, part, pl.ds(m * s.nq + q, nz, stride=rows2), :] = flip[
                            q * nz : (q + 1) * nz, part * 128 : (part + 1) * 128
                        ]
        to_core(p).start()

        @pl.when(p > 0)
        def _():
            pass_on(p - 1)

    pass_on(s.pairs - 1)
    for p in range(s.pairs):
        total = fz[p, :, pl.ds(pl.multiple_of(z * rows2, 8), rows2), :]
        for d in range(1, nz):
            source = (z + d) % nz
            arrived(fr.at[p, source], fz_r.at[p, source])
            total = total + fr[p, source]
        fg[0, p] = total
    for e in range(1, side):
        go(fg.at[0], fg.at[side - e], fg_s.at[e - 1], fg_r.at[side - e - 1], vir=vid((g + e) % side, r))
    total = fg[0]
    for d in range(1, side):
        arrived(fg.at[d], fg_r.at[d - 1])
        total = total + fg[d]
    fgx[0] = total
    for e in range(1, side):
        go(fgx.at[0], fgx.at[side - e], fx_s.at[e - 1], fx_r.at[side - e - 1], vir=vid(g, (r + e) % side))
    for d in range(1, side):
        arrived(fgx.at[d], fx_r.at[d - 1])
        total = total + fgx[d]

    tall = s.nvec * s.nq
    folded = jnp.concatenate([total[:, part].reshape(tall, 128) for part in range(s.parts)], axis=1)[:, : s.half]
    folded = split(folded)
    owner = lax.broadcasted_iota(jnp.int32, folded.shape, 0) % s.nq
    both = None
    for q in range(s.nq):
        term = dot(jnp.where(owner == q, folded.astype(F32), 0.0).astype(BF16), hq[q])
        both = term if both is None else both + term
    both = dot_nt(split(both[:tall] + both[tall:]), sec[...])
    spart[...] = both[:tall] + both[tall:]
    for n in range(s.nvec):
        value = spart[n * s.nq : n * s.nq + 1, :]
        for q in range(1, s.nq):
            value = value + spart[n * s.nq + q : n * s.nq + q + 1, :]
        sgs[n] = value
    for d in range(1, 2 * nz):
        other = (me + d) % (2 * nz)
        go(sgs.at[other // 2], sgr.at[me], s1_s.at[d - 1], s1_r.at[me], aux=other // 2, occ=other % 2)
    sgr[me] = sgs[z]
    for d in range(1, 2 * nz):
        other = (me + d) % (2 * nz)
        arrived(sgr.at[other], s1_r.at[other])
    total = sgr[0]
    for d in range(1, 2 * nz):
        total = total + sgr[d]
    spp[...] = total
    for d in range(1, side * side):
        go(spp, spr.at[v], s2_s.at[d - 1], s2_r.at[v], vir=(v + d) % (side * side))
    spr[v] = total
    for d in range(1, side * side):
        other = (v + d) % (side * side)
        arrived(spr.at[other], s2_r.at[other])
    total = spr[0]
    for d in range(1, side * side):
        total = total + spr[d]
    sigma = eo_row[...] * t32[pl.ds(z, 1), :] + total
    sigma_out[...] = sigma
    sub_out[...] = jnp.sum(t32[...] * sigma, axis=1, keepdims=True)
    for copy in started:
        copy.wait_send()
    for p in range(s.pairs):
        to_core(p).wait_send()
        for e in range(1, nz):
            along_z(p, e).wait_send()


def local(mesh, integrals, occ_coeffs, vir_coeffs, occ_energy, vir_energy, trial_vectors, shifts):
    s = Sizes(mesh, integrals, occ_coeffs, vir_energy)
    nz, side = s.nz, s.side
    vmem = pltpu.VMEM
    tall = nz * s.pack
    nq8 = s.nq * s.nvec
    rows2 = 2 * s.nq
    scratch = [
        vmem((s.nq, s.window, s.nu), BF16),
        vmem((s.nocc, s.ao), BF16),
        vmem((s.nq, s.nocc, s.nu), F32),
        vmem((s.nq, s.half, s.nu), F32),
        vmem((s.nq, s.half, s.nu), BF16),
        vmem((nz, s.pack, s.nu), F32),
        vmem((nz, s.pack, s.nu), BF16),
        vmem((side, nz, s.pack, s.nu), BF16),
        vmem((side, side, s.rows, s.nu), BF16),
        vmem((side, tall, s.rows), F32),
        vmem((side, tall, s.rows), BF16),
        vmem((side, tall, s.rows), BF16),
        vmem((s.lanes // 128, tall, 128), F32),
        vmem((s.q, s.flat), F32),
        vmem((s.q, s.flat), BF16),
        vmem((s.flat, s.q), BF16),
        vmem((8, s.flat), F32),
        vmem((s.nocc, s.nu), BF16),
        vmem((s.nocc, 128), F32),
        vmem((8, s.lanes), F32),
        vmem((8, 128), F32),
        vmem((nq8, s.half), F32),
        vmem((side, nq8, s.half), F32),
        vmem((side, nq8, s.half), F32),
        vmem((nq8, s.half), F32),
        vmem((2, nz * nq8, s.half), F32),
        vmem((2, s.parts, nz * nq8, 128), F32),
        vmem((s.nvec, s.nocc, s.q), F32),
        vmem((nz, 8, 128), F32),
        vmem((s.nvec, s.nocc, s.q), F32),
        vmem((s.pairs, 2, s.parts, nz * rows2, 128), F32),
        vmem((s.pairs, s.parts, nz * rows2, 128), F32),
        vmem((s.pairs, s.parts, nz * rows2, 128), F32),
        vmem((s.pairs, nz, s.parts, rows2, 128), F32),
        vmem((side, s.pairs, s.parts, rows2, 128), F32),
        vmem((side, s.pairs, s.parts, rows2, 128), F32),
        vmem((nq8, s.nocc), F32),
        vmem((nz, 1, s.nocc), F32),
        vmem((2 * nz, 1, s.nocc), F32),
        vmem((1, s.nocc), F32),
        vmem((side * side, 1, s.nocc), F32),
        vmem((s.nvec, s.nocc), F32),
    ]
    dma = lambda *shape: pltpu.SemaphoreType.DMA(shape)
    near = max(side - 1, 1)
    scratch += [
        dma(s.nq + 1), dma(side), dma(near, side), dma(near, side), dma(nz), dma(nz),
        dma(s.nq), dma(s.nq), dma(nz), dma(nz), dma(near, nz), dma(near, nz),
        dma(near), dma(near), dma(near), dma(near), dma(nz), dma(nz), pltpu.SemaphoreType.DMA, pltpu.SemaphoreType.DMA,
        dma(near), dma(near), dma(s.pairs), dma(s.pairs), dma(s.pairs, nz), dma(s.pairs, nz),
        dma(near), dma(near), dma(near), dma(near), dma(2 * nz), dma(2 * nz), dma(side * side), dma(side * side),
    ]
    hbm = pl.BlockSpec(memory_space=pl.ANY)
    fast = pl.BlockSpec(memory_space=pltpu.VMEM)
    scalars = pl.BlockSpec(memory_space=pltpu.SMEM)
    sigma, sub = pl.pallas_call(
        functools.partial(kernel, s),
        out_shape=(jax.ShapeDtypeStruct((1, s.nocc), F32), jax.ShapeDtypeStruct((s.nvec, 1), F32)),
        in_specs=[hbm, hbm, hbm, fast, fast, scalars, fast, scalars],
        out_specs=(fast, fast),
        scratch_shapes=scratch,
        compiler_params=pltpu.CompilerParams(
            collective_id=0, has_side_effects=True, vmem_limit_bytes=56 * 1024 * 1024
        ),
    )(
        integrals, occ_coeffs.T, vir_coeffs.T, trial_vectors.T, occ_energy[None], occ_energy, vir_energy[None], shifts,
    )
    return sigma.T, sub


def solution(mesh):
    return jax.shard_map(
        functools.partial(local, dict(mesh.shape)),
        mesh=mesh,
        in_specs=(P("aux", "occ", "vir"), P(), P("vir", None), P(), P("vir"), P(), P("aux")),
        out_specs=(P(None, "aux"), P(None, "aux")),
        check_vma=False,
    )
```

time: 442 us -> 117 us (0.26)
  waiting for transfers between devices: 178 us -> 0 us
  blocking collectives: 166 us -> 0 us
  Pallas kernels: 0 us -> 113 us
  matrix products: 50.8 us -> 0 us
  local copies, waits for them, and re-layouts: 29 us -> 2.49 us
  between operations: 15.2 us -> 1.29 us
    psum x3 -> x0, blocking collectives: 166 us -> none  [the longest x1 88.9 us: local(): pair_term = lax.psum(pair_term, 'vir')]
    all_gather x2 -> x0, waiting for transfers between devices: 116 us -> none  [the longest x1 72 us: local(): hole_pair = lax.all_gather(hole_pair, 'aux', axis=0, tiled=True)]
    pallas_call x0 -> x1, Pallas kernels: none -> 113 us  [local(): pl.pallas_call(functools.partial(kernel, s), out_shape=(jax.ShapeDtypeStr...]
    dot_general x8 -> x0, matrix products: 50.8 us -> none  [the longest x2 29.1 us: fold_block(): jnp.einsum('nija,qja->nqi', weighted, panel, preferred_element_type=jnp.f...]
    unnamed x5 -> x0, waiting for transfers between devices: 43.3 us -> none
    reduce_scatter x1 -> x0, waiting for transfers between devices: 19 us -> none  [local(): lax.psum_scatter(term.reshape(occ_local * lax.axis_size('occ'), aux_local...]
    convert_element_type x6 -> x0, local copies, waits for them, and re-layouts: 12.9 us -> none  [the longest x3 7.06 us: local(): jnp.transpose(pair_term.reshape(occ_count, occ_local, aux_local), (2, 0, 1))]
    slice x2 -> x0, local copies, waits for them, and re-layouts: 6.11 us -> none  [the longest x1 6.03 us: local(): panel = gathered[:, column].reshape(aux_count, occ_local, vir_local)]
  transfers between devices with their start and end apart: 4 -> 0, of which waited for: 4 -> 0; matrix products, arithmetic and copies ran while one was open for 5% -> 0% of each run, Pallas kernels for 0% -> 0%
where the time goes in v1:
time: 117 us
  Pallas kernels  113 us (97%)
  local copies, waits for them, and re-layouts  2.49 us (2%)
  between operations  1.29 us (1%)
    pallas_call x1, Pallas kernels, local(): pl.pallas_call(functools.partial(kernel, s), out_shape=(jax.ShapeDtypeStr...  113 us
    unnamed x2, local copies, waits for them, and re-layouts  2.49 us

profile of v1, /device:TPU:1, one launch (start us, length us, event | category | flops | bytes accessed | tf_op | source)
XLA Modules:
  0.0 117.3 jit_solution(7282839450545355742)
XLA Ops:
  1.3 113.5 %shard_map.86 = (f32[1,400]{1,0:T(1,128)}, f32[8,1]{1,0:T(8,128)}) custom-call(bf16[4,2000,250]{2,1,0:T(8,128)(2,1)} %int_h.1, bf16[400,4000]{1,0:T(8,128)(2,1)} %bitcast.6, bf16[3600,250]{1,0:T(8,128)(2,1)} %bitcast.7, bf16[8,400]{1,0:T(8,128)(2,1)} %bitcast.8, f32[1,400]{1,0:T(1,128)} %bitcast.9, f32[400]{0:T(512)} %eo_s.1, f32[1,225]{1,0:T(1,128)} %bitcast.11, ...), custom_call_target="tpu_custom_call" | custom-call | tf_op jit(solution)/shard_map/pallas_call | solution.py:482
  114.8 1.3 %copy.9 = f32[8,1]{0,1:T(1,128)} copy(f32[8,1]{1,0:T(8,128)} %get-tuple-element.7) | data formatting | bytes 64
  116.0 1.2 %copy.12 = f32[400,1]{0,1:T(1,128)} copy(f32[400,1]{0,1:T(1,128)} %bitcast.10) | data formatting | bytes 3200

commit v2 on v1

v2 whole, which is shorter than its diff:
```python
import functools
import math

import jax
import jax.numpy as jnp
from jax import lax
from jax.experimental import pallas as pl
from jax.experimental.pallas import tpu as pltpu
from jax.sharding import PartitionSpec as P

MESH = pl.DeviceIdType.MESH
F32 = jnp.float32
BF16 = jnp.bfloat16


def dot(a, b):
    return jnp.dot(a, b, preferred_element_type=F32)


def dot_nt(a, b):
    return lax.dot_general(a, b, (((1,), (1,)), ((), ())), preferred_element_type=F32)


def split(value):
    high = value.astype(BF16)
    low = (value - high.astype(F32)).astype(BF16)
    return jnp.concatenate([high.astype(F32), low.astype(F32)], axis=0).astype(BF16)


def send(src, dst, send_sem, recv_sem, **device):
    copy = pltpu.make_async_remote_copy(
        src_ref=src, dst_ref=dst, send_sem=send_sem, recv_sem=recv_sem, device_id=device, device_id_type=MESH
    )
    copy.start()
    return copy


class Sizes:
    def __init__(self, mesh, integrals, occ_coeffs, vir_energy):
        self.nz = mesh["aux"]
        self.side = math.isqrt(mesh["vir"])
        self.nq, self.mu, self.nu = integrals.shape
        self.ao, self.nocc = occ_coeffs.shape
        self.half = self.nocc // 2
        self.jb = self.half // self.nz
        self.na = vir_energy.shape[0]
        self.block = 16 * (self.na // 16)
        self.rows = self.block + 16
        assert self.na == self.block + 1 and self.side == 4
        first = (self.jb + 1) // 2
        rows = -(-(self.nq * first) // 16) * 16
        self.groups = [(0, first), (first, self.jb - first)]
        rest = self.jb - first
        self.packs = (rows, -(-(self.nq * rest) // 16) * 16)
        self.tile = 512
        self.tiles = -(-(self.jb * self.na) // self.tile)
        self.pairs = self.nz // 2
        self.lane0 = self.mu // 128 * 128
        self.shift = self.mu - self.lane0
        self.window = self.mu + self.shift
        self.lanes = -(-self.rows // 128) * 128
        self.q = self.nq * self.nz
        self.nvec = self.nz
        self.parts = -(-self.half // 128)
        last = 128 * (self.nu * (mesh["vir"] - 1) // 128) - 128
        self.view = self.ao - last
        for v in range(mesh["vir"]):
            start = 128 * (self.nu * v // 128) - 128 * ((v + 1) // mesh["vir"])
            assert start + self.view <= self.ao and self.nu * v - start + self.nu <= self.view


def exchange_kernel(
    s, int_h, occ_h, vir_h, trial, eo_row, eo_s, ve, shift_s,
    bj, bjt, base, rmf, row, hq, sec,
    ibuf, occ_v, pf, xf, pk0, pk1, hs0, hs1, hg0, hg1, vb, acc0, acc1, bs0, bs1, bx0, bx1, bm0, bm1, bf, bflat, eob, ve8, shift,
    rp, rg, rx, rmsg, rall, rl, rm32, sh,
    in_sem, v_own, v_s, v_r, sh_s, sh_r, x_s, x_r, h_s, h_r, g_s, g_r, rg_s, rg_r, rx_s, rx_r, rz_s, rz_r, rc_s, rc_r,
    b_s, b_r, m_s, m_r,
):
    nz, side = s.nz, s.side
    z, c, v = lax.axis_index("aux"), lax.axis_index("occ"), lax.axis_index("vir")
    y, x = v // side, v % side
    g = y + c * (x - y)
    r = x + c * (y - x)
    sg = side - (side - 1) * c
    sr = 1 + (side - 1) * c

    def vid(gather, reduce):
        return gather * sg + reduce * sr

    pk, hs, hg, acc, bs, bx, bm = (pk0, pk1), (hs0, hs1), (hg0, hg1), (acc0, acc1), (bs0, bs1), (bx0, bx1), (bm0, bm1)
    started = []

    def go(*args, **device):
        copy = send(*args, **device)
        started.append(copy)
        return copy

    occ_in = pltpu.make_async_copy(occ_h, occ_v, in_sem.at[s.nq])
    occ_in.start()
    zero_rows = jnp.zeros((s.shift, s.nu), BF16)
    loads = []
    for q in range(s.nq):
        if s.shift:
            ibuf[q, 0 : s.shift, :] = zero_rows
            ibuf[q, s.mu : s.mu + s.shift, :] = zero_rows
        copy = pltpu.make_async_copy(
            int_h.at[q], ibuf.at[q, pl.ds(pl.multiple_of(s.shift * c, 16), s.mu), :], in_sem.at[q]
        )
        copy.start()
        loads.append(copy)
    own_v = []
    for w in range(side):
        start = pl.multiple_of(s.block * vid(g, w), 16)
        copy = pltpu.make_async_copy(vir_h.at[pl.ds(start, s.rows), :], vb.at[0, w], v_own.at[w])
        copy.start()
        own_v.append(copy)

    for group in range(2):
        pk[group][...] = jnp.zeros(pk[group].shape, F32)

    barrier = pltpu.get_barrier_semaphore()
    pl.semaphore_signal(barrier, inc=1, device_id={"occ": 1 - c}, device_id_type=MESH)
    for d in range(1, nz):
        pl.semaphore_signal(barrier, inc=1, device_id={"aux": (z + d) % nz}, device_id_type=MESH)
    for d in range(1, side):
        pl.semaphore_signal(barrier, inc=1, device_id={"vir": vid((g + d) % side, r)}, device_id_type=MESH)
        pl.semaphore_signal(barrier, inc=1, device_id={"vir": vid(g, (r + d) % side)}, device_id_type=MESH)
    pl.semaphore_wait(barrier, nz + 2 * side - 2)

    v_copies = {}
    for e in range(1, side):
        to = (g + e) % side
        for w in range(side):
            start = pl.multiple_of(s.block * vid(to, w), 16)
            v_copies[side - e, w] = go(
                vir_h.at[pl.ds(start, s.rows), :], vb.at[side - e, w], v_s.at[e - 1, w], v_r.at[side - e - 1, w],
                vir=vid(to, r),
            )
    shift[...] = jnp.full((8, 128), shift_s[0], F32)
    for e in range(1, nz):
        go(shift, sh.at[z], sh_s.at[e - 1], sh_r.at[z], aux=(z + e) % nz)
    sh[z] = shift[...]

    occ_in.wait()
    x_copies = []
    for q in range(s.nq):
        loads[q].wait()
        columns = occ_v[:, pl.ds(pl.multiple_of(s.lane0 * c, 128), s.window)]
        pf[q] = dot(columns, ibuf[q])
        x_copies.append(
            go(pf.at[q, pl.ds(pl.multiple_of(s.half * (1 - c), 8), s.half), :], xf.at[q], x_s.at[q], x_r.at[q], occ=1 - c)
        )
    start = 128 * ((s.nu * v) // 128) - 128 * ((v + 1) // (side * side))
    view = occ_v[:, pl.ds(pl.multiple_of(start, 128), s.view)].astype(F32)
    wide = -(-s.view // 128) * 128
    view = jnp.concatenate([view, jnp.zeros((s.nocc, wide - s.view), F32)], axis=1)
    sec[...] = pltpu.roll(view, wide - (s.nu * v - start), 1)[:, : s.nu].astype(BF16)
    weights = split(dot(trial[...], sec[...]))
    for q in range(s.nq):
        x_copies[q].wait_recv()
        xf[q] = xf[q] + pf[q, pl.ds(pl.multiple_of(s.half * c, 8), s.half), :]
    near_first = [d for pair in zip(range(1, nz // 2), range(nz - 1, nz // 2, -1)) for d in pair] + [nz // 2]
    for group in range(2):
        j0, count = s.groups[group]
        for q in range(s.nq):
            for to in range(nz):
                pk[group][to, q * count : (q + 1) * count, :] = xf[q, to * s.jb + j0 : to * s.jb + j0 + count, :]
        hs[group][...] = pk[group][...].astype(BF16)
        for e in near_first:
            to = (z + e) % nz
            go(hs[group].at[to], hg[group].at[0, z], h_s.at[group, e - 1], h_r.at[group, z], aux=to)
        hg[group][0, z] = hs[group][z]
    for q in range(s.nq):
        hq[q] = xf[q].astype(BF16)

    for q in range(s.nq):
        both = dot_nt(weights, hq[q])
        rp[q * s.nvec : (q + 1) * s.nvec, :] = both[: s.nvec] + both[s.nvec :]
    for e in range(1, side):
        go(rp, rg.at[side - e], rg_s.at[e - 1], rg_r.at[side - e - 1], vir=vid((g + e) % side, r))

    ve8[...] = jnp.ones(ve8.shape, F32)
    ve8[:, 0 : s.na] = jnp.broadcast_to(ve[...], (8, s.na))
    bflat[...] = jnp.ones(bflat.shape, F32)
    first = s.half * c + s.jb * z
    for j in range(s.jb):
        bflat[0:8, j * s.na : (j + 1) * s.na] = ve8[:, 0 : s.na] - eo_s[first + j]
    for tile in range(s.tiles):
        base[tile] = bflat[0:8, tile * s.tile : (tile + 1) * s.tile]
    square = jnp.broadcast_to(eo_row[...], (128, s.nocc))
    fill = -(-s.nocc // 128) * 128 - s.nocc
    eob[...] = jnp.concatenate([square, jnp.zeros((128, fill), F32)], axis=1).T[: s.nocc]

    def arrived(dst, recv_sem):
        pltpu.make_async_remote_copy(
            src_ref=dst, dst_ref=dst, send_sem=recv_sem, recv_sem=recv_sem, device_id={"occ": c}, device_id_type=MESH
        ).wait_recv()

    ahead, behind = vid((g + 1) % side, r), vid((g + 3) % side, r)
    order = [0] + near_first

    def relay(group, k):
        source = (z + order[k]) % nz
        slot, to = (1, behind) if k % 2 == 0 else (3, ahead)
        arrived(hg[group].at[slot, source], g_r.at[group, slot - 1, source])
        go(hg[group].at[slot, source], hg[group].at[2, source], g_s.at[group, 2, k], g_r.at[group, 1, source], vir=to)

    def gather(group, steps):
        for k in steps:
            source = (z + order[k]) % nz
            if k:
                arrived(hg[group].at[0, source], h_r.at[group, source])
            go(hg[group].at[0, source], hg[group].at[3, source], g_s.at[group, 0, k], g_r.at[group, 2, source], vir=ahead)
            go(hg[group].at[0, source], hg[group].at[1, source], g_s.at[group, 1, k], g_r.at[group, 0, source], vir=behind)
            if k >= 2:
                relay(group, k - 2)

    def gathered(group, slot):
        for k in range(nz):
            if (slot, k % 2) not in ((1, 0), (3, 1)):
                source = (z + order[k]) % nz
                arrived(hg[group].at[slot, source], g_r.at[group, slot - 1, source])

    def term(group, d, w):
        return dot_nt(hg[group][d].reshape(nz * s.packs[group], s.nu), vb[d, w])

    def product(group, d):
        @pl.loop(0, side)
        def _(w):
            value = term(group, d, w)
            acc[group][w] = value if d == 0 else value + acc[group][w]

    right, left = vid(g, (r + 1) % side), vid(g, (r + 3) % side)

    def parts_of(group):
        size = nz * s.packs[group] // 2
        return pl.ds(0, size), pl.ds(size, size)

    def reduce_start(group, d):
        low, high = parts_of(group)
        for e in (2, 1, 3, 0):
            w = (r + e) % side
            value = acc[group][w] + term(group, d, w)
            acc[group][w] = value
            if e:
                bs[group][e - 1] = value.astype(BF16)
            if e == 2:
                go(bs[group].at[1, low], bm[group].at[0], m_s.at[group, 0], m_r.at[group, 0], vir=right)
                go(bs[group].at[1, high], bm[group].at[1], m_s.at[group, 1], m_r.at[group, 1], vir=left)
            if e == 1:
                go(bs[group].at[0, high], bx[group].at[0, high], b_s.at[group, 0, 1], b_r.at[group, 0, 1], vir=right)
            if e == 3:
                go(bs[group].at[2, low], bx[group].at[1, low], b_s.at[group, 1, 0], b_r.at[group, 1, 0], vir=left)

    def reduce_merge(group):
        low, high = parts_of(group)
        arrived(bm[group].at[0], m_r.at[group, 0])
        merged = acc[group][(r + 1) % side, low, :] + bm[group][0].astype(F32)
        bs[group][0, low, :] = merged.astype(BF16)
        go(bs[group].at[0, low], bx[group].at[0, low], b_s.at[group, 0, 0], b_r.at[group, 0, 0], vir=right)
        arrived(bm[group].at[1], m_r.at[group, 1])
        merged = acc[group][(r + 3) % side, high, :] + bm[group][1].astype(F32)
        bs[group][2, high, :] = merged.astype(BF16)
        go(bs[group].at[2, high], bx[group].at[1, high], b_s.at[group, 1, 1], b_r.at[group, 1, 1], vir=left)

    gather(0, range(nz))
    total = rp[...]
    for d in range(1, side):
        arrived(rg.at[d], rg_r.at[d - 1])
        total = total + rg[d]
    rx[0] = total
    for e in range(1, side):
        go(rx.at[0], rx.at[side - e], rx_s.at[e - 1], rx_r.at[side - e - 1], vir=vid(g, (r + e) % side))
    relay(0, nz - 2)
    relay(0, nz - 1)
    for w in range(side):
        own_v[w].wait()
    product(0, 0)
    total = rx[0]
    for d in range(1, side):
        arrived(rx.at[d], rx_r.at[d - 1])
        total = total + rx[d]
    rmsg[...] = total
    nq8 = s.nq * s.nvec
    for e in range(1, nz):
        go(
            rmsg, rall.at[c, pl.ds(pl.multiple_of(z * nq8, 8), nq8), :], rz_s.at[e - 1], rz_r.at[z], aux=(z + e) % nz,
        )
    rall[c, pl.ds(pl.multiple_of(z * nq8, 8), nq8), :] = total
    gather(1, range(3))
    for d in (1, 3):
        gathered(0, d)
        for w in range(side):
            v_copies[d, w].wait_recv()
        product(0, d)
        gather(1, range(3, 5) if d == 1 else range(5, 6))
    gathered(0, 2)
    for w in range(side):
        v_copies[2, w].wait_recv()
    reduce_start(0, 2)
    gather(1, range(6, nz))
    relay(1, nz - 2)
    relay(1, nz - 1)
    product(1, 0)
    reduce_merge(0)
    for d in (1, 3):
        gathered(1, d)
        product(1, d)
    gathered(1, 2)
    reduce_start(1, 2)
    for d in range(1, nz):
        source = (z + d) % nz
        arrived(rall.at[c, pl.ds(pl.multiple_of(source * nq8, 8), nq8), :], rz_r.at[source])
        arrived(sh.at[source], sh_r.at[source])
    go(rall.at[c], rall.at[c], rc_s, rc_r, occ=1 - c)
    reduce_merge(1)
    arrived(rall.at[1 - c], rc_r)
    for h in range(2):
        for part in range(s.parts):
            width = min(128, s.half - part * 128)
            rl[h, part, :, 0:width] = rall[h, :, part * 128 : part * 128 + width]
    for n in range(s.nvec):
        for h in range(2):
            halves = []
            for part in range(s.parts):
                rows = [rl[h, part, pl.ds(q * s.nvec + n, nz, stride=nq8), :] for q in range(s.nq)]
                halves.append(jnp.concatenate(rows, axis=0))
            rm32[n, h * s.half : (h + 1) * s.half, :] = jnp.concatenate(halves, axis=1).T[: s.half]
        rmf[n * s.nocc : (n + 1) * s.nocc, :] = rm32[n].astype(BF16)

    def build(group):
        j0, count = s.groups[group]
        pack = s.packs[group]
        for side_of in range(2):
            for part, rows in enumerate(parts_of(group)):
                arrived(bx[group].at[side_of, rows], b_r.at[group, side_of, part])

        @pl.loop(0, nz)
        def _(source):
            rows = pl.ds(pl.multiple_of(source * pack, 16), pack)
            value = acc[group][r, rows, :] + bx[group][0, rows, :].astype(F32) + bx[group][1, rows, :].astype(F32)
            value = value.astype(BF16).astype(F32)
            full = jnp.concatenate([value, jnp.zeros((pack, s.lanes - s.rows), F32)], axis=1)
            full = pltpu.roll(full, s.lanes - v, 1)
            for part in range(s.lanes // 128):
                bf[part, rows, :] = full[:, part * 128 : (part + 1) * 128]

        for j in range(count):
            parts = []
            for part in range(s.lanes // 128):
                rows = [bf[part, pl.ds(q * count + j, nz, stride=pack), :] for q in range(s.nq)]
                parts.append(jnp.concatenate(rows, axis=0))
            bflat[:, (j0 + j) * s.na : (j0 + j + 1) * s.na] = jnp.concatenate(parts, axis=1)[:, : s.na]

    bflat[:, s.tiles * s.tile - 128 :] = jnp.zeros((s.q, 128), F32)
    build(0)
    build(1)
    for tile in range(s.tiles):
        flat = bflat[:, tile * s.tile : (tile + 1) * s.tile]
        bj[tile] = flat.astype(BF16)
        bjt[tile] = flat.T.astype(BF16)
    for n in range(s.nvec):
        row[n * s.nocc : (n + 1) * s.nocc, :] = jnp.broadcast_to(sh[n][0:1, :], (s.nocc, 128)) - eob[...]
    for copy in started:
        copy.wait_send()


def fold_kernel(s, bj, bjt, base, rm, row, fl, fa, coupled0, coupled1, weighted0, weighted1):
    nz, tall = s.nz, 2 * s.nocc
    coupled, weighted = (coupled0, coupled1), (weighted0, weighted1)
    steps = s.pairs * s.tiles

    def couple(step, slot):
        rows = rm[pl.ds(pl.multiple_of(step // s.tiles * tall, 16), tall), :]
        coupled[slot][...] = dot(rows, bj[step % s.tiles])

    def weigh(step, slot):
        own = row[pl.ds(pl.multiple_of(step // s.tiles * tall, 8), tall), :]
        divisor = jnp.concatenate([own] * (s.tile // 128), axis=1) + base[step % s.tiles, 0:1, :]
        weighted[slot][...] = (coupled[slot][...] * pl.reciprocal(divisor, approx=True, full_range=False)).astype(BF16)

    def gather(step, slot):
        rows = pl.ds(pl.multiple_of(step // s.tiles * tall, 8), tall)
        fa[rows, :] += dot(weighted[slot][...], bjt[step % s.tiles])

    fa[...] = jnp.zeros(fa.shape, F32)
    couple(0, 0)
    couple(1, 1)
    weigh(0, 0)

    @pl.loop(1, steps // 2)
    def _(half):
        for slot in range(2):
            step = 2 * half + slot
            gather(step - 2, slot)
            weigh(step - 1, 1 - slot)
            couple(step, slot)

    gather(steps - 2, 0)
    weigh(steps - 1, 1)
    gather(steps - 1, 1)
    rows2 = 2 * s.nq

    @pl.loop(0, s.pairs)
    def _(p):
        for m in range(2):
            for h in range(2):
                start = pl.multiple_of(p * tall, 8) + m * s.nocc + h * s.half
                flip = fa[pl.ds(start, s.half), :].T
                flip = jnp.concatenate([flip, jnp.zeros((s.q, s.parts * 128 - s.half), F32)], axis=1)
                for part in range(s.parts):
                    for q in range(s.nq):
                        fl[p, h, part, pl.ds(m * s.nq + q, nz, stride=rows2), :] = flip[
                            q * nz : (q + 1) * nz, part * 128 : (part + 1) * 128
                        ]


def collect_kernel(
    s, fl, hq, sec, trial, eo_row, out,
    fx, fz, fr, fg, fgx, spart, sgs, sgr, spp, spr, t32,
    fc_s, fc_r, fz_s, fz_r, fg_s, fg_r, fx_s, fx_r, s1_s, s1_r, s2_s, s2_r,
):
    nz, side = s.nz, s.side
    z, c, v = lax.axis_index("aux"), lax.axis_index("occ"), lax.axis_index("vir")
    y, x = v // side, v % side
    g = y + c * (x - y)
    r = x + c * (y - x)
    sg = side - (side - 1) * c
    sr = 1 + (side - 1) * c

    def vid(gather, reduce):
        return gather * sg + reduce * sr

    started = []

    def go(*args, **device):
        copy = send(*args, **device)
        started.append(copy)
        return copy

    def arrived(dst, recv_sem):
        pltpu.make_async_remote_copy(
            src_ref=dst, dst_ref=dst, send_sem=recv_sem, recv_sem=recv_sem, device_id={"occ": c}, device_id_type=MESH
        ).wait_recv()

    barrier = pltpu.get_barrier_semaphore()
    me = 2 * z + c
    for d in range(1, 2 * nz):
        other = (me + d) % (2 * nz)
        pl.semaphore_signal(barrier, inc=1, device_id={"aux": other // 2, "occ": other % 2}, device_id_type=MESH)
    for d in range(1, side * side):
        pl.semaphore_signal(barrier, inc=1, device_id={"vir": (v + d) % (side * side)}, device_id_type=MESH)
    pl.semaphore_wait(barrier, 2 * nz + side * side - 2)
    t32[...] = trial[...].astype(F32)

    rows2 = 2 * s.nq
    go(fl.at[:, 1 - c], fx, fc_s, fc_r, occ=1 - c)
    arrived(fx, fc_r)
    fz[...] = fl[:, c] + fx[...]
    for d in range(1, nz):
        to = (z + d) % nz
        go(fz.at[:, :, pl.ds(pl.multiple_of(to * rows2, 8), rows2), :], fr.at[z], fz_s.at[d - 1], fz_r.at[z], aux=to)
    total = fz[:, :, pl.ds(pl.multiple_of(z * rows2, 8), rows2), :]
    for d in range(1, nz):
        source = (z + d) % nz
        arrived(fr.at[source], fz_r.at[source])
        total = total + fr[source]
    fg[0] = total
    for e in range(1, side):
        go(fg.at[0], fg.at[side - e], fg_s.at[e - 1], fg_r.at[side - e - 1], vir=vid((g + e) % side, r))
    total = fg[0]
    for d in range(1, side):
        arrived(fg.at[d], fg_r.at[d - 1])
        total = total + fg[d]
    fgx[0] = total
    for e in range(1, side):
        go(fgx.at[0], fgx.at[side - e], fx_s.at[e - 1], fx_r.at[side - e - 1], vir=vid(g, (r + e) % side))
    for d in range(1, side):
        arrived(fgx.at[d], fx_r.at[d - 1])
        total = total + fgx[d]

    tall = s.nvec * s.nq
    folded = jnp.concatenate([total[:, part].reshape(tall, 128) for part in range(s.parts)], axis=1)[:, : s.half]
    folded = split(folded)
    owner = lax.broadcasted_iota(jnp.int32, folded.shape, 0) % s.nq
    both = None
    for q in range(s.nq):
        term = dot(jnp.where(owner == q, folded.astype(F32), 0.0).astype(BF16), hq[q])
        both = term if both is None else both + term
    both = dot_nt(split(both[:tall] + both[tall:]), sec[...])
    spart[...] = both[:tall] + both[tall:]
    for n in range(s.nvec):
        value = spart[n * s.nq : n * s.nq + 1, :]
        for q in range(1, s.nq):
            value = value + spart[n * s.nq + q : n * s.nq + q + 1, :]
        sgs[n] = value
    for d in range(1, 2 * nz):
        other = (me + d) % (2 * nz)
        go(sgs.at[other // 2], sgr.at[me], s1_s.at[d - 1], s1_r.at[me], aux=other // 2, occ=other % 2)
    sgr[me] = sgs[z]
    for d in range(1, 2 * nz):
        other = (me + d) % (2 * nz)
        arrived(sgr.at[other], s1_r.at[other])
    total = sgr[0]
    for d in range(1, 2 * nz):
        total = total + sgr[d]
    spp[...] = total
    for d in range(1, side * side):
        go(spp, spr.at[v], s2_s.at[d - 1], s2_r.at[v], vir=(v + d) % (side * side))
    spr[v] = total
    for d in range(1, side * side):
        other = (v + d) % (side * side)
        arrived(spr.at[other], s2_r.at[other])
    total = spr[0]
    for d in range(1, side * side):
        total = total + spr[d]
    sigma = eo_row[...] * t32[pl.ds(z, 1), :] + total
    out[:, 0 : s.nocc] = sigma
    column = jnp.sum(t32[...] * sigma, axis=1, keepdims=True)
    out[:, s.nocc : s.nocc + s.nvec] = jnp.broadcast_to(column, (s.nvec, 128)).T[0:1]
    for copy in started:
        copy.wait_send()


def local(mesh, integrals, occ_coeffs, vir_coeffs, occ_energy, vir_energy, trial_vectors, shifts):
    s = Sizes(mesh, integrals, occ_coeffs, vir_energy)
    nz, side = s.nz, s.side
    vmem = pltpu.VMEM
    nq8 = s.nq * s.nvec
    rows2 = 2 * s.nq
    dma = lambda *shape: pltpu.SemaphoreType.DMA(shape)
    near = side - 1
    one = pltpu.SemaphoreType.DMA
    scratch = [
        vmem((s.nq, s.window, s.nu), BF16),
        vmem((s.nocc, s.ao), BF16),
        vmem((s.nq, s.nocc, s.nu), F32),
        vmem((s.nq, s.half, s.nu), F32),
        *[vmem((nz, pack, s.nu), F32) for pack in s.packs],
        *[vmem((nz, pack, s.nu), BF16) for pack in s.packs],
        *[vmem((side, nz, pack, s.nu), BF16) for pack in s.packs],
        vmem((side, side, s.rows, s.nu), BF16),
        *[vmem((side, nz * pack, s.rows), F32) for pack in s.packs],
        *[vmem((side - 1, nz * pack, s.rows), BF16) for pack in s.packs],
        *[vmem((2, nz * pack, s.rows), BF16) for pack in s.packs],
        *[vmem((2, nz * pack // 2, s.rows), BF16) for pack in s.packs],
        vmem((s.lanes // 128, nz * max(s.packs), 128), F32),
        vmem((s.q, s.tiles * s.tile), F32),
        vmem((s.nocc, 128), F32),
        vmem((8, s.lanes), F32),
        vmem((8, 128), F32),
        vmem((nq8, s.half), F32),
        vmem((side, nq8, s.half), F32),
        vmem((side, nq8, s.half), F32),
        vmem((nq8, s.half), F32),
        vmem((2, nz * nq8, s.half), F32),
        vmem((2, s.parts, nz * nq8, 128), F32),
        vmem((s.nvec, s.nocc, s.q), F32),
        vmem((nz, 8, 128), F32),
        dma(s.nq + 1), dma(side), dma(near, side), dma(near, side), dma(nz), dma(nz),
        dma(s.nq), dma(s.nq), dma(2, nz), dma(2, nz), dma(2, near, nz), dma(2, near, nz),
        dma(near), dma(near), dma(near), dma(near), dma(nz), dma(nz), one, one,
        dma(2, 2, 2), dma(2, 2, 2), dma(2, 2), dma(2, 2),
    ]
    hbm = pl.BlockSpec(memory_space=pl.ANY)
    fast = pl.BlockSpec(memory_space=pltpu.VMEM)
    scalars = pl.BlockSpec(memory_space=pltpu.SMEM)
    shape = jax.ShapeDtypeStruct
    limit = 56 * 1024 * 1024
    occ_row, trial_rows = occ_energy[None], trial_vectors.T
    bj, bjt, base, rm, row, hq, sec = pl.pallas_call(
        functools.partial(exchange_kernel, s),
        out_shape=(
            shape((s.tiles, s.q, s.tile), BF16),
            shape((s.tiles, s.tile, s.q), BF16),
            shape((s.tiles, 8, s.tile), F32),
            shape((s.nvec * s.nocc, s.q), BF16),
            shape((s.nvec * s.nocc, 128), F32),
            shape((s.nq, s.half, s.nu), BF16),
            shape((s.nocc, s.nu), BF16),
        ),
        in_specs=[hbm, hbm, hbm, fast, fast, scalars, fast, scalars],
        out_specs=(fast,) * 7,
        scratch_shapes=scratch,
        compiler_params=pltpu.CompilerParams(collective_id=0, has_side_effects=True, vmem_limit_bytes=limit),
    )(integrals, occ_coeffs.T, vir_coeffs.T, trial_rows, occ_row, occ_energy, vir_energy[None], shifts)
    tall = 2 * s.nocc
    folded = pl.pallas_call(
        functools.partial(fold_kernel, s),
        out_shape=shape((s.pairs, 2, s.parts, nz * rows2, 128), F32),
        in_specs=[fast] * 5,
        out_specs=fast,
        scratch_shapes=[
            vmem((s.nvec * s.nocc, s.q), F32),
            vmem((tall, s.tile), F32),
            vmem((tall, s.tile), F32),
            vmem((tall, s.tile), BF16),
            vmem((tall, s.tile), BF16),
        ],
        compiler_params=pltpu.CompilerParams(vmem_limit_bytes=limit),
    )(bj, bjt, base, rm, row)
    out = pl.pallas_call(
        functools.partial(collect_kernel, s),
        out_shape=shape((1, s.nocc + s.nvec), F32),
        in_specs=[fast] * 5,
        out_specs=fast,
        scratch_shapes=[
            vmem((s.pairs, s.parts, nz * rows2, 128), F32),
            vmem((s.pairs, s.parts, nz * rows2, 128), F32),
            vmem((nz, s.pairs, s.parts, rows2, 128), F32),
            vmem((side, s.pairs, s.parts, rows2, 128), F32),
            vmem((side, s.pairs, s.parts, rows2, 128), F32),
            vmem((nq8, s.nocc), F32),
            vmem((nz, 1, s.nocc), F32),
            vmem((2 * nz, 1, s.nocc), F32),
            vmem((1, s.nocc), F32),
            vmem((side * side, 1, s.nocc), F32),
            vmem((s.nvec, s.nocc), F32),
            one, one, dma(nz), dma(nz), dma(near), dma(near), dma(near), dma(near),
            dma(2 * nz), dma(2 * nz), dma(side * side), dma(side * side),
        ],
        compiler_params=pltpu.CompilerParams(collective_id=1, has_side_effects=True, vmem_limit_bytes=limit),
    )(folded, hq, sec, trial_rows, occ_row)
    return out[:, : s.nocc].T, out[:, s.nocc :].T


def solution(mesh):
    return jax.shard_map(
        functools.partial(local, dict(mesh.shape)),
        mesh=mesh,
        in_specs=(P("aux", "occ", "vir"), P(), P("vir", None), P(), P("vir"), P(), P("aux")),
        out_specs=(P(None, "aux"), P(None, "aux")),
        check_vma=False,
    )
```

time: 117 us -> 131 us (1.12)
  Pallas kernels: 113 us -> 127 us
    pallas_call x1 -> x3, Pallas kernels: 113 us -> 127 us  [the longest x1 62 us: local(): pl.pallas_call(functools.partial(exchange_kernel, s), out_shape=(shape((s...]
    transpose x0 -> x2, local copies, waits for them, and re-layouts: none -> 2.53 us  [local(): return (out[:, :s.nocc].T, out[:, s.nocc:].T)]
    unnamed x2 -> x0, local copies, waits for them, and re-layouts: 2.49 us -> none
where the time goes in v2:
time: 131 us; the launch traced here: 130 us
  Pallas kernels  127 us (97%)
  local copies, waits for them, and re-layouts  2.53 us (2%)
    pallas_call x1, Pallas kernels, local(): pl.pallas_call(functools.partial(exchange_kernel, s), out_shape=(shape((s...  62 us
    pallas_call x1, Pallas kernels, local(): pl.pallas_call(functools.partial(collect_kernel, s), out_shape=shape((1,...  36.6 us
    pallas_call x1, Pallas kernels, local(): pl.pallas_call(functools.partial(fold_kernel, s), out_shape=shape((s.pair...  28 us

profile of v2, /device:TPU:1, one launch (start us, length us, event | category | flops | bytes accessed | tf_op | source)
XLA Modules:
  0.0 130.4 jit_solution(5319630553944924947)
XLA Ops:
  1.3 62.0 %shard_map.86 = (bf16[11,32,512]{2,1,0:T(8,128)(2,1)}, bf16[11,512,32]{2,1,0:T(8,128)(2,1)}, f32[11,8,512]{2,1,0:T(8,128)}, bf16[3200,32]{1,0:T(8,128)(2,1)}, f3...) custom-call(bf16[4,2000,250]{2,1,0:T(8,128)(2,1)} %int_h.1, bf16[400,4000]{1,0:T(8,128)(2,1)} %bitcast.9, ...), custom_call_target="tpu_custom_call" | custom-call | tf_op jit(solution)/shard_map/pallas_call | solution.py:572
  63.2 28.0 %shard_map.87.fl = f32[4,2,2,64,128]{4,3,2,1,0:T(8,128)} custom-call(bf16[11,32,512]{2,1,0:T(8,128)(2,1)} %get-tuple-element.9.bj, bf16[11,512,32]{2,1,0:T(8,128)(2,1)} %get-tuple-element.10.bjt, f32[11,8,512]{2,1,0:T(8,128)} %get-tuple-element.11.base, bf16[3200,32]{1,0:T(8,128)(2,1)} %get-tuple-element.12.rm, f32[3200,128]{1,0:T(8,128)} %get-tuple-element.13.row), custom_call_target="tpu_custom_call" | custom-call | tf_op jit(solution)/shard_map/pallas_call | solution.py:589
  91.2 36.6 %shard_map.88 = f32[1,408]{1,0:T(1,128)} custom-call(f32[4,2,2,64,128]{4,3,2,1,0:T(8,128)} %shard_map.87.fl, bf16[4,200,250]{2,1,0:T(8,128)(2,1)} %get-tuple-element.14.hq, bf16[400,250]{1,0:T(8,128)(2,1)} %get-tuple-element.15.sec, bf16[8,400]{1,0:T(8,128)(2,1)} %bitcast.12, f32[1,400]{1,0:T(1,128)} %bitcast.14), custom_call_target="tpu_custom_call" | custom-call | tf_op jit(solution)/shard_map/pallas_call | solution.py:603
  127.9 1.3 slice_bitcast_fusion.1
  129.1 1.3 slice_bitcast_fusion

commit v3 on v1

v3 whole, which is shorter than its diff:
```python
import functools
import math

import jax
import jax.numpy as jnp
from jax import lax
from jax.experimental import pallas as pl
from jax.experimental.pallas import tpu as pltpu
from jax.sharding import PartitionSpec as P

MESH = pl.DeviceIdType.MESH
F32 = jnp.float32
BF16 = jnp.bfloat16


def dot(a, b):
    return jnp.dot(a, b, preferred_element_type=F32)


def dot_nt(a, b):
    return lax.dot_general(a, b, (((1,), (1,)), ((), ())), preferred_element_type=F32)


def split(value):
    high = value.astype(BF16)
    low = (value - high.astype(F32)).astype(BF16)
    return jnp.concatenate([high.astype(F32), low.astype(F32)], axis=0).astype(BF16)


def send(src, dst, send_sem, recv_sem, **device):
    copy = pltpu.make_async_remote_copy(
        src_ref=src, dst_ref=dst, send_sem=send_sem, recv_sem=recv_sem, device_id=device, device_id_type=MESH
    )
    copy.start()
    return copy


class Sizes:
    def __init__(self, mesh, integrals, occ_coeffs, vir_energy):
        self.nz = mesh["aux"]
        self.side = math.isqrt(mesh["vir"])
        self.nq, self.mu, self.nu = integrals.shape
        self.ao, self.nocc = occ_coeffs.shape
        self.half = self.nocc // 2
        self.jb = self.half // self.nz
        self.na = vir_energy.shape[0]
        self.block = 16 * (self.na // 16)
        self.rows = self.block + 16
        assert self.na == self.block + 1 and self.side == 4
        first = (self.jb + 1) // 2
        rows = -(-(self.nq * first) // 16) * 16
        self.groups = [(0, first), (first, self.jb - first)]
        rest = self.jb - first
        self.packs = (rows, -(-(self.nq * rest) // 16) * 16)
        self.tile = 512
        self.tiles = -(-(self.jb * self.na) // self.tile)
        self.early = first * self.na // self.tile
        self.pairs = self.nz // 2
        self.lane0 = self.mu // 128 * 128
        self.shift = self.mu - self.lane0
        self.window = self.mu + self.shift
        self.lanes = -(-self.rows // 128) * 128
        self.q = self.nq * self.nz
        self.nvec = self.nz
        self.parts = -(-self.half // 128)
        last = 128 * (self.nu * (mesh["vir"] - 1) // 128) - 128
        self.view = self.ao - last
        for v in range(mesh["vir"]):
            start = 128 * (self.nu * v // 128) - 128 * ((v + 1) // mesh["vir"])
            assert start + self.view <= self.ao and self.nu * v - start + self.nu <= self.view


def kernel(
    s, int_h, occ_h, vir_h, trial, eo_row, eo_s, ve, shift_s,
    out,
    bj, bjt, base, rm, row, hq, sec, fa, coupled0, coupled1, weighted0, weighted1,
    fl, fx, fz, fr, fg, fgx, spart, sgs, sgr, spp, spr,
    ibuf, occ_v, pf, xf, pk0, pk1, hs0, hs1, hg0, hg1, vb, acc0, acc1, bs0, bs1, bx0, bx1, bm0, bm1, bf, bflat, eob, ve8, shift,
    rp, rg, rx, rmsg, rall, rl, rm32, sh,
    in_sem, v_own, v_s, v_r, sh_s, sh_r, x_s, x_r, h_s, h_r, g_s, g_r, rg_s, rg_r, rx_s, rx_r, rz_s, rz_r, rc_s, rc_r,
    b_s, b_r, m_s, m_r, fc_s, fc_r, fz_s, fz_r, fg_s, fg_r, fx_s, fx_r, s1_s, s1_r, s2_s, s2_r,
):
    nz, side = s.nz, s.side
    z, c, v = lax.axis_index("aux"), lax.axis_index("occ"), lax.axis_index("vir")
    y, x = v // side, v % side
    g = y + c * (x - y)
    r = x + c * (y - x)
    sg = side - (side - 1) * c
    sr = 1 + (side - 1) * c

    def vid(gather, reduce):
        return gather * sg + reduce * sr

    pk, hs, hg, acc, bs, bx, bm = (pk0, pk1), (hs0, hs1), (hg0, hg1), (acc0, acc1), (bs0, bs1), (bx0, bx1), (bm0, bm1)
    started = []

    def go(*args, **device):
        copy = send(*args, **device)
        started.append(copy)
        return copy

    occ_in = pltpu.make_async_copy(occ_h, occ_v, in_sem.at[s.nq])
    occ_in.start()
    zero_rows = jnp.zeros((s.shift, s.nu), BF16)
    loads = []
    for q in range(s.nq):
        if s.shift:
            ibuf[q, 0 : s.shift, :] = zero_rows
            ibuf[q, s.mu : s.mu + s.shift, :] = zero_rows
        copy = pltpu.make_async_copy(
            int_h.at[q], ibuf.at[q, pl.ds(pl.multiple_of(s.shift * c, 16), s.mu), :], in_sem.at[q]
        )
        copy.start()
        loads.append(copy)
    own_v = []
    for w in range(side):
        start = pl.multiple_of(s.block * vid(g, w), 16)
        copy = pltpu.make_async_copy(
            vir_h.at[pl.ds(start, s.rows), :], vb.at[0, pl.ds(w * s.lanes, s.rows), :], v_own.at[w]
        )
        copy.start()
        own_v.append(copy)

    for group in range(2):
        pk[group][...] = jnp.zeros(pk[group].shape, F32)
    rp[...] = jnp.zeros(rp.shape, F32)
    for d in range(side):
        for w in range(side):
            vb[d, w * s.lanes + s.rows : (w + 1) * s.lanes, :] = jnp.zeros((s.lanes - s.rows, s.nu), BF16)

    barrier = pltpu.get_barrier_semaphore()
    me = 2 * z + c
    for d in range(1, 2 * nz):
        other = (me + d) % (2 * nz)
        pl.semaphore_signal(barrier, inc=1, device_id={"aux": other // 2, "occ": other % 2}, device_id_type=MESH)
    for d in range(1, side * side):
        pl.semaphore_signal(barrier, inc=1, device_id={"vir": (v + d) % (side * side)}, device_id_type=MESH)
    pl.semaphore_wait(barrier, 2 * nz + side * side - 2)

    v_copies = {}
    for e in range(1, side):
        to = (g + e) % side
        for w in range(side):
            start = pl.multiple_of(s.block * vid(to, w), 16)
            v_copies[side - e, w] = go(
                vir_h.at[pl.ds(start, s.rows), :], vb.at[side - e, pl.ds(w * s.lanes, s.rows), :], v_s.at[e - 1, w], v_r.at[side - e - 1, w],
                vir=vid(to, r),
            )
    shift[...] = jnp.full((8, 128), shift_s[0], F32)
    for e in range(1, nz):
        go(shift, sh.at[z], sh_s.at[e - 1], sh_r.at[z], aux=(z + e) % nz)
    sh[z] = shift[...]

    occ_in.wait()
    x_copies = []
    for q in range(s.nq):
        loads[q].wait()
        columns = occ_v[:, pl.ds(pl.multiple_of(s.lane0 * c, 128), s.window)]
        pf[q] = dot(columns, ibuf[q])
        x_copies.append(
            go(pf.at[q, pl.ds(pl.multiple_of(s.half * (1 - c), 8), s.half), :], xf.at[q], x_s.at[q], x_r.at[q], occ=1 - c)
        )
    start = 128 * ((s.nu * v) // 128) - 128 * ((v + 1) // (side * side))
    view = occ_v[:, pl.ds(pl.multiple_of(start, 128), s.view)].astype(F32)
    wide = -(-s.view // 128) * 128
    view = jnp.concatenate([view, jnp.zeros((s.nocc, wide - s.view), F32)], axis=1)
    sec[...] = pltpu.roll(view, wide - (s.nu * v - start), 1)[:, : s.nu].astype(BF16)
    weights = split(dot(trial[...], sec[...]))
    for q in range(s.nq):
        x_copies[q].wait_recv()
        xf[q] = xf[q] + pf[q, pl.ds(pl.multiple_of(s.half * c, 8), s.half), :]
    near_first = [d for pair in zip(range(1, nz // 2), range(nz - 1, nz // 2, -1)) for d in pair] + [nz // 2]
    for group in range(2):
        j0, count = s.groups[group]
        for q in range(s.nq):
            for to in range(nz):
                pk[group][to, q * count : (q + 1) * count, :] = xf[q, to * s.jb + j0 : to * s.jb + j0 + count, :]
        hs[group][...] = pk[group][...].astype(BF16)
        for e in near_first:
            to = (z + e) % nz
            go(hs[group].at[to], hg[group].at[0, z], h_s.at[group, e - 1], h_r.at[group, z], aux=to)
        hg[group][0, z] = hs[group][z]
    for q in range(s.nq):
        hq[q] = xf[q].astype(BF16)

    for q in range(s.nq):
        both = dot_nt(weights, hq[q])
        rp[q * s.nvec : (q + 1) * s.nvec, 0 : s.half] = both[: s.nvec] + both[s.nvec :]
    for e in range(1, side):
        go(rp, rg.at[side - e], rg_s.at[e - 1], rg_r.at[side - e - 1], vir=vid((g + e) % side, r))

    ve8[...] = jnp.ones(ve8.shape, F32)
    ve8[:, 0 : s.na] = jnp.broadcast_to(ve[...], (8, s.na))
    bflat[...] = jnp.ones(bflat.shape, F32)
    first = s.half * c + s.jb * z
    for j in range(s.jb):
        bflat[0:8, j * s.na : (j + 1) * s.na] = ve8[:, 0 : s.na] - eo_s[first + j]
    for tile in range(s.tiles):
        base[tile] = bflat[0:8, tile * s.tile : (tile + 1) * s.tile]
    square = jnp.broadcast_to(eo_row[...], (128, s.nocc))
    fill = -(-s.nocc // 128) * 128 - s.nocc
    eob[...] = jnp.concatenate([square, jnp.zeros((128, fill), F32)], axis=1).T[: s.nocc]

    def arrived(dst, recv_sem):
        pltpu.make_async_remote_copy(
            src_ref=dst, dst_ref=dst, send_sem=recv_sem, recv_sem=recv_sem, device_id={"occ": c}, device_id_type=MESH
        ).wait_recv()

    ahead, behind = vid((g + 1) % side, r), vid((g + 3) % side, r)
    halves = (pl.ds(0, nz // 2), pl.ds(nz // 2, nz // 2))

    def gather(group):
        for d in near_first:
            source = (z + d) % nz
            arrived(hg[group].at[0, source], h_r.at[group, source])
        for n in range(2):
            for to, slot, part in ((behind, 1, n), (ahead, 3, 1 - n)):
                part_ref = hg[group].at[0, halves[part]]
                go(
                    part_ref, hg[group].at[slot, halves[part]], g_s.at[group, slot - 1, part], g_r.at[group, slot - 1, part],
                    vir=to,
                )

    def relay(group):
        for slot, to, part in ((1, behind, 0), (3, ahead, 1)):
            arrived(hg[group].at[slot, halves[part]], g_r.at[group, slot - 1, part])
            go(
                hg[group].at[slot, halves[part]], hg[group].at[2, halves[part]], g_s.at[group, 1, part],
                g_r.at[group, 1, part], vir=to,
            )

    def gathered(group, slot):
        for part in range(2):
            if (slot, part) not in ((1, 0), (3, 1)):
                arrived(hg[group].at[slot, halves[part]], g_r.at[group, slot - 1, part])

    def term(group, d):
        return dot_nt(hg[group][d].reshape(nz * s.packs[group], s.nu), vb[d])

    def product(group, slots):
        value = term(group, slots[0])
        for d in slots[1:]:
            value = value + term(group, d)
        acc[group][...] = value if slots[0] == 0 else value + acc[group][...]

    def columns_of(w):
        return pl.ds(pl.multiple_of(w * s.lanes, 128), s.lanes)

    right, left = vid(g, (r + 1) % side), vid(g, (r + 3) % side)

    def parts_of(group):
        size = nz * s.packs[group] // 2
        return pl.ds(0, size), pl.ds(size, size)

    def reduce_start(group):
        low, high = parts_of(group)
        for e in (2, 1, 3):
            bs[group][e - 1] = acc[group][:, columns_of((r + e) % side)].astype(BF16)
            if e == 2:
                go(bs[group].at[1, low], bm[group].at[0], m_s.at[group, 0], m_r.at[group, 0], vir=right)
                go(bs[group].at[1, high], bm[group].at[1], m_s.at[group, 1], m_r.at[group, 1], vir=left)
            if e == 1:
                go(bs[group].at[0, high], bx[group].at[0, high], b_s.at[group, 0, 1], b_r.at[group, 0, 1], vir=right)
            if e == 3:
                go(bs[group].at[2, low], bx[group].at[1, low], b_s.at[group, 1, 0], b_r.at[group, 1, 0], vir=left)

    def reduce_merge(group):
        low, high = parts_of(group)
        arrived(bm[group].at[0], m_r.at[group, 0])
        merged = acc[group][low, columns_of((r + 1) % side)] + bm[group][0].astype(F32)
        bs[group][0, low, :] = merged.astype(BF16)
        go(bs[group].at[0, low], bx[group].at[0, low], b_s.at[group, 0, 0], b_r.at[group, 0, 0], vir=right)
        arrived(bm[group].at[1], m_r.at[group, 1])
        merged = acc[group][high, columns_of((r + 3) % side)] + bm[group][1].astype(F32)
        bs[group][2, high, :] = merged.astype(BF16)
        go(bs[group].at[2, high], bx[group].at[1, high], b_s.at[group, 1, 1], b_r.at[group, 1, 1], vir=left)

    nq8 = s.nq * s.nvec
    gather(0)
    total = rp[...]
    for d in range(1, side):
        arrived(rg.at[d], rg_r.at[d - 1])
        total = total + rg[d]
    rx[0] = total
    for e in range(1, side):
        go(rx.at[0], rx.at[side - e], rx_s.at[e - 1], rx_r.at[side - e - 1], vir=vid(g, (r + e) % side))
    for w in range(side):
        own_v[w].wait()
    product(0, (0,))
    relay(0)
    total = rx[0]
    for d in range(1, side):
        arrived(rx.at[d], rx_r.at[d - 1])
        total = total + rx[d]
    rmsg[...] = total.astype(BF16)
    own_rows = pl.ds(pl.multiple_of(z * nq8, 16), nq8)
    for e in near_first:
        go(rmsg, rall.at[c, own_rows, :], rz_s.at[e - 1], rz_r.at[z], aux=(z + e) % nz)
    rall[c, own_rows, :] = rmsg[...]
    gathered(0, 1)
    gathered(0, 3)
    for d in range(1, side):
        for w in range(side):
            v_copies[d, w].wait_recv()
    product(0, (1, 3))
    gather(1)
    gathered(0, 2)
    product(0, (2,))
    reduce_start(0)
    relay(1)
    product(1, (0,))
    reduce_merge(0)
    gathered(1, 1)
    gathered(1, 3)
    product(1, (1, 3))
    for d in near_first:
        source = (z + d) % nz
        arrived(rall.at[c, pl.ds(pl.multiple_of(source * nq8, 16), nq8), :], rz_r.at[source])
        arrived(sh.at[source], sh_r.at[source])
    go(rall.at[c], rall.at[c], rc_s, rc_r, occ=1 - c)
    gathered(1, 2)
    product(1, (2,))
    reduce_start(1)
    arrived(rall.at[1 - c], rc_r)
    for h in range(2):
        for part in range(s.parts):
            rl[h, part] = rall[h, :, part * 128 : (part + 1) * 128].astype(F32)
    for n in range(s.nvec):
        for h in range(2):
            sides = []
            for part in range(s.parts):
                rows = [rl[h, part, pl.ds(q * s.nvec + n, nz, stride=nq8), :] for q in range(s.nq)]
                sides.append(jnp.concatenate(rows, axis=0))
            rm32[n, h * s.half : (h + 1) * s.half, :] = jnp.concatenate(sides, axis=1).T[: s.half]
        rm[n * s.nocc : (n + 1) * s.nocc, :] = rm32[n].astype(BF16)
        row[n * s.nocc : (n + 1) * s.nocc, :] = jnp.broadcast_to(sh[n][0:1, :], (s.nocc, 128)) - eob[...]
    reduce_merge(1)

    def build(group):
        j0, count = s.groups[group]
        pack = s.packs[group]
        for side_of in range(2):
            for part, rows in enumerate(parts_of(group)):
                arrived(bx[group].at[side_of, rows], b_r.at[group, side_of, part])

        @pl.loop(0, nz)
        def _(source):
            rows = pl.ds(pl.multiple_of(source * pack, 16), pack)
            value = acc[group][rows, columns_of(r)] + bx[group][0, rows, :].astype(F32) + bx[group][1, rows, :].astype(F32)
            full = pltpu.roll(value.astype(BF16).astype(F32), s.lanes - v, 1)
            for part in range(s.lanes // 128):
                bf[part, rows, :] = full[:, part * 128 : (part + 1) * 128]

        for j in range(count):
            parts = []
            for part in range(s.lanes // 128):
                rows = [bf[part, pl.ds(q * count + j, nz, stride=pack), :] for q in range(s.nq)]
                parts.append(jnp.concatenate(rows, axis=0))
            bflat[:, (j0 + j) * s.na : (j0 + j + 1) * s.na] = jnp.concatenate(parts, axis=1)[:, : s.na]

    def tiles_ready(first_tile, last_tile):
        for tile in range(first_tile, last_tile):
            flat = bflat[:, tile * s.tile : (tile + 1) * s.tile]
            bj[tile] = flat.astype(BF16)
            bjt[tile] = flat.T.astype(BF16)

    tall = 2 * s.nocc
    coupled, weighted = (coupled0, coupled1), (weighted0, weighted1)

    def rows_of(step, tiles):
        return pl.ds(pl.multiple_of(step // tiles * tall, 16), tall)

    def couple(step, slot, start, tiles):
        coupled[slot][...] = dot(rm[rows_of(step, tiles), :], bj[start + step % tiles])

    def weigh(step, slot, start, tiles):
        own = row[rows_of(step, tiles), :]
        divisor = jnp.concatenate([own] * (s.tile // 128), axis=1) + base[start + step % tiles, 0:1, :]
        weighted[slot][...] = (coupled[slot][...] * pl.reciprocal(divisor, approx=True, full_range=False)).astype(BF16)

    def fold(step, slot, start, tiles):
        fa[rows_of(step, tiles), :] += dot(weighted[slot][...], bjt[start + step % tiles])

    def begin(*span):
        couple(0, 0, *span)
        couple(1, 1, *span)
        weigh(0, 0, *span)

    def advance(first, last, span):
        @pl.loop(first, last)
        def _(half):
            for slot in range(2):
                step = 2 * half + slot
                fold(step - 2, slot, *span)
                weigh(step - 1, 1 - slot, *span)
                couple(step, slot, *span)

    def end(steps, span):
        fold(steps - 2, 0, *span)
        weigh(steps - 1, 1, *span)
        fold(steps - 1, 1, *span)

    fa[...] = jnp.zeros(fa.shape, F32)
    build(0)
    tiles_ready(0, s.early)
    span = (0, s.early)
    steps = s.pairs * s.early
    begin(*span)
    advance(1, steps // 2, span)
    end(steps, span)

    rows2 = 2 * s.nq

    def to_core(p):
        return pltpu.make_async_remote_copy(
            src_ref=fl.at[p, 1 - c], dst_ref=fx.at[p], send_sem=fc_s.at[p], recv_sem=fc_r.at[p],
            device_id={"occ": 1 - c}, device_id_type=MESH,
        )

    def along_z(p, e):
        to = (z + e) % nz
        return pltpu.make_async_remote_copy(
            src_ref=fz.at[p, :, pl.ds(pl.multiple_of(to * rows2, 8), rows2), :], dst_ref=fr.at[p, z],
            send_sem=fz_s.at[p, e - 1], recv_sem=fz_r.at[p, z], device_id={"aux": to}, device_id_type=MESH,
        )

    def pass_on(p):
        to_core(p).wait_recv()
        fz[p] = fl[p, c] + fx[p]
        for e in near_first:
            along_z(p, e).start()

    def finish(p):
        for m in range(2):
            for h in range(2):
                start = pl.multiple_of(p * tall, 8) + m * s.nocc + h * s.half
                flip = fa[pl.ds(start, s.half), :].T
                flip = jnp.concatenate([flip, jnp.zeros((s.q, s.parts * 128 - s.half), F32)], axis=1)
                for part in range(s.parts):
                    for q in range(s.nq):
                        fl[p, h, part, pl.ds(m * s.nq + q, nz, stride=rows2), :] = flip[
                            q * nz : (q + 1) * nz, part * 128 : (part + 1) * 128
                        ]
        to_core(p).start()

    bflat[:, s.tiles * s.tile - 128 :] = jnp.zeros((s.q, 128), F32)
    build(1)
    tiles_ready(s.early, s.tiles)
    span = (s.early, s.tiles - s.early)
    each = (s.tiles - s.early) // 2
    begin(*span)

    @pl.loop(0, s.pairs)
    def _(p):
        advance(p * each + 1 - (p + s.pairs - 1) // s.pairs, (p + 1) * each, span)

        @pl.when(p > 0)
        def _():
            finish(p - 1)

        @pl.when(p > 1)
        def _():
            pass_on(p - 2)

    end(s.pairs * (s.tiles - s.early), span)
    finish(s.pairs - 1)
    pass_on(s.pairs - 2)
    for p in range(s.pairs - 1):
        total = fz[p, :, pl.ds(pl.multiple_of(z * rows2, 8), rows2), :]
        for d in near_first:
            source = (z + d) % nz
            arrived(fr.at[p, source], fz_r.at[p, source])
            total = total + fr[p, source]
        fg[0, p] = total
    pass_on(s.pairs - 1)
    for copy in started:
        copy.wait_send()
    started.clear()
    p = s.pairs - 1
    total = fz[p, :, pl.ds(pl.multiple_of(z * rows2, 8), rows2), :]
    for d in near_first:
        source = (z + d) % nz
        arrived(fr.at[p, source], fz_r.at[p, source])
        total = total + fr[p, source]
    fg[0, p] = total
    for e in range(1, side):
        go(fg.at[0], fg.at[side - e], fg_s.at[e - 1], fg_r.at[side - e - 1], vir=vid((g + e) % side, r))
    total = fg[0]
    for p in range(s.pairs):
        to_core(p).wait_send()
        for e in near_first:
            along_z(p, e).wait_send()
    for d in range(1, side):
        arrived(fg.at[d], fg_r.at[d - 1])
        total = total + fg[d]
    fgx[0] = total
    for e in range(1, side):
        go(fgx.at[0], fgx.at[side - e], fx_s.at[e - 1], fx_r.at[side - e - 1], vir=vid(g, (r + e) % side))
    for d in range(1, side):
        arrived(fgx.at[d], fx_r.at[d - 1])
        total = total + fgx[d]

    tall = nq8
    folded = jnp.concatenate([total[:, part].reshape(tall, 128) for part in range(s.parts)], axis=1)[:, : s.half]
    folded = split(folded)
    owner = lax.broadcasted_iota(jnp.int32, folded.shape, 0) % s.nq
    both = None
    for q in range(s.nq):
        term = dot(jnp.where(owner == q, folded.astype(F32), 0.0).astype(BF16), hq[q])
        both = term if both is None else both + term
    both = dot_nt(split(both[:tall] + both[tall:]), sec[...])
    spart[...] = both[:tall] + both[tall:]
    for n in range(s.nvec):
        value = spart[n * s.nq : n * s.nq + 1, :]
        for q in range(1, s.nq):
            value = value + spart[n * s.nq + q : n * s.nq + q + 1, :]
        sgs[n] = value
    for d in range(1, 2 * nz):
        other = (me + d) % (2 * nz)
        go(sgs.at[other // 2], sgr.at[me], s1_s.at[d - 1], s1_r.at[me], aux=other // 2, occ=other % 2)
    sgr[me] = sgs[z]
    for d in range(1, 2 * nz):
        other = (me + d) % (2 * nz)
        arrived(sgr.at[other], s1_r.at[other])
    total = sgr[0]
    for d in range(1, 2 * nz):
        total = total + sgr[d]
    spp[...] = total
    for d in range(1, side * side):
        go(spp, spr.at[v], s2_s.at[d - 1], s2_r.at[v], vir=(v + d) % (side * side))
    spr[v] = total
    for d in range(1, side * side):
        other = (v + d) % (side * side)
        arrived(spr.at[other], s2_r.at[other])
    total = spr[0]
    for d in range(1, side * side):
        total = total + spr[d]
    out[...] = total
    for copy in started:
        copy.wait_send()


def output_kernel(terms, trial, eo_row, sigma_out, sub_out, t32):
    t32[...] = trial[...].astype(F32)
    sigma = eo_row[...] * t32[pl.ds(lax.axis_index("aux"), 1), :] + terms[...]
    sigma_out[...] = sigma
    column = jnp.sum(t32[...] * sigma, axis=1, keepdims=True)
    sub_out[...] = jnp.broadcast_to(column, (column.shape[0], 128)).T[0:1]


def local(mesh, integrals, occ_coeffs, vir_coeffs, occ_energy, vir_energy, trial_vectors, shifts):
    s = Sizes(mesh, integrals, occ_coeffs, vir_energy)
    nz, side = s.nz, s.side
    vmem = pltpu.VMEM
    nq8 = s.nq * s.nvec
    rows2 = 2 * s.nq
    dma = lambda *shape: pltpu.SemaphoreType.DMA(shape)
    near = side - 1
    one = pltpu.SemaphoreType.DMA
    tall = 2 * s.nocc
    flat = s.parts * 128
    scratch = [
        vmem((s.tiles, s.q, s.tile), BF16),
        vmem((s.tiles, s.tile, s.q), BF16),
        vmem((s.tiles, 8, s.tile), F32),
        vmem((s.nvec * s.nocc, s.q), BF16),
        vmem((s.nvec * s.nocc, 128), F32),
        vmem((s.nq, s.half, s.nu), BF16),
        vmem((s.nocc, s.nu), BF16),
        vmem((s.nvec * s.nocc, s.q), F32),
        vmem((tall, s.tile), F32),
        vmem((tall, s.tile), F32),
        vmem((tall, s.tile), BF16),
        vmem((tall, s.tile), BF16),
        vmem((s.pairs, 2, s.parts, nz * rows2, 128), F32),
        vmem((s.pairs, s.parts, nz * rows2, 128), F32),
        vmem((s.pairs, s.parts, nz * rows2, 128), F32),
        vmem((s.pairs, nz, s.parts, rows2, 128), F32),
        vmem((side, s.pairs, s.parts, rows2, 128), F32),
        vmem((side, s.pairs, s.parts, rows2, 128), F32),
        vmem((nq8, s.nocc), F32),
        vmem((nz, 1, s.nocc), F32),
        vmem((2 * nz, 1, s.nocc), F32),
        vmem((1, s.nocc), F32),
        vmem((side * side, 1, s.nocc), F32),
        vmem((s.nq, s.window, s.nu), BF16),
        vmem((s.nocc, s.ao), BF16),
        vmem((s.nq, s.nocc, s.nu), F32),
        vmem((s.nq, s.half, s.nu), F32),
        *[vmem((nz, pack, s.nu), F32) for pack in s.packs],
        *[vmem((nz, pack, s.nu), BF16) for pack in s.packs],
        *[vmem((side, nz, pack, s.nu), BF16) for pack in s.packs],
        vmem((side, side * s.lanes, s.nu), BF16),
        *[vmem((nz * pack, side * s.lanes), F32) for pack in s.packs],
        *[vmem((side - 1, nz * pack, s.lanes), BF16) for pack in s.packs],
        *[vmem((2, nz * pack, s.lanes), BF16) for pack in s.packs],
        *[vmem((2, nz * pack // 2, s.lanes), BF16) for pack in s.packs],
        vmem((s.lanes // 128, nz * max(s.packs), 128), F32),
        vmem((s.q, s.tiles * s.tile), F32),
        vmem((s.nocc, 128), F32),
        vmem((8, s.lanes), F32),
        vmem((8, 128), F32),
        vmem((nq8, flat), F32),
        vmem((side, nq8, flat), F32),
        vmem((side, nq8, flat), F32),
        vmem((nq8, flat), BF16),
        vmem((2, nz * nq8, flat), BF16),
        vmem((2, s.parts, nz * nq8, 128), F32),
        vmem((s.nvec, s.nocc, s.q), F32),
        vmem((nz, 8, 128), F32),
        dma(s.nq + 1), dma(side), dma(near, side), dma(near, side), dma(nz), dma(nz),
        dma(s.nq), dma(s.nq), dma(2, nz), dma(2, nz), dma(2, near, 2), dma(2, near, 2),
        dma(near), dma(near), dma(near), dma(near), dma(nz), dma(nz), one, one,
        dma(2, 2, 2), dma(2, 2, 2), dma(2, 2), dma(2, 2),
        dma(s.pairs), dma(s.pairs), dma(s.pairs, nz), dma(s.pairs, nz),
        dma(near), dma(near), dma(near), dma(near), dma(2 * nz), dma(2 * nz), dma(side * side), dma(side * side),
    ]
    hbm = pl.BlockSpec(memory_space=pl.ANY)
    fast = pl.BlockSpec(memory_space=pltpu.VMEM)
    scalars = pl.BlockSpec(memory_space=pltpu.SMEM)
    shape = jax.ShapeDtypeStruct
    limit = 56 * 1024 * 1024
    occ_row, trial_rows = occ_energy[None], trial_vectors.T
    terms = pl.pallas_call(
        functools.partial(kernel, s),
        out_shape=shape((1, s.nocc), F32),
        in_specs=[hbm, hbm, hbm, fast, fast, scalars, fast, scalars],
        out_specs=fast,
        scratch_shapes=scratch,
        compiler_params=pltpu.CompilerParams(collective_id=0, has_side_effects=True, vmem_limit_bytes=limit),
    )(integrals, occ_coeffs.T, vir_coeffs.T, trial_rows, occ_row, occ_energy, vir_energy[None], shifts)
    sigma, sub = pl.pallas_call(
        output_kernel,
        out_shape=(shape((1, s.nocc), F32), shape((1, s.nvec), F32)),
        in_specs=[fast] * 3,
        out_specs=(fast, fast),
        scratch_shapes=[vmem((s.nvec, s.nocc), F32)],
    )(terms, trial_rows, occ_row)
    return sigma.T, sub.T


def solution(mesh):
    return jax.shard_map(
        functools.partial(local, dict(mesh.shape)),
        mesh=mesh,
        in_specs=(P("aux", "occ", "vir"), P(), P("vir", None), P(), P("vir"), P(), P("aux")),
        out_specs=(P(None, "aux"), P(None, "aux")),
        check_vma=False,
    )
```

time: 117 us -> 110 us (0.940)
  Pallas kernels: 113 us -> 109 us
  local copies, waits for them, and re-layouts: 2.49 us -> 0 us
    pallas_call x1 -> x2, Pallas kernels: 113 us -> 109 us  [the longest x1 108 us: local(): pl.pallas_call(functools.partial(kernel, s), out_shape=shape((1, s.nocc),...]
    unnamed x2 -> x0, local copies, waits for them, and re-layouts: 2.49 us -> none
where the time goes in v3:
time: 110 us
  Pallas kernels  109 us (99%)
  between operations  1.29 us (1%)
    pallas_call x1, Pallas kernels, local(): pl.pallas_call(functools.partial(kernel, s), out_shape=shape((1, s.nocc),...  108 us

profile of v3, /device:TPU:1, one launch (start us, length us, event | category | flops | bytes accessed | tf_op | source)
XLA Modules:
  0.0 110.2 jit_solution(593458814111248640)
XLA Ops:
  1.3 107.6 %shard_map.86.terms = f32[1,400]{1,0:T(1,128)} custom-call(bf16[4,2000,250]{2,1,0:T(8,128)(2,1)} %int_h.1, bf16[400,4000]{1,0:T(8,128)(2,1)} %bitcast.7, bf16[3600,250]{1,0:T(8,128)(2,1)} %bitcast.8, bf16[8,400]{1,0:T(8,128)(2,1)} %bitcast.9, f32[1,400]{1,0:T(1,128)} %bitcast.11, f32[400]{0:T(512)} %eo_s.1, f32[1,225]{1,0:T(1,128)} %bitcast.13, ...), custom_call_target="tpu_custom_call" | custom-call | tf_op jit(solution)/shard_map/pallas_call | solution.py:624
  108.8 1.4 %shard_map.87 = (f32[1,400]{1,0:T(1,128)}, f32[1,8]{1,0:T(1,128)}) custom-call(f32[1,400]{1,0:T(1,128)} %shard_map.86.terms, bf16[8,400]{1,0:T(8,128)(2,1)} %bitcast.10, f32[1,400]{1,0:T(1,128)} %bitcast.12), custom_call_target="tpu_custom_call" | custom-call | tf_op jit(solution)/shard_map/pallas_call | solution.py:632

commit v4 on v3

--- a/solution.py
+++ b/solution.py
@@ -55,7 +55,7 @@
         self.tile = 512
         self.tiles = -(-(self.jb * self.na) // self.tile)
         self.early = first * self.na // self.tile
-        self.pairs = self.nz // 2
+        self.quads = self.nz // 4
         self.lane0 = self.mu // 128 * 128
         self.shift = self.mu - self.lane0
         self.window = self.mu + self.shift
@@ -74,11 +74,11 @@
     s, int_h, occ_h, vir_h, trial, eo_row, eo_s, ve, shift_s,
     out,
     bj, bjt, base, rm, row, hq, sec, fa, coupled0, coupled1, weighted0, weighted1,
-    fl, fx, fz, fr, fg, fgx, spart, sgs, sgr, spp, spr,
+    hp, fl, fb, fr, fp, fq, spart, sgs, sgr, spp, spr,
     ibuf, occ_v, pf, xf, pk0, pk1, hs0, hs1, hg0, hg1, vb, acc0, acc1, bs0, bs1, bx0, bx1, bm0, bm1, bf, bflat, eob, ve8, shift,
     rp, rg, rx, rmsg, rall, rl, rm32, sh,
     in_sem, v_own, v_s, v_r, sh_s, sh_r, x_s, x_r, h_s, h_r, g_s, g_r, rg_s, rg_r, rx_s, rx_r, rz_s, rz_r, rc_s, rc_r,
-    b_s, b_r, m_s, m_r, fc_s, fc_r, fz_s, fz_r, fg_s, fg_r, fx_s, fx_r, s1_s, s1_r, s2_s, s2_r,
+    b_s, b_r, m_s, m_r, fz_s, fz_r, fp_s, fp_r, s1_s, s1_r, s2_s, s2_r,
 ):
     nz, side = s.nz, s.side
     z, c, v = lax.axis_index("aux"), lax.axis_index("occ"), lax.axis_index("vir")
@@ -183,6 +183,8 @@
     for q in range(s.nq):
         hq[q] = xf[q].astype(BF16)
 
+    for q in range(s.nq):
+        hp[q] = dot_nt(hq[q], sec[...]).astype(BF16)
     for q in range(s.nq):
         both = dot_nt(weights, hq[q])
         rp[q * s.nvec : (q + 1) * s.nvec, 0 : s.half] = both[: s.nvec] + both[s.nvec :]
@@ -364,7 +366,7 @@
             bj[tile] = flat.astype(BF16)
             bjt[tile] = flat.T.astype(BF16)
 
-    tall = 2 * s.nocc
+    tall = 4 * s.nocc
     coupled, weighted = (coupled0, coupled1), (weighted0, weighted1)
 
     def rows_of(step, tiles):
@@ -386,14 +388,16 @@
         couple(1, 1, *span)
         weigh(0, 0, *span)
 
-    def advance(first, last, span):
-        @pl.loop(first, last)
+    def advance(last, span, after=None):
+        @pl.loop(1, last)
         def _(half):
             for slot in range(2):
                 step = 2 * half + slot
                 fold(step - 2, slot, *span)
                 weigh(step - 1, 1 - slot, *span)
                 couple(step, slot, *span)
+            if after is not None:
+                after(half)
 
     def end(steps, span):
         fold(steps - 2, 0, *span)
@@ -404,117 +408,105 @@
     build(0)
     tiles_ready(0, s.early)
     span = (0, s.early)
-    steps = s.pairs * s.early
+    steps = s.quads * s.early
     begin(*span)
-    advance(1, steps // 2, span)
+    advance(steps // 2, span)
     end(steps, span)
 
-    rows2 = 2 * s.nq
-
-    def to_core(p):
+    rows4 = 4 * s.nq
+    around = side * side
+
+    def to_owner(u, d):
+        other = (me + d) % (2 * nz)
         return pltpu.make_async_remote_copy(
-            src_ref=fl.at[p, 1 - c], dst_ref=fx.at[p], send_sem=fc_s.at[p], recv_sem=fc_r.at[p],
-            device_id={"occ": 1 - c}, device_id_type=MESH,
+            src_ref=fb.at[u, other % 2, pl.ds(pl.multiple_of(other // 2 * rows4, 16), rows4), :], dst_ref=fr.at[u, me],
+            send_sem=fz_s.at[u, d - 1], recv_sem=fz_r.at[u, me],
+            device_id={"aux": other // 2, "occ": other % 2}, device_id_type=MESH,
         )
 
-    def along_z(p, e):
-        to = (z + e) % nz
+    def to_plane(u, d):
         return pltpu.make_async_remote_copy(
-            src_ref=fz.at[p, :, pl.ds(pl.multiple_of(to * rows2, 8), rows2), :], dst_ref=fr.at[p, z],
-            send_sem=fz_s.at[p, e - 1], recv_sem=fz_r.at[p, z], device_id={"aux": to}, device_id_type=MESH,
+            src_ref=fp.at[u], dst_ref=fq.at[u, v], send_sem=fp_s.at[u, d - 1], recv_sem=fp_r.at[u, v],
+            device_id={"vir": (v + d) % around}, device_id_type=MESH,
         )
 
-    def pass_on(p):
-        to_core(p).wait_recv()
-        fz[p] = fl[p, c] + fx[p]
-        for e in near_first:
-            along_z(p, e).start()
-
-    def finish(p):
-        for m in range(2):
+    def finish(u):
+        for m in range(4):
             for h in range(2):
-                start = pl.multiple_of(p * tall, 8) + m * s.nocc + h * s.half
-                flip = fa[pl.ds(start, s.half), :].T
+                start = u * tall + m * s.nocc + h * s.half
+                flip = fa[start : start + s.half, :].T
                 flip = jnp.concatenate([flip, jnp.zeros((s.q, s.parts * 128 - s.half), F32)], axis=1)
                 for part in range(s.parts):
                     for q in range(s.nq):
-                        fl[p, h, part, pl.ds(m * s.nq + q, nz, stride=rows2), :] = flip[
+                        fl[h, part, pl.ds(m * s.nq + q, nz, stride=rows4), :] = flip[
                             q * nz : (q + 1) * nz, part * 128 : (part + 1) * 128
                         ]
-        to_core(p).start()
+        for h in range(2):
+            fb[u, h] = jnp.concatenate([fl[h, part] for part in range(s.parts)], axis=1).astype(BF16)
+        for d in range(1, 2 * nz):
+            to_owner(u, d).start()
+        fr[u, me] = fb[u, c, pl.ds(pl.multiple_of(z * rows4, 16), rows4), :]
+
+    def pass_on(u):
+        for d in range(1, 2 * nz):
+            other = (me + d) % (2 * nz)
+            arrived(fr.at[u, other], fz_r.at[u, other])
+        total = fr[u, 0].astype(F32)
+        for other in range(1, 2 * nz):
+            total = total + fr[u, other].astype(F32)
+        fp[u] = total.astype(BF16)
+        for d in range(1, around):
+            to_plane(u, d).start()
+        fq[u, v] = fp[u]
+
+    def apply(u):
+        for d in range(1, around):
+            other = (v + d) % around
+            arrived(fq.at[u, other], fp_r.at[u, other])
+        total = fq[u, 0].astype(F32)
+        for other in range(1, around):
+            total = total + fq[u, other].astype(F32)
+        folded = split(total[:, : s.half])
+        owner = lax.broadcasted_iota(jnp.int32, folded.shape, 0) % s.nq
+        both = None
+        for q in range(s.nq):
+            value = dot(jnp.where(owner == q, folded.astype(F32), 0.0).astype(BF16), hp[q])
+            both = value if both is None else both + value
+        spart[...] = both[:rows4] + both[rows4:]
+        for m in range(4):
+            value = spart[m * s.nq : m * s.nq + 1, :]
+            for q in range(1, s.nq):
+                value = value + spart[m * s.nq + q : m * s.nq + q + 1, :]
+            sgs[4 * u + m] = value
 
     bflat[:, s.tiles * s.tile - 128 :] = jnp.zeros((s.q, 128), F32)
     build(1)
     tiles_ready(s.early, s.tiles)
-    span = (s.early, s.tiles - s.early)
-    each = (s.tiles - s.early) // 2
+    late = s.tiles - s.early
+    span = (s.early, late)
     begin(*span)
 
-    @pl.loop(0, s.pairs)
-    def _(p):
-        advance(p * each + 1 - (p + s.pairs - 1) // s.pairs, (p + 1) * each, span)
-
-        @pl.when(p > 0)
+    def serve(half):
+        @pl.when(half == late // 2)
         def _():
-            finish(p - 1)
-
-        @pl.when(p > 1)
+            finish(0)
+
+        @pl.when(half == late - 1)
         def _():
-            pass_on(p - 2)
-
-    end(s.pairs * (s.tiles - s.early), span)
-    finish(s.pairs - 1)
-    pass_on(s.pairs - 2)
-    for p in range(s.pairs - 1):
-        total = fz[p, :, pl.ds(pl.multiple_of(z * rows2, 8), rows2), :]
-        for d in near_first:
-            source = (z + d) % nz
-            arrived(fr.at[p, source], fz_r.at[p, source])
-            total = total + fr[p, source]
-        fg[0, p] = total
-    pass_on(s.pairs - 1)
+            pass_on(0)
+
+    advance(late, span, serve)
+    end(2 * late, span)
+    finish(1)
     for copy in started:
         copy.wait_send()
     started.clear()
-    p = s.pairs - 1
-    total = fz[p, :, pl.ds(pl.multiple_of(z * rows2, 8), rows2), :]
-    for d in near_first:
-        source = (z + d) % nz
-        arrived(fr.at[p, source], fz_r.at[p, source])
-        total = total + fr[p, source]
-    fg[0, p] = total
-    for e in range(1, side):
-        go(fg.at[0], fg.at[side - e], fg_s.at[e - 1], fg_r.at[side - e - 1], vir=vid((g + e) % side, r))
-    total = fg[0]
-    for p in range(s.pairs):
-        to_core(p).wait_send()
-        for e in near_first:
-            along_z(p, e).wait_send()
-    for d in range(1, side):
-        arrived(fg.at[d], fg_r.at[d - 1])
-        total = total + fg[d]
-    fgx[0] = total
-    for e in range(1, side):
-        go(fgx.at[0], fgx.at[side - e], fx_s.at[e - 1], fx_r.at[side - e - 1], vir=vid(g, (r + e) % side))
-    for d in range(1, side):
-        arrived(fgx.at[d], fx_r.at[d - 1])
-        total = total + fgx[d]
-
-    tall = nq8
-    folded = jnp.concatenate([total[:, part].reshape(tall, 128) for part in range(s.parts)], axis=1)[:, : s.half]
-    folded = split(folded)
-    owner = lax.broadcasted_iota(jnp.int32, folded.shape, 0) % s.nq
-    both = None
-    for q in range(s.nq):
-        term = dot(jnp.where(owner == q, folded.astype(F32), 0.0).astype(BF16), hq[q])
-        both = term if both is None else both + term
-    both = dot_nt(split(both[:tall] + both[tall:]), sec[...])
-    spart[...] = both[:tall] + both[tall:]
-    for n in range(s.nvec):
-        value = spart[n * s.nq : n * s.nq + 1, :]
-        for q in range(1, s.nq):
-            value = value + spart[n * s.nq + q : n * s.nq + q + 1, :]
-        sgs[n] = value
+    apply(0)
+    pass_on(1)
+    for u in range(2):
+        for d in range(1, 2 * nz):
+            to_owner(u, d).wait_send()
+    apply(1)
     for d in range(1, 2 * nz):
         other = (me + d) % (2 * nz)
         go(sgs.at[other // 2], sgr.at[me], s1_s.at[d - 1], s1_r.at[me], aux=other // 2, occ=other % 2)
@@ -538,6 +530,9 @@
     out[...] = total
     for copy in started:
         copy.wait_send()
+    for u in range(2):
+        for d in range(1, around):
+            to_plane(u, d).wait_send()
 
 
 def output_kernel(terms, trial, eo_row, sigma_out, sub_out, t32):
@@ -553,11 +548,11 @@
     nz, side = s.nz, s.side
     vmem = pltpu.VMEM
     nq8 = s.nq * s.nvec
-    rows2 = 2 * s.nq
+    rows4 = 4 * s.nq
     dma = lambda *shape: pltpu.SemaphoreType.DMA(shape)
     near = side - 1
     one = pltpu.SemaphoreType.DMA
-    tall = 2 * s.nocc
+    tall = 4 * s.nocc
     flat = s.parts * 128
     scratch = [
         vmem((s.tiles, s.q, s.tile), BF16),
@@ -572,13 +567,13 @@
         vmem((tall, s.tile), F32),
         vmem((tall, s.tile), BF16),
         vmem((tall, s.tile), BF16),
-        vmem((s.pairs, 2, s.parts, nz * rows2, 128), F32),
-        vmem((s.pairs, s.parts, nz * rows2, 128), F32),
-        vmem((s.pairs, s.parts, nz * rows2, 128), F32),
-        vmem((s.pairs, nz, s.parts, rows2, 128), F32),
-        vmem((side, s.pairs, s.parts, rows2, 128), F32),
-        vmem((side, s.pairs, s.parts, rows2, 128), F32),
-        vmem((nq8, s.nocc), F32),
+        vmem((s.nq, s.half, s.nocc), BF16),
+        vmem((2, s.parts, nz * rows4, 128), F32),
+        vmem((s.quads, 2, nz * rows4, flat), BF16),
+        vmem((s.quads, 2 * nz, rows4, flat), BF16),
+        vmem((s.quads, rows4, flat), BF16),
+        vmem((s.quads, side * side, rows4, flat), BF16),
+        vmem((rows4, s.nocc), F32),
         vmem((nz, 1, s.nocc), F32),
         vmem((2 * nz, 1, s.nocc), F32),
         vmem((1, s.nocc), F32),
@@ -612,8 +607,7 @@
         dma(s.nq), dma(s.nq), dma(2, nz), dma(2, nz), dma(2, near, 2), dma(2, near, 2),
         dma(near), dma(near), dma(near), dma(near), dma(nz), dma(nz), one, one,
         dma(2, 2, 2), dma(2, 2, 2), dma(2, 2), dma(2, 2),
-        dma(s.pairs), dma(s.pairs), dma(s.pairs, nz), dma(s.pairs, nz),
-        dma(near), dma(near), dma(near), dma(near), dma(2 * nz), dma(2 * nz), dma(side * side), dma(side * side),
+        dma(s.quads, 2 * nz), dma(s.quads, 2 * nz), dma(s.quads, side * side), dma(s.quads, side * side), dma(2 * nz), dma(2 * nz), dma(side * side), dma(side * side),
     ]
     hbm = pl.BlockSpec(memory_space=pl.ANY)
     fast = pl.BlockSpec(memory_space=pltpu.VMEM)

time: 110 us -> 102 us (0.927)
  Pallas kernels: 109 us -> 101 us
    pallas_call x1, Pallas kernels: 108 us -> 99.2 us  [local(): pl.pallas_call(functools.partial(kernel, s), out_shape=shape((1, s.nocc),...]
where the time goes in v4:
time: 102 us
  Pallas kernels  101 us (99%)
  between operations  1.29 us (1%)
    pallas_call x1, Pallas kernels, local(): pl.pallas_call(functools.partial(kernel, s), out_shape=shape((1, s.nocc),...  99.2 us

profile of v4, /device:TPU:1, one launch (start us, length us, event | category | flops | bytes accessed | tf_op | source)
XLA Modules:
  0.0 101.8 jit_solution(2189658269541350371)
XLA Ops:
  1.3 99.2 %shard_map.86.terms = f32[1,400]{1,0:T(1,128)} custom-call(bf16[4,2000,250]{2,1,0:T(8,128)(2,1)} %int_h.1, bf16[400,4000]{1,0:T(8,128)(2,1)} %bitcast.7, bf16[3600,250]{1,0:T(8,128)(2,1)} %bitcast.8, bf16[8,400]{1,0:T(8,128)(2,1)} %bitcast.9, f32[1,400]{1,0:T(1,128)} %bitcast.11, f32[400]{0:T(512)} %eo_s.1, f32[1,225]{1,0:T(1,128)} %bitcast.13, ...), custom_call_target="tpu_custom_call" | custom-call | tf_op jit(solution)/shard_map/pallas_call | solution.py:618
  100.4 1.4 %shard_map.87 = (f32[1,400]{1,0:T(1,128)}, f32[1,8]{1,0:T(1,128)}) custom-call(f32[1,400]{1,0:T(1,128)} %shard_map.86.terms, bf16[8,400]{1,0:T(8,128)(2,1)} %bitcast.10, f32[1,400]{1,0:T(1,128)} %bitcast.12), custom_call_target="tpu_custom_call" | custom-call | tf_op jit(solution)/shard_map/pallas_call | solution.py:626

commit v5 on v4

--- a/solution.py
+++ b/solution.py
@@ -47,14 +47,13 @@
         self.block = 16 * (self.na // 16)
         self.rows = self.block + 16
         assert self.na == self.block + 1 and self.side == 4
-        first = (self.jb + 1) // 2
-        rows = -(-(self.nq * first) // 16) * 16
-        self.groups = [(0, first), (first, self.jb - first)]
-        rest = self.jb - first
-        self.packs = (rows, -(-(self.nq * rest) // 16) * 16)
+        third = self.jb // 12 * 4
+        self.groups = [(0, third), (third, third), (2 * third, self.jb - 2 * third)]
+        self.packs = [-(-(self.nq * count) // 16) * 16 for _, count in self.groups]
         self.tile = 512
         self.tiles = -(-(self.jb * self.na) // self.tile)
-        self.early = first * self.na // self.tile
+        ends = [(j0 + count) * self.na // self.tile for j0, count in self.groups[:-1]] + [self.tiles]
+        self.spans = [(start, end - start) for start, end in zip([0] + ends, ends)]
         self.quads = self.nz // 4
         self.lane0 = self.mu // 128 * 128
         self.shift = self.mu - self.lane0
@@ -75,7 +74,8 @@
     out,
     bj, bjt, base, rm, row, hq, sec, fa, coupled0, coupled1, weighted0, weighted1,
     hp, fl, fb, fr, fp, fq, spart, sgs, sgr, spp, spr,
-    ibuf, occ_v, pf, xf, pk0, pk1, hs0, hs1, hg0, hg1, vb, acc0, acc1, bs0, bs1, bx0, bx1, bm0, bm1, bf, bflat, eob, ve8, shift,
+    ibuf, occ_v, pf, xf, pk0, pk1, pk2, hs0, hs1, hs2, hg0, hg1, hg2, vb,
+    acc0, acc1, acc2, bs0, bs1, bs2, bx0, bx1, bx2, bm0, bm1, bm2, bf, bflat, eob, ve8, shift,
     rp, rg, rx, rmsg, rall, rl, rm32, sh,
     in_sem, v_own, v_s, v_r, sh_s, sh_r, x_s, x_r, h_s, h_r, g_s, g_r, rg_s, rg_r, rx_s, rx_r, rz_s, rz_r, rc_s, rc_r,
     b_s, b_r, m_s, m_r, fz_s, fz_r, fp_s, fp_r, s1_s, s1_r, s2_s, s2_r,
@@ -91,7 +91,8 @@
     def vid(gather, reduce):
         return gather * sg + reduce * sr
 
-    pk, hs, hg, acc, bs, bx, bm = (pk0, pk1), (hs0, hs1), (hg0, hg1), (acc0, acc1), (bs0, bs1), (bx0, bx1), (bm0, bm1)
+    pk, hs, hg, acc = (pk0, pk1, pk2), (hs0, hs1, hs2), (hg0, hg1, hg2), (acc0, acc1, acc2)
+    bs, bx, bm = (bs0, bs1, bs2), (bx0, bx1, bx2), (bm0, bm1, bm2)
     started = []
 
     def go(*args, **device):
@@ -121,7 +122,7 @@
         copy.start()
         own_v.append(copy)
 
-    for group in range(2):
+    for group in range(3):
         pk[group][...] = jnp.zeros(pk[group].shape, F32)
     rp[...] = jnp.zeros(rp.shape, F32)
     for d in range(side):
@@ -160,36 +161,39 @@
         x_copies.append(
             go(pf.at[q, pl.ds(pl.multiple_of(s.half * (1 - c), 8), s.half), :], xf.at[q], x_s.at[q], x_r.at[q], occ=1 - c)
         )
+    for q in range(s.nq):
+        x_copies[q].wait_recv()
+        xf[q] = xf[q] + pf[q, pl.ds(pl.multiple_of(s.half * c, 8), s.half), :]
+        for group, (j0, count) in enumerate(s.groups):
+            for to in range(nz):
+                pk[group][to, q * count : (q + 1) * count, :] = xf[q, to * s.jb + j0 : to * s.jb + j0 + count, :]
+    near_first = [d for pair in zip(range(1, nz // 2), range(nz - 1, nz // 2, -1)) for d in pair] + [nz // 2]
+
+    def scatter(group):
+        hs[group][...] = pk[group][...].astype(BF16)
+        for e in near_first:
+            to = (z + e) % nz
+            go(hs[group].at[to], hg[group].at[0, z], h_s.at[group, e - 1], h_r.at[group, z], aux=to)
+        hg[group][0, z] = hs[group][z]
+
+    scatter(0)
+    scatter(1)
+    for q in range(s.nq):
+        hq[q] = xf[q].astype(BF16)
     start = 128 * ((s.nu * v) // 128) - 128 * ((v + 1) // (side * side))
     view = occ_v[:, pl.ds(pl.multiple_of(start, 128), s.view)].astype(F32)
     wide = -(-s.view // 128) * 128
     view = jnp.concatenate([view, jnp.zeros((s.nocc, wide - s.view), F32)], axis=1)
     sec[...] = pltpu.roll(view, wide - (s.nu * v - start), 1)[:, : s.nu].astype(BF16)
     weights = split(dot(trial[...], sec[...]))
-    for q in range(s.nq):
-        x_copies[q].wait_recv()
-        xf[q] = xf[q] + pf[q, pl.ds(pl.multiple_of(s.half * c, 8), s.half), :]
-    near_first = [d for pair in zip(range(1, nz // 2), range(nz - 1, nz // 2, -1)) for d in pair] + [nz // 2]
-    for group in range(2):
-        j0, count = s.groups[group]
-        for q in range(s.nq):
-            for to in range(nz):
-                pk[group][to, q * count : (q + 1) * count, :] = xf[q, to * s.jb + j0 : to * s.jb + j0 + count, :]
-        hs[group][...] = pk[group][...].astype(BF16)
-        for e in near_first:
-            to = (z + e) % nz
-            go(hs[group].at[to], hg[group].at[0, z], h_s.at[group, e - 1], h_r.at[group, z], aux=to)
-        hg[group][0, z] = hs[group][z]
-    for q in range(s.nq):
-        hq[q] = xf[q].astype(BF16)
-
-    for q in range(s.nq):
-        hp[q] = dot_nt(hq[q], sec[...]).astype(BF16)
+
     for q in range(s.nq):
         both = dot_nt(weights, hq[q])
         rp[q * s.nvec : (q + 1) * s.nvec, 0 : s.half] = both[: s.nvec] + both[s.nvec :]
     for e in range(1, side):
         go(rp, rg.at[side - e], rg_s.at[e - 1], rg_r.at[side - e - 1], vir=vid((g + e) % side, r))
+    for q in range(s.nq):
+        hp[q] = dot_nt(hq[q], sec[...]).astype(BF16)
 
     ve8[...] = jnp.ones(ve8.shape, F32)
     ve8[:, 0 : s.na] = jnp.broadcast_to(ve[...], (8, s.na))
@@ -278,7 +282,6 @@
         go(bs[group].at[2, high], bx[group].at[1, high], b_s.at[group, 1, 1], b_r.at[group, 1, 1], vir=left)
 
     nq8 = s.nq * s.nvec
-    gather(0)
     total = rp[...]
     for d in range(1, side):
         arrived(rg.at[d], rg_r.at[d - 1])
@@ -286,10 +289,7 @@
     rx[0] = total
     for e in range(1, side):
         go(rx.at[0], rx.at[side - e], rx_s.at[e - 1], rx_r.at[side - e - 1], vir=vid(g, (r + e) % side))
-    for w in range(side):
-        own_v[w].wait()
-    product(0, (0,))
-    relay(0)
+    gather(0)
     total = rx[0]
     for d in range(1, side):
         arrived(rx.at[d], rx_r.at[d - 1])
@@ -299,30 +299,36 @@
     for e in near_first:
         go(rmsg, rall.at[c, own_rows, :], rz_s.at[e - 1], rz_r.at[z], aux=(z + e) % nz)
     rall[c, own_rows, :] = rmsg[...]
+    scatter(2)
+    for w in range(side):
+        own_v[w].wait()
+    product(0, (0,))
+    relay(0)
+    gather(1)
     gathered(0, 1)
     gathered(0, 3)
     for d in range(1, side):
         for w in range(side):
             v_copies[d, w].wait_recv()
     product(0, (1, 3))
-    gather(1)
     gathered(0, 2)
     product(0, (2,))
     reduce_start(0)
+    product(1, (0,))
     relay(1)
-    product(1, (0,))
     reduce_merge(0)
     gathered(1, 1)
     gathered(1, 3)
     product(1, (1, 3))
+    gathered(1, 2)
+    product(1, (2,))
+    reduce_start(1)
     for d in near_first:
         source = (z + d) % nz
         arrived(rall.at[c, pl.ds(pl.multiple_of(source * nq8, 16), nq8), :], rz_r.at[source])
         arrived(sh.at[source], sh_r.at[source])
     go(rall.at[c], rall.at[c], rc_s, rc_r, occ=1 - c)
-    gathered(1, 2)
-    product(1, (2,))
-    reduce_start(1)
+    gather(2)
     arrived(rall.at[1 - c], rc_r)
     for h in range(2):
         for part in range(s.parts):
@@ -337,6 +343,8 @@
         rm[n * s.nocc : (n + 1) * s.nocc, :] = rm32[n].astype(BF16)
         row[n * s.nocc : (n + 1) * s.nocc, :] = jnp.broadcast_to(sh[n][0:1, :], (s.nocc, 128)) - eob[...]
     reduce_merge(1)
+    product(2, (0,))
+    relay(2)
 
     def build(group):
         j0, count = s.groups[group]
@@ -360,8 +368,10 @@
                 parts.append(jnp.concatenate(rows, axis=0))
             bflat[:, (j0 + j) * s.na : (j0 + j + 1) * s.na] = jnp.concatenate(parts, axis=1)[:, : s.na]
 
-    def tiles_ready(first_tile, last_tile):
-        for tile in range(first_tile, last_tile):
+    def ready(group):
+        build(group)
+        start, count = s.spans[group]
+        for tile in range(start, start + count):
             flat = bflat[:, tile * s.tile : (tile + 1) * s.tile]
             bj[tile] = flat.astype(BF16)
             bjt[tile] = flat.T.astype(BF16)
@@ -383,35 +393,51 @@
     def fold(step, slot, start, tiles):
         fa[rows_of(step, tiles), :] += dot(weighted[slot][...], bjt[start + step % tiles])
 
-    def begin(*span):
-        couple(0, 0, *span)
-        couple(1, 1, *span)
-        weigh(0, 0, *span)
-
-    def advance(last, span, after=None):
-        @pl.loop(1, last)
+    def half_step(half, span):
+        for slot in range(2):
+            step = 2 * half + slot
+            fold(step - 2, slot, *span)
+            weigh(step - 1, 1 - slot, *span)
+            couple(step, slot, *span)
+
+    def advance(span, after=None):
+        @pl.loop(1, span[1])
         def _(half):
-            for slot in range(2):
-                step = 2 * half + slot
-                fold(step - 2, slot, *span)
-                weigh(step - 1, 1 - slot, *span)
-                couple(step, slot, *span)
+            half_step(half, span)
             if after is not None:
                 after(half)
 
-    def end(steps, span):
-        fold(steps - 2, 0, *span)
-        weigh(steps - 1, 1, *span)
-        fold(steps - 1, 1, *span)
+    def bridge(span, later):
+        last = 2 * span[1] - 1
+        fold(last - 1, 0, *span)
+        weigh(last, 1, *span)
+        couple(0, 0, *later)
+        fold(last, 1, *span)
+        weigh(0, 0, *later)
+        couple(1, 1, *later)
 
     fa[...] = jnp.zeros(fa.shape, F32)
-    build(0)
-    tiles_ready(0, s.early)
-    span = (0, s.early)
-    steps = s.quads * s.early
-    begin(*span)
-    advance(steps // 2, span)
-    end(steps, span)
+    bflat[:, s.tiles * s.tile - 128 :] = jnp.zeros((s.q, 128), F32)
+    ready(0)
+    spans = s.spans
+    couple(0, 0, *spans[0])
+    couple(1, 1, *spans[0])
+    weigh(0, 0, *spans[0])
+    for half in range(1, spans[0][1]):
+        half_step(half, spans[0])
+        if half == 1:
+            gathered(2, 1)
+            gathered(2, 3)
+            product(2, (1, 3))
+            gathered(2, 2)
+            product(2, (2,))
+            reduce_start(2)
+    reduce_merge(2)
+    ready(1)
+    bridge(spans[0], spans[1])
+    advance(spans[1])
+    ready(2)
+    bridge(spans[1], spans[2])
 
     rows4 = 4 * s.nq
     around = side * side
@@ -479,12 +505,7 @@
                 value = value + spart[m * s.nq + q : m * s.nq + q + 1, :]
             sgs[4 * u + m] = value
 
-    bflat[:, s.tiles * s.tile - 128 :] = jnp.zeros((s.q, 128), F32)
-    build(1)
-    tiles_ready(s.early, s.tiles)
-    late = s.tiles - s.early
-    span = (s.early, late)
-    begin(*span)
+    late = spans[2][1]
 
     def serve(half):
         @pl.when(half == late // 2)
@@ -495,8 +516,10 @@
         def _():
             pass_on(0)
 
-    advance(late, span, serve)
-    end(2 * late, span)
+    advance(spans[2], serve)
+    fold(2 * late - 2, 0, *spans[2])
+    weigh(2 * late - 1, 1, *spans[2])
+    fold(2 * late - 1, 1, *spans[2])
     finish(1)
     for copy in started:
         copy.wait_send()
@@ -604,9 +627,9 @@
         vmem((s.nvec, s.nocc, s.q), F32),
         vmem((nz, 8, 128), F32),
         dma(s.nq + 1), dma(side), dma(near, side), dma(near, side), dma(nz), dma(nz),
-        dma(s.nq), dma(s.nq), dma(2, nz), dma(2, nz), dma(2, near, 2), dma(2, near, 2),
+        dma(s.nq), dma(s.nq), dma(3, nz), dma(3, nz), dma(3, near, 2), dma(3, near, 2),
         dma(near), dma(near), dma(near), dma(near), dma(nz), dma(nz), one, one,
-        dma(2, 2, 2), dma(2, 2, 2), dma(2, 2), dma(2, 2),
+        dma(3, 2, 2), dma(3, 2, 2), dma(3, 2), dma(3, 2),
         dma(s.quads, 2 * nz), dma(s.quads, 2 * nz), dma(s.quads, side * side), dma(s.quads, side * side), dma(2 * nz), dma(2 * nz), dma(side * side), dma(side * side),
     ]
     hbm = pl.BlockSpec(memory_space=pl.ANY)

time: 102 us -> 104 us (1.020)
  Pallas kernels: 101 us -> 103 us
    pallas_call x1, Pallas kernels: 99.2 us -> 101 us  [local(): pl.pallas_call(functools.partial(kernel, s), out_shape=shape((1, s.nocc),...]
where the time goes in v5:
time: 104 us
  Pallas kernels  103 us (99%)
  between operations  1.29 us (1%)
    pallas_call x1, Pallas kernels, local(): pl.pallas_call(functools.partial(kernel, s), out_shape=shape((1, s.nocc),...  101 us

profile of v5, /device:TPU:1, one launch (start us, length us, event | category | flops | bytes accessed | tf_op | source)
XLA Modules:
  0.0 104.2 jit_solution(5732099989139280459)
XLA Ops:
  1.3 101.5 %shard_map.86.terms = f32[1,400]{1,0:T(1,128)} custom-call(bf16[4,2000,250]{2,1,0:T(8,128)(2,1)} %int_h.1, bf16[400,4000]{1,0:T(8,128)(2,1)} %bitcast.7, bf16[3600,250]{1,0:T(8,128)(2,1)} %bitcast.8, bf16[8,400]{1,0:T(8,128)(2,1)} %bitcast.9, f32[1,400]{1,0:T(1,128)} %bitcast.11, f32[400]{0:T(512)} %eo_s.1, f32[1,225]{1,0:T(1,128)} %bitcast.13, ...), custom_call_target="tpu_custom_call" | custom-call | tf_op jit(solution)/shard_map/pallas_call | solution.py:641
  102.8 1.4 %shard_map.87 = (f32[1,400]{1,0:T(1,128)}, f32[1,8]{1,0:T(1,128)}) custom-call(f32[1,400]{1,0:T(1,128)} %shard_map.86.terms, bf16[8,400]{1,0:T(8,128)(2,1)} %bitcast.10, f32[1,400]{1,0:T(1,128)} %bitcast.12), custom_call_target="tpu_custom_call" | custom-call | tf_op jit(solution)/shard_map/pallas_call | solution.py:649

commit v6 on v5

--- a/solution.py
+++ b/solution.py
@@ -27,12 +27,10 @@
     return jnp.concatenate([high.astype(F32), low.astype(F32)], axis=0).astype(BF16)
 
 
-def send(src, dst, send_sem, recv_sem, **device):
-    copy = pltpu.make_async_remote_copy(
+def remote(src, dst, send_sem, recv_sem, **device):
+    return pltpu.make_async_remote_copy(
         src_ref=src, dst_ref=dst, send_sem=send_sem, recv_sem=recv_sem, device_id=device, device_id_type=MESH
     )
-    copy.start()
-    return copy
 
 
 class Sizes:
@@ -78,7 +76,7 @@
     acc0, acc1, acc2, bs0, bs1, bs2, bx0, bx1, bx2, bm0, bm1, bm2, bf, bflat, eob, ve8, shift,
     rp, rg, rx, rmsg, rall, rl, rm32, sh,
     in_sem, v_own, v_s, v_r, sh_s, sh_r, x_s, x_r, h_s, h_r, g_s, g_r, rg_s, rg_r, rx_s, rx_r, rz_s, rz_r, rc_s, rc_r,
-    b_s, b_r, m_s, m_r, fz_s, fz_r, fp_s, fp_r, s1_s, s1_r, s2_s, s2_r,
+    b_s, b_r, m_r, fz_s, fz_r, fp_s, fp_r, s1_s, s1_r, s2_s, s2_r,
 ):
     nz, side = s.nz, s.side
     z, c, v = lax.axis_index("aux"), lax.axis_index("occ"), lax.axis_index("vir")
@@ -93,35 +91,45 @@
 
     pk, hs, hg, acc = (pk0, pk1, pk2), (hs0, hs1, hs2), (hg0, hg1, hg2), (acc0, acc1, acc2)
     bs, bx, bm = (bs0, bs1, bs2), (bx0, bx1, bx2), (bm0, bm1, bm2)
-    started = []
+    me = 2 * z + c
+    around = side * side
+
+    def fan(first, last, copy):
+        @pl.loop(first, last)
+        def _(d):
+            copy(d).start()
 
     def go(*args, **device):
-        copy = send(*args, **device)
-        started.append(copy)
-        return copy
+        remote(*args, **device).start()
+
+    def arrived(ref, sem):
+        remote(ref, ref, sem, sem, occ=c).wait_recv()
+
+    def sent(ref, sem):
+        remote(ref, ref, sem, sem, occ=c).wait_send()
 
     occ_in = pltpu.make_async_copy(occ_h, occ_v, in_sem.at[s.nq])
     occ_in.start()
     zero_rows = jnp.zeros((s.shift, s.nu), BF16)
-    loads = []
+
+    def load(q):
+        return pltpu.make_async_copy(
+            int_h.at[q], ibuf.at[q, pl.ds(pl.multiple_of(s.shift * c, 16), s.mu), :], in_sem.at[q]
+        )
+
     for q in range(s.nq):
         if s.shift:
             ibuf[q, 0 : s.shift, :] = zero_rows
             ibuf[q, s.mu : s.mu + s.shift, :] = zero_rows
-        copy = pltpu.make_async_copy(
-            int_h.at[q], ibuf.at[q, pl.ds(pl.multiple_of(s.shift * c, 16), s.mu), :], in_sem.at[q]
-        )
-        copy.start()
-        loads.append(copy)
-    own_v = []
-    for w in range(side):
-        start = pl.multiple_of(s.block * vid(g, w), 16)
-        copy = pltpu.make_async_copy(
-            vir_h.at[pl.ds(start, s.rows), :], vb.at[0, pl.ds(w * s.lanes, s.rows), :], v_own.at[w]
-        )
-        copy.start()
-        own_v.append(copy)
-
+    fan(0, s.nq, load)
+
+    def window(gather, w):
+        return vir_h.at[pl.ds(pl.multiple_of(s.block * vid(gather, w), 16), s.rows), :]
+
+    def place(slot, w):
+        return vb.at[slot, pl.ds(pl.multiple_of(w * s.lanes, 16), s.rows), :]
+
+    fan(0, side, lambda w: pltpu.make_async_copy(window(g, w), place(0, w), v_own))
     for group in range(3):
         pk[group][...] = jnp.zeros(pk[group].shape, F32)
     rp[...] = jnp.zeros(rp.shape, F32)
@@ -130,50 +138,53 @@
             vb[d, w * s.lanes + s.rows : (w + 1) * s.lanes, :] = jnp.zeros((s.lanes - s.rows, s.nu), BF16)
 
     barrier = pltpu.get_barrier_semaphore()
-    me = 2 * z + c
-    for d in range(1, 2 * nz):
+
+    @pl.loop(1, 2 * nz)
+    def _(d):
         other = (me + d) % (2 * nz)
         pl.semaphore_signal(barrier, inc=1, device_id={"aux": other // 2, "occ": other % 2}, device_id_type=MESH)
-    for d in range(1, side * side):
-        pl.semaphore_signal(barrier, inc=1, device_id={"vir": (v + d) % (side * side)}, device_id_type=MESH)
-    pl.semaphore_wait(barrier, 2 * nz + side * side - 2)
-
-    v_copies = {}
-    for e in range(1, side):
+
+    @pl.loop(1, around)
+    def _(d):
+        pl.semaphore_signal(barrier, inc=1, device_id={"vir": (v + d) % around}, device_id_type=MESH)
+
+    pl.semaphore_wait(barrier, 2 * nz + around - 2)
+
+    def v_copy(d):
+        e, w = 1 + d // side, d % side
         to = (g + e) % side
-        for w in range(side):
-            start = pl.multiple_of(s.block * vid(to, w), 16)
-            v_copies[side - e, w] = go(
-                vir_h.at[pl.ds(start, s.rows), :], vb.at[side - e, pl.ds(w * s.lanes, s.rows), :], v_s.at[e - 1, w], v_r.at[side - e - 1, w],
-                vir=vid(to, r),
-            )
+        return remote(window(to, w), place(side - e, w), v_s, v_r, vir=vid(to, r))
+
+    fan(0, (side - 1) * side, v_copy)
     shift[...] = jnp.full((8, 128), shift_s[0], F32)
-    for e in range(1, nz):
-        go(shift, sh.at[z], sh_s.at[e - 1], sh_r.at[z], aux=(z + e) % nz)
+    fan(1, nz, lambda d: remote(shift, sh.at[z], sh_s, sh_r, aux=(z + d) % nz))
     sh[z] = shift[...]
 
     occ_in.wait()
-    x_copies = []
-    for q in range(s.nq):
-        loads[q].wait()
+
+    @pl.loop(0, s.nq)
+    def _(q):
+        load(q).wait()
         columns = occ_v[:, pl.ds(pl.multiple_of(s.lane0 * c, 128), s.window)]
         pf[q] = dot(columns, ibuf[q])
-        x_copies.append(
-            go(pf.at[q, pl.ds(pl.multiple_of(s.half * (1 - c), 8), s.half), :], xf.at[q], x_s.at[q], x_r.at[q], occ=1 - c)
-        )
+        theirs = pf.at[q, pl.ds(pl.multiple_of(s.half * (1 - c), 8), s.half), :]
+        go(theirs, xf.at[q], x_s, x_r.at[q], occ=1 - c)
+
     for q in range(s.nq):
-        x_copies[q].wait_recv()
+        arrived(xf.at[q], x_r.at[q])
         xf[q] = xf[q] + pf[q, pl.ds(pl.multiple_of(s.half * c, 8), s.half), :]
         for group, (j0, count) in enumerate(s.groups):
             for to in range(nz):
                 pk[group][to, q * count : (q + 1) * count, :] = xf[q, to * s.jb + j0 : to * s.jb + j0 + count, :]
-    near_first = [d for pair in zip(range(1, nz // 2), range(nz - 1, nz // 2, -1)) for d in pair] + [nz // 2]
 
     def scatter(group):
         hs[group][...] = pk[group][...].astype(BF16)
-        for e in near_first:
-            to = (z + e) % nz
-            go(hs[group].at[to], hg[group].at[0, z], h_s.at[group, e - 1], h_r.at[group, z], aux=to)
+
+        def copy(d):
+            to = (z + d) % nz
+            return remote(hs[group].at[to], hg[group].at[0, z], h_s.at[group], h_r.at[group], aux=to)
+
+        fan(1, nz, copy)
         hg[group][0, z] = hs[group][z]
 
     scatter(0)
@@ -190,8 +201,13 @@
     for q in range(s.nq):
         both = dot_nt(weights, hq[q])
         rp[q * s.nvec : (q + 1) * s.nvec, 0 : s.half] = both[: s.nvec] + both[s.nvec :]
-    for e in range(1, side):
-        go(rp, rg.at[side - e], rg_s.at[e - 1], rg_r.at[side - e - 1], vir=vid((g + e) % side, r))
+    def to_gather(d):
+        return remote(rp, rg.at[side - d], rg_s, rg_r, vir=vid((g + d) % side, r))
+
+    def to_reduce(d):
+        return remote(rx.at[0], rx.at[side - d], rx_s, rx_r, vir=vid(g, (r + d) % side))
+
+    fan(1, side, to_gather)
     for q in range(s.nq):
         hp[q] = dot_nt(hq[q], sec[...]).astype(BF16)
 
@@ -207,38 +223,26 @@
     fill = -(-s.nocc // 128) * 128 - s.nocc
     eob[...] = jnp.concatenate([square, jnp.zeros((128, fill), F32)], axis=1).T[: s.nocc]
 
-    def arrived(dst, recv_sem):
-        pltpu.make_async_remote_copy(
-            src_ref=dst, dst_ref=dst, send_sem=recv_sem, recv_sem=recv_sem, device_id={"occ": c}, device_id_type=MESH
-        ).wait_recv()
-
     ahead, behind = vid((g + 1) % side, r), vid((g + 3) % side, r)
     halves = (pl.ds(0, nz // 2), pl.ds(nz // 2, nz // 2))
 
     def gather(group):
-        for d in near_first:
-            source = (z + d) % nz
-            arrived(hg[group].at[0, source], h_r.at[group, source])
-        for n in range(2):
-            for to, slot, part in ((behind, 1, n), (ahead, 3, 1 - n)):
-                part_ref = hg[group].at[0, halves[part]]
-                go(
-                    part_ref, hg[group].at[slot, halves[part]], g_s.at[group, slot - 1, part], g_r.at[group, slot - 1, part],
-                    vir=to,
-                )
+        arrived(hg[group].at[0, pl.ds(0, nz - 1)], h_r.at[group])
+        for to, slot, part, sem in ((behind, 1, 0, 0), (ahead, 3, 1, 1), (behind, 1, 1, 2), (ahead, 3, 0, 2)):
+            block = hg[group].at[0, halves[part]]
+            go(block, hg[group].at[slot, halves[part]], g_s.at[group], g_r.at[group, sem], vir=to)
 
     def relay(group):
         for slot, to, part in ((1, behind, 0), (3, ahead, 1)):
-            arrived(hg[group].at[slot, halves[part]], g_r.at[group, slot - 1, part])
-            go(
-                hg[group].at[slot, halves[part]], hg[group].at[2, halves[part]], g_s.at[group, 1, part],
-                g_r.at[group, 1, part], vir=to,
-            )
-
-    def gathered(group, slot):
-        for part in range(2):
-            if (slot, part) not in ((1, 0), (3, 1)):
-                arrived(hg[group].at[slot, halves[part]], g_r.at[group, slot - 1, part])
+            block = hg[group].at[slot, halves[part]]
+            arrived(block, g_r.at[group, part])
+            go(block, hg[group].at[2, halves[part]], g_s.at[group], g_r.at[group, 3], vir=to)
+
+    def near_in(group):
+        arrived(hg[group].at[1], g_r.at[group, 2])
+
+    def far_in(group):
+        arrived(hg[group].at[2], g_r.at[group, 3])
 
     def term(group, d):
         return dot_nt(hg[group][d].reshape(nz * s.packs[group], s.nu), vb[d])
@@ -263,70 +267,60 @@
         for e in (2, 1, 3):
             bs[group][e - 1] = acc[group][:, columns_of((r + e) % side)].astype(BF16)
             if e == 2:
-                go(bs[group].at[1, low], bm[group].at[0], m_s.at[group, 0], m_r.at[group, 0], vir=right)
-                go(bs[group].at[1, high], bm[group].at[1], m_s.at[group, 1], m_r.at[group, 1], vir=left)
+                go(bs[group].at[1, low], bm[group].at[0], b_s.at[group], m_r.at[group], vir=right)
+                go(bs[group].at[1, high], bm[group].at[1], b_s.at[group], m_r.at[group], vir=left)
             if e == 1:
-                go(bs[group].at[0, high], bx[group].at[0, high], b_s.at[group, 0, 1], b_r.at[group, 0, 1], vir=right)
+                go(bs[group].at[0, high], bx[group].at[0, high], b_s.at[group], b_r.at[group], vir=right)
             if e == 3:
-                go(bs[group].at[2, low], bx[group].at[1, low], b_s.at[group, 1, 0], b_r.at[group, 1, 0], vir=left)
+                go(bs[group].at[2, low], bx[group].at[1, low], b_s.at[group], b_r.at[group], vir=left)
 
     def reduce_merge(group):
         low, high = parts_of(group)
-        arrived(bm[group].at[0], m_r.at[group, 0])
+        arrived(bm[group], m_r.at[group])
         merged = acc[group][low, columns_of((r + 1) % side)] + bm[group][0].astype(F32)
         bs[group][0, low, :] = merged.astype(BF16)
-        go(bs[group].at[0, low], bx[group].at[0, low], b_s.at[group, 0, 0], b_r.at[group, 0, 0], vir=right)
-        arrived(bm[group].at[1], m_r.at[group, 1])
+        go(bs[group].at[0, low], bx[group].at[0, low], b_s.at[group], b_r.at[group], vir=right)
         merged = acc[group][high, columns_of((r + 3) % side)] + bm[group][1].astype(F32)
         bs[group][2, high, :] = merged.astype(BF16)
-        go(bs[group].at[2, high], bx[group].at[1, high], b_s.at[group, 1, 1], b_r.at[group, 1, 1], vir=left)
+        go(bs[group].at[2, high], bx[group].at[1, high], b_s.at[group], b_r.at[group], vir=left)
 
     nq8 = s.nq * s.nvec
+    arrived(rg.at[pl.ds(1, side - 1)], rg_r)
     total = rp[...]
     for d in range(1, side):
-        arrived(rg.at[d], rg_r.at[d - 1])
         total = total + rg[d]
     rx[0] = total
-    for e in range(1, side):
-        go(rx.at[0], rx.at[side - e], rx_s.at[e - 1], rx_r.at[side - e - 1], vir=vid(g, (r + e) % side))
+    fan(1, side, to_reduce)
     gather(0)
+    arrived(rx.at[pl.ds(1, side - 1)], rx_r)
     total = rx[0]
     for d in range(1, side):
-        arrived(rx.at[d], rx_r.at[d - 1])
         total = total + rx[d]
     rmsg[...] = total.astype(BF16)
     own_rows = pl.ds(pl.multiple_of(z * nq8, 16), nq8)
-    for e in near_first:
-        go(rmsg, rall.at[c, own_rows, :], rz_s.at[e - 1], rz_r.at[z], aux=(z + e) % nz)
+    fan(1, nz, lambda d: remote(rmsg, rall.at[c, own_rows, :], rz_s, rz_r, aux=(z + d) % nz))
     rall[c, own_rows, :] = rmsg[...]
     scatter(2)
-    for w in range(side):
-        own_v[w].wait()
+    pltpu.make_async_copy(vir_h.at[pl.ds(0, side * s.rows), :], vb.at[0, pl.ds(0, side * s.rows), :], v_own).wait()
     product(0, (0,))
     relay(0)
     gather(1)
-    gathered(0, 1)
-    gathered(0, 3)
-    for d in range(1, side):
-        for w in range(side):
-            v_copies[d, w].wait_recv()
+    near_in(0)
+    arrived(vb.at[pl.ds(1, side - 1), pl.ds(0, side * s.rows), :], v_r)
     product(0, (1, 3))
-    gathered(0, 2)
+    far_in(0)
     product(0, (2,))
     reduce_start(0)
     product(1, (0,))
     relay(1)
     reduce_merge(0)
-    gathered(1, 1)
-    gathered(1, 3)
+    near_in(1)
     product(1, (1, 3))
-    gathered(1, 2)
+    far_in(1)
     product(1, (2,))
     reduce_start(1)
-    for d in near_first:
-        source = (z + d) % nz
-        arrived(rall.at[c, pl.ds(pl.multiple_of(source * nq8, 16), nq8), :], rz_r.at[source])
-        arrived(sh.at[source], sh_r.at[source])
+    arrived(rall.at[c, pl.ds(0, (nz - 1) * nq8), :], rz_r)
+    arrived(sh.at[pl.ds(0, nz - 1)], sh_r)
     go(rall.at[c], rall.at[c], rc_s, rc_r, occ=1 - c)
     gather(2)
     arrived(rall.at[1 - c], rc_r)
@@ -349,9 +343,7 @@
     def build(group):
         j0, count = s.groups[group]
         pack = s.packs[group]
-        for side_of in range(2):
-            for part, rows in enumerate(parts_of(group)):
-                arrived(bx[group].at[side_of, rows], b_r.at[group, side_of, part])
+        arrived(bx[group], b_r.at[group])
 
         @pl.loop(0, nz)
         def _(source):
@@ -379,80 +371,66 @@
     tall = 4 * s.nocc
     coupled, weighted = (coupled0, coupled1), (weighted0, weighted1)
 
-    def rows_of(step, tiles):
-        return pl.ds(pl.multiple_of(step // tiles * tall, 16), tall)
-
-    def couple(step, slot, start, tiles):
-        coupled[slot][...] = dot(rm[rows_of(step, tiles), :], bj[start + step % tiles])
-
-    def weigh(step, slot, start, tiles):
-        own = row[rows_of(step, tiles), :]
-        divisor = jnp.concatenate([own] * (s.tile // 128), axis=1) + base[start + step % tiles, 0:1, :]
+    def couple(slot, tile, quad):
+        coupled[slot][...] = dot(rm[pl.ds(pl.multiple_of(quad * tall, 16), tall), :], bj[tile])
+
+    def weigh(slot, tile, quad):
+        own = row[pl.ds(pl.multiple_of(quad * tall, 8), tall), :]
+        divisor = jnp.concatenate([own] * (s.tile // 128), axis=1) + base[tile, 0:1, :]
         weighted[slot][...] = (coupled[slot][...] * pl.reciprocal(divisor, approx=True, full_range=False)).astype(BF16)
 
-    def fold(step, slot, start, tiles):
-        fa[rows_of(step, tiles), :] += dot(weighted[slot][...], bjt[start + step % tiles])
-
-    def half_step(half, span):
-        for slot in range(2):
-            step = 2 * half + slot
-            fold(step - 2, slot, *span)
-            weigh(step - 1, 1 - slot, *span)
-            couple(step, slot, *span)
-
-    def advance(span, after=None):
-        @pl.loop(1, span[1])
-        def _(half):
-            half_step(half, span)
-            if after is not None:
-                after(half)
-
-    def bridge(span, later):
-        last = 2 * span[1] - 1
-        fold(last - 1, 0, *span)
-        weigh(last, 1, *span)
-        couple(0, 0, *later)
-        fold(last, 1, *span)
-        weigh(0, 0, *later)
-        couple(1, 1, *later)
+    def fold(slot, tile, quad):
+        fa[pl.ds(pl.multiple_of(quad * tall, 8), tall), :] += dot(weighted[slot][...], bjt[tile])
+
+    def advance(older, old, new, newer):
+        fold(0, *older)
+        weigh(1, *old)
+        couple(0, *new)
+        fold(1, *old)
+        weigh(0, *new)
+        couple(1, *newer)
 
     fa[...] = jnp.zeros(fa.shape, F32)
     bflat[:, s.tiles * s.tile - 128 :] = jnp.zeros((s.q, 128), F32)
     ready(0)
-    spans = s.spans
-    couple(0, 0, *spans[0])
-    couple(1, 1, *spans[0])
-    weigh(0, 0, *spans[0])
-    for half in range(1, spans[0][1]):
-        half_step(half, spans[0])
-        if half == 1:
-            gathered(2, 1)
-            gathered(2, 3)
+    couple(0, 0, 0)
+    couple(1, 0, 1)
+    weigh(0, 0, 0)
+    second, third = s.spans[1][0], s.spans[2][0]
+
+    @pl.loop(1, third)
+    def _(tile):
+        @pl.when(tile == 2)
+        def _():
+            near_in(2)
             product(2, (1, 3))
-            gathered(2, 2)
+            far_in(2)
             product(2, (2,))
             reduce_start(2)
-    reduce_merge(2)
-    ready(1)
-    bridge(spans[0], spans[1])
-    advance(spans[1])
+
+        @pl.when(tile == second)
+        def _():
+            reduce_merge(2)
+            ready(1)
+
+        advance((tile - 1, 0), (tile - 1, 1), (tile, 0), (tile, 1))
+
     ready(2)
-    bridge(spans[1], spans[2])
+    advance((third - 1, 0), (third - 1, 1), (third, 0), (third + 1, 0))
 
     rows4 = 4 * s.nq
-    around = side * side
 
     def to_owner(u, d):
         other = (me + d) % (2 * nz)
         return pltpu.make_async_remote_copy(
             src_ref=fb.at[u, other % 2, pl.ds(pl.multiple_of(other // 2 * rows4, 16), rows4), :], dst_ref=fr.at[u, me],
-            send_sem=fz_s.at[u, d - 1], recv_sem=fz_r.at[u, me],
+            send_sem=fz_s.at[u], recv_sem=fz_r.at[u],
             device_id={"aux": other // 2, "occ": other % 2}, device_id_type=MESH,
         )
 
     def to_plane(u, d):
         return pltpu.make_async_remote_copy(
-            src_ref=fp.at[u], dst_ref=fq.at[u, v], send_sem=fp_s.at[u, d - 1], recv_sem=fp_r.at[u, v],
+            src_ref=fp.at[u], dst_ref=fq.at[u, v], send_sem=fp_s.at[u], recv_sem=fp_r.at[u],
             device_id={"vir": (v + d) % around}, device_id_type=MESH,
         )
 
@@ -469,26 +447,20 @@
                         ]
         for h in range(2):
             fb[u, h] = jnp.concatenate([fl[h, part] for part in range(s.parts)], axis=1).astype(BF16)
-        for d in range(1, 2 * nz):
-            to_owner(u, d).start()
+        fan(1, 2 * nz, functools.partial(to_owner, u))
         fr[u, me] = fb[u, c, pl.ds(pl.multiple_of(z * rows4, 16), rows4), :]
 
     def pass_on(u):
-        for d in range(1, 2 * nz):
-            other = (me + d) % (2 * nz)
-            arrived(fr.at[u, other], fz_r.at[u, other])
+        arrived(fr.at[u, pl.ds(0, 2 * nz - 1)], fz_r.at[u])
         total = fr[u, 0].astype(F32)
         for other in range(1, 2 * nz):
             total = total + fr[u, other].astype(F32)
         fp[u] = total.astype(BF16)
-        for d in range(1, around):
-            to_plane(u, d).start()
+        fan(1, around, functools.partial(to_plane, u))
         fq[u, v] = fp[u]
 
     def apply(u):
-        for d in range(1, around):
-            other = (v + d) % around
-            arrived(fq.at[u, other], fp_r.at[u, other])
+        arrived(fq.at[u, pl.ds(0, around - 1)], fp_r.at[u])
         total = fq[u, 0].astype(F32)
         for other in range(1, around):
             total = total + fq[u, other].astype(F32)
@@ -505,9 +477,16 @@
                 value = value + spart[m * s.nq + q : m * s.nq + q + 1, :]
             sgs[4 * u + m] = value
 
-    late = spans[2][1]
-
-    def serve(half):
+    late = s.spans[2][1]
+
+    def pair(step):
+        return third + step % late, step // late
+
+    @pl.loop(1, late)
+    def _(half):
+        step = 2 * half
+        advance(pair(step - 2), pair(step - 1), pair(step), pair(step + 1))
+
         @pl.when(half == late // 2)
         def _():
             finish(0)
@@ -516,46 +495,50 @@
         def _():
             pass_on(0)
 
-    advance(spans[2], serve)
-    fold(2 * late - 2, 0, *spans[2])
-    weigh(2 * late - 1, 1, *spans[2])
-    fold(2 * late - 1, 1, *spans[2])
+    last = 2 * late - 1
+    fold(0, *pair(last - 1))
+    weigh(1, *pair(last))
+    fold(1, *pair(last))
     finish(1)
-    for copy in started:
-        copy.wait_send()
-    started.clear()
+    for group in range(3):
+        sent(hs[group].at[pl.ds(0, nz - 1)], h_s.at[group])
+        sent(hg[group].at[pl.ds(0, side - 1)], g_s.at[group])
+        sent(bs[group], b_s.at[group])
+    sent(vir_h.at[pl.ds(0, (side - 1) * side * s.rows), :], v_s)
+    sent(sh.at[pl.ds(0, nz - 1)], sh_s)
+    sent(xf, x_s)
+    sent(rg.at[pl.ds(1, side - 1)], rg_s)
+    sent(rx.at[pl.ds(1, side - 1)], rx_s)
+    sent(rall.at[c, pl.ds(0, (nz - 1) * nq8), :], rz_s)
+    sent(rall.at[c], rc_s)
     apply(0)
     pass_on(1)
     for u in range(2):
-        for d in range(1, 2 * nz):
-            to_owner(u, d).wait_send()
+        sent(fr.at[u, pl.ds(0, 2 * nz - 1)], fz_s.at[u])
     apply(1)
-    for d in range(1, 2 * nz):
+
+    def to_aux(d):
         other = (me + d) % (2 * nz)
-        go(sgs.at[other // 2], sgr.at[me], s1_s.at[d - 1], s1_r.at[me], aux=other // 2, occ=other % 2)
+        return remote(sgs.at[other // 2], sgr.at[me], s1_s, s1_r, aux=other // 2, occ=other % 2)
+
+    fan(1, 2 * nz, to_aux)
     sgr[me] = sgs[z]
-    for d in range(1, 2 * nz):
-        other = (me + d) % (2 * nz)
-        arrived(sgr.at[other], s1_r.at[other])
+    arrived(sgr.at[pl.ds(0, 2 * nz - 1)], s1_r)
     total = sgr[0]
     for d in range(1, 2 * nz):
         total = total + sgr[d]
     spp[...] = total
-    for d in range(1, side * side):
-        go(spp, spr.at[v], s2_s.at[d - 1], s2_r.at[v], vir=(v + d) % (side * side))
+    fan(1, around, lambda d: remote(spp, spr.at[v], s2_s, s2_r, vir=(v + d) % around))
     spr[v] = total
-    for d in range(1, side * side):
-        other = (v + d) % (side * side)
-        arrived(spr.at[other], s2_r.at[other])
+    arrived(spr.at[pl.ds(0, around - 1)], s2_r)
     total = spr[0]
     for d in range(1, side * side):
         total = total + spr[d]
     out[...] = total
-    for copy in started:
-        copy.wait_send()
     for u in range(2):
-        for d in range(1, around):
-            to_plane(u, d).wait_send()
+        sent(fq.at[u, pl.ds(0, around - 1)], fp_s.at[u])
+    sent(sgr.at[pl.ds(0, 2 * nz - 1)], s1_s)
+    sent(spr.at[pl.ds(0, around - 1)], s2_s)
 
 
 def output_kernel(terms, trial, eo_row, sigma_out, sub_out, t32):
@@ -573,7 +556,6 @@
     nq8 = s.nq * s.nvec
     rows4 = 4 * s.nq
     dma = lambda *shape: pltpu.SemaphoreType.DMA(shape)
-    near = side - 1
     one = pltpu.SemaphoreType.DMA
     tall = 4 * s.nocc
     flat = s.parts * 128
@@ -626,11 +608,11 @@
         vmem((2, s.parts, nz * nq8, 128), F32),
         vmem((s.nvec, s.nocc, s.q), F32),
         vmem((nz, 8, 128), F32),
-        dma(s.nq + 1), dma(side), dma(near, side), dma(near, side), dma(nz), dma(nz),
-        dma(s.nq), dma(s.nq), dma(3, nz), dma(3, nz), dma(3, near, 2), dma(3, near, 2),
-        dma(near), dma(near), dma(near), dma(near), dma(nz), dma(nz), one, one,
-        dma(3, 2, 2), dma(3, 2, 2), dma(3, 2), dma(3, 2),
-        dma(s.quads, 2 * nz), dma(s.quads, 2 * nz), dma(s.quads, side * side), dma(s.quads, side * side), dma(2 * nz), dma(2 * nz), dma(side * side), dma(side * side),
+        dma(s.nq + 1), one, one, one, one, one,
+        one, dma(s.nq), dma(3), dma(3), dma(3), dma(3, 4),
+        one, one, one, one, one, one, one, one,
+        dma(3), dma(3), dma(3),
+        dma(s.quads), dma(s.quads), dma(s.quads), dma(s.quads), one, one, one, one,
     ]
     hbm = pl.BlockSpec(memory_space=pl.ANY)
     fast = pl.BlockSpec(memory_space=pltpu.VMEM)

time: 104 us -> 102 us (0.981)
  Pallas kernels: 103 us -> 100 us
    pallas_call x1, Pallas kernels: 101 us -> 98.9 us  [local(): pl.pallas_call(functools.partial(kernel, s), out_shape=shape((1, s.nocc),...]
where the time goes in v6:
time: 102 us
  Pallas kernels  100 us (98%)
  between operations  1.29 us (1%)
    pallas_call x1, Pallas kernels, local(): pl.pallas_call(functools.partial(kernel, s), out_shape=shape((1, s.nocc),...  98.9 us

profile of v6, /device:TPU:1, one launch (start us, length us, event | category | flops | bytes accessed | tf_op | source)
XLA Modules:
  0.0 101.5 jit_solution(9860356889577947214)
XLA Ops:
  1.3 98.9 %shard_map.86.terms = f32[1,400]{1,0:T(1,128)} custom-call(bf16[4,2000,250]{2,1,0:T(8,128)(2,1)} %int_h.1, bf16[400,4000]{1,0:T(8,128)(2,1)} %bitcast.7, bf16[3600,250]{1,0:T(8,128)(2,1)} %bitcast.8, bf16[8,400]{1,0:T(8,128)(2,1)} %bitcast.9, f32[1,400]{1,0:T(1,128)} %bitcast.11, f32[400]{0:T(512)} %eo_s.1, f32[1,225]{1,0:T(1,128)} %bitcast.13, ...), custom_call_target="tpu_custom_call" | custom-call | tf_op jit(solution)/shard_map/pallas_call | solution.py:623
  100.2 1.4 %shard_map.87 = (f32[1,400]{1,0:T(1,128)}, f32[1,8]{1,0:T(1,128)}) custom-call(f32[1,400]{1,0:T(1,128)} %shard_map.86.terms, bf16[8,400]{1,0:T(8,128)(2,1)} %bitcast.10, f32[1,400]{1,0:T(1,128)} %bitcast.12), custom_call_target="tpu_custom_call" | custom-call | tf_op jit(solution)/shard_map/pallas_call | solution.py:631

commit v7 on v6

--- a/solution.py
+++ b/solution.py
@@ -72,10 +72,10 @@
     out,
     bj, bjt, base, rm, row, hq, sec, fa, coupled0, coupled1, weighted0, weighted1,
     hp, fl, fb, fr, fp, fq, spart, sgs, sgr, spp, spr,
-    ibuf, occ_v, pf, xf, pk0, pk1, pk2, hs0, hs1, hs2, hg0, hg1, hg2, vb,
+    ibuf, occ_v, pf, xf, pk0, pk1, pk2, hs0, hs1, hs2, hg0, hg1, hg2, vb, vbt, vst,
     acc0, acc1, acc2, bs0, bs1, bs2, bx0, bx1, bx2, bm0, bm1, bm2, bf, bflat, eob, ve8, shift,
     rp, rg, rx, rmsg, rall, rl, rm32, sh,
-    in_sem, v_own, v_s, v_r, sh_s, sh_r, x_s, x_r, h_s, h_r, g_s, g_r, rg_s, rg_r, rx_s, rx_r, rz_s, rz_r, rc_s, rc_r,
+    in_sem, v_own, v_s, v_r, st_r, sh_s, sh_r, x_s, x_r, h_s, h_r, g_s, g_r, rg_s, rg_r, rx_s, rx_r, rz_s, rz_r, rc_s, rc_r,
     b_s, b_r, m_r, fz_s, fz_r, fp_s, fp_r, s1_s, s1_r, s2_s, s2_r,
 ):
     nz, side = s.nz, s.side
@@ -150,12 +150,19 @@
 
     pl.semaphore_wait(barrier, 2 * nz + around - 2)
 
-    def v_copy(d):
-        e, w = 1 + d // side, d % side
-        to = (g + e) % side
-        return remote(window(to, w), place(side - e, w), v_s, v_r, vir=vid(to, r))
-
-    fan(0, (side - 1) * side, v_copy)
+    ahead, behind = vid((g + 1) % side, r), vid((g + 3) % side, r)
+    opposite = (g + 2) % side
+
+    @pl.loop(0, 2)
+    def _(w):
+        go(window(opposite, w), vst.at[0, w], v_s, st_r.at[0], vir=ahead)
+        go(window(opposite, w + 2), vst.at[1, w], v_s, st_r.at[1], vir=behind)
+
+    @pl.loop(0, side)
+    def _(w):
+        go(window((g + 1) % side, w), place(3, w), v_s, v_r.at[0], vir=ahead)
+        go(window((g + 3) % side, w), place(1, w), v_s, v_r.at[0], vir=behind)
+
     shift[...] = jnp.full((8, 128), shift_s[0], F32)
     fan(1, nz, lambda d: remote(shift, sh.at[z], sh_s, sh_r, aux=(z + d) % nz))
     sh[z] = shift[...]
@@ -169,6 +176,14 @@
         pf[q] = dot(columns, ibuf[q])
         theirs = pf.at[q, pl.ds(pl.multiple_of(s.half * (1 - c), 8), s.half), :]
         go(theirs, xf.at[q], x_s, x_r.at[q], occ=1 - c)
+
+    arrived(vst.at[0], st_r.at[0])
+    arrived(vst.at[1], st_r.at[1])
+
+    @pl.loop(0, 2)
+    def _(w):
+        go(vst.at[0, w], place(2, w), v_s, v_r.at[1], vir=ahead)
+        go(vst.at[1, w], place(2, w + 2), v_s, v_r.at[1], vir=behind)
 
     for q in range(s.nq):
         arrived(xf.at[q], x_r.at[q])
@@ -223,7 +238,6 @@
     fill = -(-s.nocc // 128) * 128 - s.nocc
     eob[...] = jnp.concatenate([square, jnp.zeros((128, fill), F32)], axis=1).T[: s.nocc]
 
-    ahead, behind = vid((g + 1) % side, r), vid((g + 3) % side, r)
     halves = (pl.ds(0, nz // 2), pl.ds(nz // 2, nz // 2))
 
     def gather(group):
@@ -245,7 +259,7 @@
         arrived(hg[group].at[2], g_r.at[group, 3])
 
     def term(group, d):
-        return dot_nt(hg[group][d].reshape(nz * s.packs[group], s.nu), vb[d])
+        return dot(hg[group][d].reshape(nz * s.packs[group], s.nu), vbt[d])
 
     def product(group, slots):
         value = term(group, slots[0])
@@ -285,6 +299,14 @@
         go(bs[group].at[2, high], bx[group].at[1, high], b_s.at[group], b_r.at[group], vir=left)
 
     nq8 = s.nq * s.nvec
+    iota = functools.partial(lax.broadcasted_iota, jnp.int32, (s.nu, s.nu))
+    identity = jnp.where(iota(0) == iota(1), 1.0, 0.0).astype(BF16)
+
+    def turn(d):
+        vbt[d] = dot_nt(identity, vb[d]).astype(BF16)
+
+    pltpu.make_async_copy(vir_h.at[pl.ds(0, side * s.rows), :], vb.at[0, pl.ds(0, side * s.rows), :], v_own).wait()
+    turn(0)
     arrived(rg.at[pl.ds(1, side - 1)], rg_r)
     total = rp[...]
     for d in range(1, side):
@@ -301,13 +323,16 @@
     fan(1, nz, lambda d: remote(rmsg, rall.at[c, own_rows, :], rz_s, rz_r, aux=(z + d) % nz))
     rall[c, own_rows, :] = rmsg[...]
     scatter(2)
-    pltpu.make_async_copy(vir_h.at[pl.ds(0, side * s.rows), :], vb.at[0, pl.ds(0, side * s.rows), :], v_own).wait()
     product(0, (0,))
+    arrived(vb.at[pl.ds(1, 2), pl.ds(0, side * s.rows), :], v_r.at[0])
     relay(0)
+    turn(1)
+    turn(3)
+    near_in(0)
+    product(0, (1, 3))
+    arrived(vb.at[2, pl.ds(0, side * s.rows), :], v_r.at[1])
+    turn(2)
     gather(1)
-    near_in(0)
-    arrived(vb.at[pl.ds(1, side - 1), pl.ds(0, side * s.rows), :], v_r)
-    product(0, (1, 3))
     far_in(0)
     product(0, (2,))
     reduce_start(0)
@@ -504,7 +529,7 @@
         sent(hs[group].at[pl.ds(0, nz - 1)], h_s.at[group])
         sent(hg[group].at[pl.ds(0, side - 1)], g_s.at[group])
         sent(bs[group], b_s.at[group])
-    sent(vir_h.at[pl.ds(0, (side - 1) * side * s.rows), :], v_s)
+    sent(vb.at[:, pl.ds(0, side * s.rows), :], v_s)
     sent(sh.at[pl.ds(0, nz - 1)], sh_s)
     sent(xf, x_s)
     sent(rg.at[pl.ds(1, side - 1)], rg_s)
@@ -591,6 +616,8 @@
         *[vmem((nz, pack, s.nu), BF16) for pack in s.packs],
         *[vmem((side, nz, pack, s.nu), BF16) for pack in s.packs],
         vmem((side, side * s.lanes, s.nu), BF16),
+        vmem((side, s.nu, side * s.lanes), BF16),
+        vmem((2, 2, s.rows, s.nu), BF16),
         *[vmem((nz * pack, side * s.lanes), F32) for pack in s.packs],
         *[vmem((side - 1, nz * pack, s.lanes), BF16) for pack in s.packs],
         *[vmem((2, nz * pack, s.lanes), BF16) for pack in s.packs],
@@ -608,7 +635,7 @@
         vmem((2, s.parts, nz * nq8, 128), F32),
         vmem((s.nvec, s.nocc, s.q), F32),
         vmem((nz, 8, 128), F32),
-        dma(s.nq + 1), one, one, one, one, one,
+        dma(s.nq + 1), one, one, dma(2), dma(2), one, one,
         one, dma(s.nq), dma(3), dma(3), dma(3), dma(3, 4),
         one, one, one, one, one, one, one, one,
         dma(3), dma(3), dma(3),

time: 102 us -> 102 us (level)
  no operation moved by 1% of the time
where the time goes in v7:
time: 102 us
  Pallas kernels  101 us (99%)
  between operations  1.29 us (1%)
    pallas_call x1, Pallas kernels, local(): pl.pallas_call(functools.partial(kernel, s), out_shape=shape((1, s.nocc),...  99.3 us

profile of v7, /device:TPU:1, one launch (start us, length us, event | category | flops | bytes accessed | tf_op | source)
XLA Modules:
  0.0 102.0 jit_solution(9661593275701924452)
XLA Ops:
  1.3 99.3 %shard_map.86.terms = f32[1,400]{1,0:T(1,128)} custom-call(bf16[4,2000,250]{2,1,0:T(8,128)(2,1)} %int_h.1, bf16[400,4000]{1,0:T(8,128)(2,1)} %bitcast.7, bf16[3600,250]{1,0:T(8,128)(2,1)} %bitcast.8, bf16[8,400]{1,0:T(8,128)(2,1)} %bitcast.9, f32[1,400]{1,0:T(1,128)} %bitcast.11, f32[400]{0:T(512)} %eo_s.1, f32[1,225]{1,0:T(1,128)} %bitcast.13, ...), custom_call_target="tpu_custom_call" | custom-call | tf_op jit(solution)/shard_map/pallas_call | solution.py:650
  100.6 1.4 %shard_map.87 = (f32[1,400]{1,0:T(1,128)}, f32[1,8]{1,0:T(1,128)}) custom-call(f32[1,400]{1,0:T(1,128)} %shard_map.86.terms, bf16[8,400]{1,0:T(8,128)(2,1)} %bitcast.10, f32[1,400]{1,0:T(1,128)} %bitcast.12), custom_call_target="tpu_custom_call" | custom-call | tf_op jit(solution)/shard_map/pallas_call | solution.py:658

commit v8 on v7

--- a/solution.py
+++ b/solution.py
@@ -73,10 +73,10 @@
     bj, bjt, base, rm, row, hq, sec, fa, coupled0, coupled1, weighted0, weighted1,
     hp, fl, fb, fr, fp, fq, spart, sgs, sgr, spp, spr,
     ibuf, occ_v, pf, xf, pk0, pk1, pk2, hs0, hs1, hs2, hg0, hg1, hg2, vb, vbt, vst,
-    acc0, acc1, acc2, bs0, bs1, bs2, bx0, bx1, bx2, bm0, bm1, bm2, bf, bflat, eob, ve8, shift,
-    rp, rg, rx, rmsg, rall, rl, rm32, sh,
-    in_sem, v_own, v_s, v_r, st_r, sh_s, sh_r, x_s, x_r, h_s, h_r, g_s, g_r, rg_s, rg_r, rx_s, rx_r, rz_s, rz_r, rc_s, rc_r,
-    b_s, b_r, m_r, fz_s, fz_r, fp_s, fp_r, s1_s, s1_r, s2_s, s2_r,
+    acc0, acc1, acc2, bs0, bs1, bs2, bx0, bx1, bx2, bf, bflat, eob, ve8, shift,
+    rp, rg, rmsg, rall, rl, rm32, sh,
+    in_sem, v_own, v_s, v_r, st_r, sh_s, sh_r, x_s, x_r, h_s, h_r, g_s, g_r, rg_s, rg_r, rz_s, rz_r, rc_s, rc_r,
+    b_s, b_r, fz_s, fz_r, fp_s, fp_r, s1_s, s1_r, s2_s, s2_r,
 ):
     nz, side = s.nz, s.side
     z, c, v = lax.axis_index("aux"), lax.axis_index("occ"), lax.axis_index("vir")
@@ -90,7 +90,7 @@
         return gather * sg + reduce * sr
 
     pk, hs, hg, acc = (pk0, pk1, pk2), (hs0, hs1, hs2), (hg0, hg1, hg2), (acc0, acc1, acc2)
-    bs, bx, bm = (bs0, bs1, bs2), (bx0, bx1, bx2), (bm0, bm1, bm2)
+    bs, bx = (bs0, bs1, bs2), (bx0, bx1, bx2)
     me = 2 * z + c
     around = side * side
 
@@ -177,6 +177,12 @@
         theirs = pf.at[q, pl.ds(pl.multiple_of(s.half * (1 - c), 8), s.half), :]
         go(theirs, xf.at[q], x_s, x_r.at[q], occ=1 - c)
 
+    start = 128 * ((s.nu * v) // 128) - 128 * ((v + 1) // (side * side))
+    view = occ_v[:, pl.ds(pl.multiple_of(start, 128), s.view)].astype(F32)
+    wide = -(-s.view // 128) * 128
+    view = jnp.concatenate([view, jnp.zeros((s.nocc, wide - s.view), F32)], axis=1)
+    sec[...] = pltpu.roll(view, wide - (s.nu * v - start), 1)[:, : s.nu].astype(BF16)
+    weights = split(dot(trial[...], sec[...]))
     arrived(vst.at[0], st_r.at[0])
     arrived(vst.at[1], st_r.at[1])
 
@@ -203,26 +209,14 @@
         hg[group][0, z] = hs[group][z]
 
     scatter(0)
-    scatter(1)
     for q in range(s.nq):
         hq[q] = xf[q].astype(BF16)
-    start = 128 * ((s.nu * v) // 128) - 128 * ((v + 1) // (side * side))
-    view = occ_v[:, pl.ds(pl.multiple_of(start, 128), s.view)].astype(F32)
-    wide = -(-s.view // 128) * 128
-    view = jnp.concatenate([view, jnp.zeros((s.nocc, wide - s.view), F32)], axis=1)
-    sec[...] = pltpu.roll(view, wide - (s.nu * v - start), 1)[:, : s.nu].astype(BF16)
-    weights = split(dot(trial[...], sec[...]))
-
     for q in range(s.nq):
         both = dot_nt(weights, hq[q])
         rp[q * s.nvec : (q + 1) * s.nvec, 0 : s.half] = both[: s.nvec] + both[s.nvec :]
-    def to_gather(d):
-        return remote(rp, rg.at[side - d], rg_s, rg_r, vir=vid((g + d) % side, r))
-
-    def to_reduce(d):
-        return remote(rx.at[0], rx.at[side - d], rx_s, rx_r, vir=vid(g, (r + d) % side))
-
-    fan(1, side, to_gather)
+    rg[v] = rp[...].astype(BF16)
+    fan(1, around, lambda d: remote(rg.at[v], rg.at[v], rg_s, rg_r, vir=(v + d) % around))
+    scatter(1)
     for q in range(s.nq):
         hp[q] = dot_nt(hq[q], sec[...]).astype(BF16)
 
@@ -238,25 +232,18 @@
     fill = -(-s.nocc // 128) * 128 - s.nocc
     eob[...] = jnp.concatenate([square, jnp.zeros((128, fill), F32)], axis=1).T[: s.nocc]
 
-    halves = (pl.ds(0, nz // 2), pl.ds(nz // 2, nz // 2))
+    across = vid((g + 2) % side, r)
 
     def gather(group):
         arrived(hg[group].at[0, pl.ds(0, nz - 1)], h_r.at[group])
-        for to, slot, part, sem in ((behind, 1, 0, 0), (ahead, 3, 1, 1), (behind, 1, 1, 2), (ahead, 3, 0, 2)):
-            block = hg[group].at[0, halves[part]]
-            go(block, hg[group].at[slot, halves[part]], g_s.at[group], g_r.at[group, sem], vir=to)
-
-    def relay(group):
-        for slot, to, part in ((1, behind, 0), (3, ahead, 1)):
-            block = hg[group].at[slot, halves[part]]
-            arrived(block, g_r.at[group, part])
-            go(block, hg[group].at[2, halves[part]], g_s.at[group], g_r.at[group, 3], vir=to)
+        for slot, to, sem in ((1, behind, 0), (3, ahead, 0), (2, across, 1)):
+            go(hg[group].at[0], hg[group].at[slot], g_s.at[group], g_r.at[group, sem], vir=to)
 
     def near_in(group):
-        arrived(hg[group].at[1], g_r.at[group, 2])
+        arrived(hg[group].at[pl.ds(0, 2)], g_r.at[group, 0])
 
     def far_in(group):
-        arrived(hg[group].at[2], g_r.at[group, 3])
+        arrived(hg[group].at[2], g_r.at[group, 1])
 
     def term(group, d):
         return dot(hg[group][d].reshape(nz * s.packs[group], s.nu), vbt[d])
@@ -270,33 +257,11 @@
     def columns_of(w):
         return pl.ds(pl.multiple_of(w * s.lanes, 128), s.lanes)
 
-    right, left = vid(g, (r + 1) % side), vid(g, (r + 3) % side)
-
-    def parts_of(group):
-        size = nz * s.packs[group] // 2
-        return pl.ds(0, size), pl.ds(size, size)
-
     def reduce_start(group):
-        low, high = parts_of(group)
         for e in (2, 1, 3):
-            bs[group][e - 1] = acc[group][:, columns_of((r + e) % side)].astype(BF16)
-            if e == 2:
-                go(bs[group].at[1, low], bm[group].at[0], b_s.at[group], m_r.at[group], vir=right)
-                go(bs[group].at[1, high], bm[group].at[1], b_s.at[group], m_r.at[group], vir=left)
-            if e == 1:
-                go(bs[group].at[0, high], bx[group].at[0, high], b_s.at[group], b_r.at[group], vir=right)
-            if e == 3:
-                go(bs[group].at[2, low], bx[group].at[1, low], b_s.at[group], b_r.at[group], vir=left)
-
-    def reduce_merge(group):
-        low, high = parts_of(group)
-        arrived(bm[group], m_r.at[group])
-        merged = acc[group][low, columns_of((r + 1) % side)] + bm[group][0].astype(F32)
-        bs[group][0, low, :] = merged.astype(BF16)
-        go(bs[group].at[0, low], bx[group].at[0, low], b_s.at[group], b_r.at[group], vir=right)
-        merged = acc[group][high, columns_of((r + 3) % side)] + bm[group][1].astype(F32)
-        bs[group][2, high, :] = merged.astype(BF16)
-        go(bs[group].at[2, high], bx[group].at[1, high], b_s.at[group], b_r.at[group], vir=left)
+            w = (r + e) % side
+            bs[group][e - 1] = acc[group][:, columns_of(w)].astype(BF16)
+            go(bs[group].at[e - 1], bx[group].at[e - 1], b_s.at[group], b_r.at[group], vir=vid(g, w))
 
     nq8 = s.nq * s.nvec
     iota = functools.partial(lax.broadcasted_iota, jnp.int32, (s.nu, s.nu))
@@ -307,17 +272,11 @@
 
     pltpu.make_async_copy(vir_h.at[pl.ds(0, side * s.rows), :], vb.at[0, pl.ds(0, side * s.rows), :], v_own).wait()
     turn(0)
-    arrived(rg.at[pl.ds(1, side - 1)], rg_r)
-    total = rp[...]
-    for d in range(1, side):
-        total = total + rg[d]
-    rx[0] = total
-    fan(1, side, to_reduce)
     gather(0)
-    arrived(rx.at[pl.ds(1, side - 1)], rx_r)
-    total = rx[0]
-    for d in range(1, side):
-        total = total + rx[d]
+    arrived(rg.at[pl.ds(0, around - 1)], rg_r)
+    total = rg[0].astype(F32)
+    for other in range(1, around):
+        total = total + rg[other].astype(F32)
     rmsg[...] = total.astype(BF16)
     own_rows = pl.ds(pl.multiple_of(z * nq8, 16), nq8)
     fan(1, nz, lambda d: remote(rmsg, rall.at[c, own_rows, :], rz_s, rz_r, aux=(z + d) % nz))
@@ -325,28 +284,25 @@
     scatter(2)
     product(0, (0,))
     arrived(vb.at[pl.ds(1, 2), pl.ds(0, side * s.rows), :], v_r.at[0])
-    relay(0)
     turn(1)
     turn(3)
+    gather(1)
     near_in(0)
     product(0, (1, 3))
     arrived(vb.at[2, pl.ds(0, side * s.rows), :], v_r.at[1])
     turn(2)
-    gather(1)
     far_in(0)
     product(0, (2,))
     reduce_start(0)
     product(1, (0,))
-    relay(1)
-    reduce_merge(0)
+    arrived(rall.at[c, pl.ds(0, (nz - 1) * nq8), :], rz_r)
+    arrived(sh.at[pl.ds(0, nz - 1)], sh_r)
+    go(rall.at[c], rall.at[c], rc_s, rc_r, occ=1 - c)
     near_in(1)
     product(1, (1, 3))
     far_in(1)
     product(1, (2,))
     reduce_start(1)
-    arrived(rall.at[c, pl.ds(0, (nz - 1) * nq8), :], rz_r)
-    arrived(sh.at[pl.ds(0, nz - 1)], sh_r)
-    go(rall.at[c], rall.at[c], rc_s, rc_r, occ=1 - c)
     gather(2)
     arrived(rall.at[1 - c], rc_r)
     for h in range(2):
@@ -361,9 +317,7 @@
             rm32[n, h * s.half : (h + 1) * s.half, :] = jnp.concatenate(sides, axis=1).T[: s.half]
         rm[n * s.nocc : (n + 1) * s.nocc, :] = rm32[n].astype(BF16)
         row[n * s.nocc : (n + 1) * s.nocc, :] = jnp.broadcast_to(sh[n][0:1, :], (s.nocc, 128)) - eob[...]
-    reduce_merge(1)
     product(2, (0,))
-    relay(2)
 
     def build(group):
         j0, count = s.groups[group]
@@ -373,7 +327,9 @@
         @pl.loop(0, nz)
         def _(source):
             rows = pl.ds(pl.multiple_of(source * pack, 16), pack)
-            value = acc[group][rows, columns_of(r)] + bx[group][0, rows, :].astype(F32) + bx[group][1, rows, :].astype(F32)
+            value = acc[group][rows, columns_of(r)]
+            for e in range(side - 1):
+                value = value + bx[group][e, rows, :].astype(F32)
             full = pltpu.roll(value.astype(BF16).astype(F32), s.lanes - v, 1)
             for part in range(s.lanes // 128):
                 bf[part, rows, :] = full[:, part * 128 : (part + 1) * 128]
@@ -435,7 +391,6 @@
 
         @pl.when(tile == second)
         def _():
-            reduce_merge(2)
             ready(1)
 
         advance((tile - 1, 0), (tile - 1, 1), (tile, 0), (tile, 1))
@@ -532,8 +487,7 @@
     sent(vb.at[:, pl.ds(0, side * s.rows), :], v_s)
     sent(sh.at[pl.ds(0, nz - 1)], sh_s)
     sent(xf, x_s)
-    sent(rg.at[pl.ds(1, side - 1)], rg_s)
-    sent(rx.at[pl.ds(1, side - 1)], rx_s)
+    sent(rg.at[pl.ds(0, around - 1)], rg_s)
     sent(rall.at[c, pl.ds(0, (nz - 1) * nq8), :], rz_s)
     sent(rall.at[c], rc_s)
     apply(0)
@@ -620,25 +574,23 @@
         vmem((2, 2, s.rows, s.nu), BF16),
         *[vmem((nz * pack, side * s.lanes), F32) for pack in s.packs],
         *[vmem((side - 1, nz * pack, s.lanes), BF16) for pack in s.packs],
-        *[vmem((2, nz * pack, s.lanes), BF16) for pack in s.packs],
-        *[vmem((2, nz * pack // 2, s.lanes), BF16) for pack in s.packs],
+        *[vmem((side - 1, nz * pack, s.lanes), BF16) for pack in s.packs],
         vmem((s.lanes // 128, nz * max(s.packs), 128), F32),
         vmem((s.q, s.tiles * s.tile), F32),
         vmem((s.nocc, 128), F32),
         vmem((8, s.lanes), F32),
         vmem((8, 128), F32),
         vmem((nq8, flat), F32),
-        vmem((side, nq8, flat), F32),
-        vmem((side, nq8, flat), F32),
+        vmem((side * side, nq8, flat), BF16),
         vmem((nq8, flat), BF16),
         vmem((2, nz * nq8, flat), BF16),
         vmem((2, s.parts, nz * nq8, 128), F32),
         vmem((s.nvec, s.nocc, s.q), F32),
         vmem((nz, 8, 128), F32),
         dma(s.nq + 1), one, one, dma(2), dma(2), one, one,
-        one, dma(s.nq), dma(3), dma(3), dma(3), dma(3, 4),
-        one, one, one, one, one, one, one, one,
-        dma(3), dma(3), dma(3),
+        one, dma(s.nq), dma(3), dma(3), dma(3), dma(3, 2),
+        one, one, one, one, one, one,
+        dma(3), dma(3),
         dma(s.quads), dma(s.quads), dma(s.quads), dma(s.quads), one, one, one, one,
     ]
     hbm = pl.BlockSpec(memory_space=pl.ANY)

time: 102 us -> 97 us (0.951)
  Pallas kernels: 101 us -> 95.6 us
    pallas_call x1, Pallas kernels: 99.3 us -> 94.2 us  [local(): pl.pallas_call(functools.partial(kernel, s), out_shape=shape((1, s.nocc),...]
where the time goes in v8:
time: 97 us; the launch traced here: 96.9 us
  Pallas kernels  95.6 us (99%)
  between operations  1.29 us (1%)
    pallas_call x1, Pallas kernels, local(): pl.pallas_call(functools.partial(kernel, s), out_shape=shape((1, s.nocc),...  94.2 us

profile of v8, /device:TPU:1, one launch (start us, length us, event | category | flops | bytes accessed | tf_op | source)
XLA Modules:
  0.0 96.9 jit_solution(14946061061140630763)
XLA Ops:
  1.3 94.2 %shard_map.86.terms = f32[1,400]{1,0:T(1,128)} custom-call(bf16[4,2000,250]{2,1,0:T(8,128)(2,1)} %int_h.1, bf16[400,4000]{1,0:T(8,128)(2,1)} %bitcast.7, bf16[3600,250]{1,0:T(8,128)(2,1)} %bitcast.8, bf16[8,400]{1,0:T(8,128)(2,1)} %bitcast.9, f32[1,400]{1,0:T(1,128)} %bitcast.11, f32[400]{0:T(512)} %eo_s.1, f32[1,225]{1,0:T(1,128)} %bitcast.13, ...), custom_call_target="tpu_custom_call" | custom-call | tf_op jit(solution)/shard_map/pallas_call | solution.py:602
  95.5 1.4 %shard_map.87 = (f32[1,400]{1,0:T(1,128)}, f32[1,8]{1,0:T(1,128)}) custom-call(f32[1,400]{1,0:T(1,128)} %shard_map.86.terms, bf16[8,400]{1,0:T(8,128)(2,1)} %bitcast.10, f32[1,400]{1,0:T(1,128)} %bitcast.12), custom_call_target="tpu_custom_call" | custom-call | tf_op jit(solution)/shard_map/pallas_call | solution.py:610

commit v9 on v8

--- a/solution.py
+++ b/solution.py
@@ -216,7 +216,6 @@
         rp[q * s.nvec : (q + 1) * s.nvec, 0 : s.half] = both[: s.nvec] + both[s.nvec :]
     rg[v] = rp[...].astype(BF16)
     fan(1, around, lambda d: remote(rg.at[v], rg.at[v], rg_s, rg_r, vir=(v + d) % around))
-    scatter(1)
     for q in range(s.nq):
         hp[q] = dot_nt(hq[q], sec[...]).astype(BF16)
 
@@ -281,6 +280,7 @@
     own_rows = pl.ds(pl.multiple_of(z * nq8, 16), nq8)
     fan(1, nz, lambda d: remote(rmsg, rall.at[c, own_rows, :], rz_s, rz_r, aux=(z + d) % nz))
     rall[c, own_rows, :] = rmsg[...]
+    scatter(1)
     scatter(2)
     product(0, (0,))
     arrived(vb.at[pl.ds(1, 2), pl.ds(0, side * s.rows), :], v_r.at[0])
@@ -304,19 +304,24 @@
     product(1, (2,))
     reduce_start(1)
     gather(2)
-    arrived(rall.at[1 - c], rc_r)
-    for h in range(2):
+    for n in range(s.nvec):
+        row[n * s.nocc : (n + 1) * s.nocc, :] = jnp.broadcast_to(sh[n][0:1, :], (s.nocc, 128)) - eob[...]
+
+    def lay_out(h):
         for part in range(s.parts):
             rl[h, part] = rall[h, :, part * 128 : (part + 1) * 128].astype(F32)
-    for n in range(s.nvec):
-        for h in range(2):
+        for n in range(s.nvec):
             sides = []
             for part in range(s.parts):
                 rows = [rl[h, part, pl.ds(q * s.nvec + n, nz, stride=nq8), :] for q in range(s.nq)]
                 sides.append(jnp.concatenate(rows, axis=0))
-            rm32[n, h * s.half : (h + 1) * s.half, :] = jnp.concatenate(sides, axis=1).T[: s.half]
+            rm32[n, pl.ds(pl.multiple_of(h * s.half, 8), s.half), :] = jnp.concatenate(sides, axis=1).T[: s.half]
+
+    lay_out(c)
+    arrived(rall.at[1 - c], rc_r)
+    lay_out(1 - c)
+    for n in range(s.nvec):
         rm[n * s.nocc : (n + 1) * s.nocc, :] = rm32[n].astype(BF16)
-        row[n * s.nocc : (n + 1) * s.nocc, :] = jnp.broadcast_to(sh[n][0:1, :], (s.nocc, 128)) - eob[...]
     product(2, (0,))
 
     def build(group):

time: 97 us -> 107 us (1.10)
  Pallas kernels: 95.6 us -> 106 us
    pallas_call x1, Pallas kernels: 94.2 us -> 104 us  [local(): pl.pallas_call(functools.partial(kernel, s), out_shape=shape((1, s.nocc),...]
where the time goes in v9:
time: 107 us
  Pallas kernels  106 us (99%)
  between operations  1.29 us (1%)
    pallas_call x1, Pallas kernels, local(): pl.pallas_call(functools.partial(kernel, s), out_shape=shape((1, s.nocc),...  104 us

profile of v9, /device:TPU:1, one launch (start us, length us, event | category | flops | bytes accessed | tf_op | source)
XLA Modules:
  0.0 106.8 jit_solution(1005277926732106555)
XLA Ops:
  1.3 104.2 %shard_map.86.terms = f32[1,400]{1,0:T(1,128)} custom-call(bf16[4,2000,250]{2,1,0:T(8,128)(2,1)} %int_h.1, bf16[400,4000]{1,0:T(8,128)(2,1)} %bitcast.7, bf16[3600,250]{1,0:T(8,128)(2,1)} %bitcast.8, bf16[8,400]{1,0:T(8,128)(2,1)} %bitcast.9, f32[1,400]{1,0:T(1,128)} %bitcast.11, f32[400]{0:T(512)} %eo_s.1, f32[1,225]{1,0:T(1,128)} %bitcast.13, ...), custom_call_target="tpu_custom_call" | custom-call | tf_op jit(solution)/shard_map/pallas_call | solution.py:607
  105.5 1.4 %shard_map.87 = (f32[1,400]{1,0:T(1,128)}, f32[1,8]{1,0:T(1,128)}) custom-call(f32[1,400]{1,0:T(1,128)} %shard_map.86.terms, bf16[8,400]{1,0:T(8,128)(2,1)} %bitcast.10, f32[1,400]{1,0:T(1,128)} %bitcast.12), custom_call_target="tpu_custom_call" | custom-call | tf_op jit(solution)/shard_map/pallas_call | solution.py:615
